TPU v7x, 32 devices: a whole 2x2x4 slice. The times are simulated.
32 devices in a mesh: dp: 16 (over z, y, core), seq: 2 (over x).
Axes of the slice: x: 2, y: 2, z: 4, core: 2. Of those that a mesh axis runs over, the one named last changes fastest.
Arguments:
- inputs: bfloat16 [16, 2048, 512], P('dp', 'seq'), may hold values from -6 to 6
- cotangent: bfloat16 [16, 2048, 512], P('dp', 'seq'), may hold values from -6 to 6
- mixer_gain: float32 [512], replicated, may hold values from 0.5 to 1.5
- mixer_bias: float32 [512], replicated, may hold values from -1.75 to 1.75
- query_weight: bfloat16 [512, 512], replicated, may hold values from -0.25 to 0.25
- key_weight: bfloat16 [512, 512], replicated, may hold values from -0.25 to 0.25
- value_weight: bfloat16 [512, 512], replicated, may hold values from -0.25 to 0.25
- gate_weight: bfloat16 [512, 8], replicated, may hold values from -0.25 to 0.25
- gate_bias: float32 [8], replicated, may hold values from 3 to 9
- output_weight: bfloat16 [512, 512], replicated, may hold values from -0.5 to 0.5
- projections: float32 [8, 64, 128], replicated, may hold values from -6 to 6
- start_state: float32 [8, 256, 64], replicated, may hold values from -1.75 to 1.75
- start_norm: float32 [8, 256], replicated, may hold values from -1.75 to 1.75
- feed_gain: float32 [512], replicated, may hold values from 0.5 to 1.5
- feed_bias: float32 [512], replicated, may hold values from -1.75 to 1.75
- up_weight: bfloat16 [512, 2048], P(None, 'seq'), may hold values from -0.25 to 0.25
- up_bias: bfloat16 [2048], P('seq'), may hold values from -3 to 3
- down_weight: bfloat16 [512, 2048], P(None, 'seq'), may hold values from -0.1875 to 0.1875
- down_bias: float32 [512], replicated, may hold values from -1.75 to 1.75
Outputs:
- block_output: bfloat16 [16, 2048, 512], P('dp', 'seq')
- input_grad: float32 [16, 2048, 512], P('dp', 'seq')
- mixer_gain_grad: float32 [512], replicated
- mixer_bias_grad: float32 [512], replicated
- query_weight_grad: float32 [512, 512], replicated
- key_weight_grad: float32 [512, 512], replicated
- value_weight_grad: float32 [512, 512], replicated
- gate_weight_grad: float32 [512, 8], replicated
- gate_bias_grad: float32 [8], replicated
- output_weight_grad: float32 [512, 512], replicated
- start_state_grad: float32 [8, 256, 64], replicated
- start_norm_grad: float32 [8, 256], replicated
- feed_gain_grad: float32 [512], replicated
- feed_bias_grad: float32 [512], replicated
- up_weight_grad: float32 [512, 2048], P(None, 'seq')
- up_bias_grad: float32 [2048], P('seq')
- down_weight_grad: float32 [512, 2048], P(None, 'seq')
- down_bias_grad: float32 [512], replicated
All inputs are finite; a program needn't handle non-finite values.
Results may differ from a plain program's by a relative error of at most 0.02.
Values may be sent and summed in bfloat16 or wider, within the bound.
A program may use at most 256 MiB of HBM per device.

v0:
```python
from functools import partial
import math

import jax
import jax.numpy as jnp
from jax import lax
from jax.sharding import PartitionSpec as P

GROUP = 32


EPS_NORM = 1e-05
EPS_UNIT = 1e-06
GUARD = 0.0625
HIGH = lax.Precision.HIGHEST
CONTRACT_ROWS = (((0,), (0,)), ((), ()))
CONTRACT_LAST = (((1,), (1,)), ((), ()))


def carried_in(array, axis, combine, identity):
    length, index = (lax.axis_size(axis), lax.axis_index(axis))
    everything = jax.tree.map(
        lambda part, kind: lax.all_gather(part.astype(kind), axis),
        array,
        (jnp.bfloat16, jnp.bfloat16, jnp.bfloat16),
    )
    start = jax.tree.map(
        lambda part, zero: jnp.broadcast_to(jnp.asarray(zero, part.dtype), part.shape),
        array,
        identity,
    )

    def turn(k, before):
        reached = k < index
        new = combine(
            before, jax.tree.map(lambda part, own: part[k].astype(own.dtype), everything, array)
        )
        return jax.tree.map(lambda a, b: jnp.where(reached, a, b), new, before)

    return lax.fori_loop(0, length, turn, start)


def carried_in_2(array, axis, combine, identity):
    length, index = (lax.axis_size(axis), lax.axis_index(axis))
    everything = jax.tree.map(
        lambda part, kind: lax.all_gather(part.astype(kind), axis),
        array,
        jax.tree.map(lambda a: jnp.bfloat16 if a.dtype == jnp.float32 else a.dtype, array),
    )
    start = jax.tree.map(
        lambda part, zero: jnp.broadcast_to(jnp.asarray(zero, part.dtype), part.shape),
        array,
        identity,
    )

    def turn(k, before):
        at = length - 1 - k
        reached = at > index
        new = combine(
            before, jax.tree.map(lambda part, own: part[at].astype(own.dtype), everything, array)
        )
        return jax.tree.map(lambda a, b: jnp.where(reached, a, b), new, before)

    return lax.fori_loop(0, length, turn, start)


def layer_norm(values_in, gain_row, bias_row):
    centred = values_in - jnp.mean(values_in, axis=-1, keepdims=True)
    scaling = lax.rsqrt(jnp.mean(centred * centred, axis=-1, keepdims=True) + EPS_NORM)
    return centred * scaling * gain_row + bias_row


def gelu_exact(values_in):
    return jax.nn.gelu(values_in, approximate=False)


def row_product(left, right):
    return lax.dot_general(left, right, CONTRACT_ROWS, preferred_element_type=jnp.float32)


def last_product(left, right):
    return lax.dot_general(left, right, CONTRACT_LAST, preferred_element_type=jnp.float32)


def unit_features(vectors, projections):
    unit_rows = vectors * lax.rsqrt(jnp.sum(vectors * vectors, axis=-1, keepdims=True) + EPS_UNIT)
    angles = jnp.einsum("rnchd,hdf->rnchf", unit_rows, projections, precision=HIGH)
    return jnp.concatenate([jnp.sin(angles), jnp.cos(angles)], axis=-1) / math.sqrt(
        projections.shape[2]
    )


def prepare(query_flat, key_flat, value_flat, logit_flat, projections, row_count, group_width):
    head_count = projections.shape[0]
    head_size = projections.shape[1]
    blocks = query_flat.shape[0] // (row_count * group_width)
    layout = (row_count, blocks, group_width, head_count, head_size)
    query_feats = unit_features(query_flat.reshape(layout), projections).astype(jnp.bfloat16)
    key_feats = unit_features(key_flat.reshape(layout), projections).astype(jnp.bfloat16)
    value_rows = value_flat.reshape(layout).astype(jnp.bfloat16)
    logit_rows = logit_flat.reshape(layout[:4])
    decay_log = jnp.cumsum(jax.nn.log_sigmoid(logit_rows), axis=2)
    inflow = jax.nn.sigmoid(-logit_rows)
    to_end = jnp.exp(decay_log[:, :, -1:, :] - decay_log) * inflow
    weighted = (key_feats.astype(jnp.float32) * to_end[..., None]).astype(jnp.bfloat16)
    group_state = jnp.einsum(
        "rnshf,rnshd->rnhfd", weighted, value_rows, preferred_element_type=jnp.float32
    )
    group_norm = jnp.sum(weighted.astype(jnp.float32), axis=2)
    return (query_feats, key_feats, value_rows, decay_log, inflow, group_state, group_norm)


def summarize(prepared):
    decay_log = prepared[3]
    group_state = prepared[5]
    group_norm = prepared[6]
    running = jnp.cumsum(decay_log[:, :, -1, :], axis=1)
    to_end = jnp.exp(running[:, -1:, :] - running)
    device_state = jnp.einsum("rnh,rnhfd->rhfd", to_end, group_state, precision=HIGH)
    device_norm = jnp.einsum("rnh,rnhf->rhf", to_end, group_norm, precision=HIGH)
    return (jnp.exp(running[:, -1, :]), device_state, device_norm)


def mix_output(prepared, entry_state, entry_norm):
    query_feats, key_feats, value_rows, decay_log, inflow, group_state, group_norm = prepared
    blocks = decay_log.shape[1]
    group_width = decay_log.shape[2]
    group_log = decay_log[:, :, -1, :]
    running = jnp.cumsum(group_log, axis=1)
    before = running - group_log
    earlier_mask = (jnp.arange(blocks)[:, None] > jnp.arange(blocks)[None, :])[None, None]
    spread = before.transpose(0, 2, 1)[:, :, :, None] - running.transpose(0, 2, 1)[:, :, None, :]
    carry_weights = jnp.where(earlier_mask, jnp.exp(jnp.where(earlier_mask, spread, 0.0)), 0.0)
    starts = (
        jnp.einsum("rhcb,rbhfd->rchfd", carry_weights, group_state, precision=HIGH)
        + jnp.exp(before)[:, :, :, None, None] * entry_state[:, None]
    )
    start_norms = (
        jnp.einsum("rhcb,rbhf->rchf", carry_weights, group_norm, precision=HIGH)
        + jnp.exp(before)[:, :, :, None] * entry_norm[:, None]
    )
    causal = (jnp.arange(group_width)[:, None] >= jnp.arange(group_width)[None, :])[
        None, None, None
    ]
    logs_first = decay_log.transpose(0, 1, 3, 2)
    log_gap = logs_first[..., :, None] - logs_first[..., None, :]
    decay_pairs = (
        jnp.where(causal, jnp.exp(jnp.where(causal, log_gap, 0.0)), 0.0)
        * inflow.transpose(0, 1, 3, 2)[..., None, :]
    )
    raw_scores = jnp.einsum(
        "rnthf,rnshf->rnhts", query_feats, key_feats, preferred_element_type=jnp.float32
    )
    scores_low = (raw_scores * decay_pairs).astype(jnp.bfloat16)
    inner_sum = jnp.einsum(
        "rnhts,rnshd->rnthd", scores_low, value_rows, preferred_element_type=jnp.float32
    )
    lifted = query_feats.astype(jnp.float32) * jnp.exp(decay_log)[..., None]
    numerator = inner_sum + jnp.einsum("rnthf,rnhfd->rnthd", lifted, starts, precision=HIGH)
    denominator = jnp.sum(scores_low.astype(jnp.float32), axis=-1).transpose(
        0, 1, 3, 2
    ) + jnp.einsum("rnthf,rnhf->rnth", lifted, start_norms, precision=HIGH)
    mixed_rows = numerator * lax.rsqrt(denominator * denominator + GUARD)[..., None]
    return mixed_rows.reshape(-1, mixed_rows.shape[3] * mixed_rows.shape[4])


def chain_combine(first_part, second_part):
    first_decay, first_state, first_norm = first_part
    second_decay, second_state, second_norm = second_part
    return (
        first_decay * second_decay,
        second_decay[:, :, None, None] * first_state + second_state,
        second_decay[:, :, None] * first_norm + second_norm,
    )


def local(
    inputs,
    cotangent,
    mixer_gain,
    mixer_bias,
    query_weight,
    key_weight,
    value_weight,
    gate_weight,
    gate_bias,
    output_weight,
    projections,
    start_state,
    start_norm,
    feed_gain,
    feed_bias,
    up_weight,
    up_bias,
    down_weight,
    down_bias,
):
    row_count, span, model_width = inputs.shape
    tokens_here = row_count * span
    flat_input = inputs.reshape(tokens_here, model_width).astype(jnp.float32)
    mixer_in, mixer_back = jax.vjp(layer_norm, flat_input, mixer_gain, mixer_bias)
    mixer_low = mixer_in.astype(jnp.bfloat16)
    query_flat = jnp.dot(mixer_low, query_weight, preferred_element_type=jnp.float32)
    key_flat = jnp.dot(mixer_low, key_weight, preferred_element_type=jnp.float32)
    value_flat = jnp.dot(mixer_low, value_weight, preferred_element_type=jnp.float32)
    logit_flat = jnp.dot(mixer_low, gate_weight, preferred_element_type=jnp.float32) + gate_bias
    prepared, prepare_back = jax.vjp(
        partial(prepare, projections=projections, row_count=row_count, group_width=GROUP),
        query_flat,
        key_flat,
        value_flat,
        logit_flat,
    )
    summary, summary_back = jax.vjp(summarize, prepared)
    device_decay, device_state, device_norm = summary
    identity = (
        jnp.ones_like(device_decay),
        jnp.zeros_like(device_state),
        jnp.zeros_like(device_norm),
    )
    entry_decay, entry_state, entry_norm = carried_in(
        (device_decay, device_state, device_norm), "seq", chain_combine, identity
    )
    begin_state = entry_decay[:, :, None, None] * start_state[None] + entry_state
    begin_norm = entry_decay[:, :, None] * start_norm[None] + entry_norm
    mixed, mix_back = jax.vjp(mix_output, prepared, begin_state, begin_norm)
    mixed_low = mixed.astype(jnp.bfloat16)
    middle = flat_input + jnp.dot(mixed_low, output_weight, preferred_element_type=jnp.float32)
    feed_in, feed_back = jax.vjp(layer_norm, middle, feed_gain, feed_bias)
    feed_low = feed_in.astype(jnp.bfloat16)
    grad_low = cotangent.reshape(tokens_here, model_width)
    grad_out = grad_low.astype(jnp.float32)
    gathered = lax.all_gather(feed_low, "seq", axis=0, tiled=True)
    hidden_pre = jnp.dot(gathered, up_weight, preferred_element_type=jnp.float32) + up_bias.astype(
        jnp.float32
    )
    hidden, gelu_back = jax.vjp(gelu_exact, hidden_pre)
    hidden_low = hidden.astype(jnp.bfloat16)
    feed_out = lax.psum_scatter(
        last_product(hidden_low, down_weight).astype(jnp.bfloat16),
        "seq",
        scatter_dimension=0,
        tiled=True,
    ).astype(jnp.float32)
    block_output = (middle + feed_out + down_bias).astype(jnp.bfloat16)
    every_grad = lax.all_gather(grad_low, "seq", axis=0, tiled=True)
    down_grad = row_product(every_grad, hidden_low)
    hidden_grad = jnp.dot(every_grad, down_weight, preferred_element_type=jnp.float32)
    pre_low = gelu_back(hidden_grad)[0].astype(jnp.bfloat16)
    up_grad = row_product(gathered, pre_low)
    up_bias_grad = jnp.sum(pre_low.astype(jnp.float32), axis=0)
    feed_grad = lax.psum_scatter(
        last_product(pre_low, up_weight).astype(jnp.bfloat16),
        "seq",
        scatter_dimension=0,
        tiled=True,
    ).astype(jnp.float32)
    middle_part, feed_gain_grad, feed_bias_grad = feed_back(feed_grad)
    middle_grad = grad_out + middle_part
    branch_low = middle_grad.astype(jnp.bfloat16)
    output_grad = row_product(mixed_low, branch_low)
    mixed_grad = last_product(branch_low, output_weight)
    prepared_grad, begin_state_grad, begin_norm_grad = mix_back(mixed_grad)
    unused_decay, after_state, after_norm = carried_in_2(
        (device_decay, begin_state_grad, begin_norm_grad), "seq", chain_combine, identity
    )
    decay_grad = jnp.sum(begin_state * after_state, axis=(2, 3)) + jnp.sum(
        begin_norm * after_norm, axis=2
    )
    summary_grad = summary_back((decay_grad, after_state, after_norm))[0]
    total_grad = jax.tree.map(jnp.add, prepared_grad, summary_grad)
    query_grad, key_grad, value_grad, logit_grad = prepare_back(total_grad)
    leading = lax.axis_index("seq") == 0
    state_grad = jnp.where(
        leading,
        jnp.sum(begin_state_grad + device_decay[:, :, None, None] * after_state, axis=0),
        0.0,
    )
    norm_grad = jnp.where(
        leading, jnp.sum(begin_norm_grad + device_decay[:, :, None] * after_norm, axis=0), 0.0
    )
    query_low = query_grad.astype(jnp.bfloat16)
    key_low = key_grad.astype(jnp.bfloat16)
    value_low = value_grad.astype(jnp.bfloat16)
    logit_low = logit_grad.astype(jnp.bfloat16)
    mixer_grad = (
        last_product(query_low, query_weight)
        + last_product(key_low, key_weight)
        + last_product(value_low, value_weight)
        + last_product(logit_low, gate_weight)
    )
    input_part, mixer_gain_grad, mixer_bias_grad = mixer_back(mixer_grad)
    input_grad = (middle_grad + input_part).reshape(inputs.shape)
    (
        sum_mixer_gain,
        sum_mixer_bias,
        sum_query,
        sum_key,
        sum_value,
        sum_gate,
        sum_gate_bias,
        sum_output,
        sum_state,
        sum_norm,
        sum_feed_gain,
        sum_feed_bias,
        sum_down_bias,
    ) = lax.psum(
        (
            mixer_gain_grad,
            mixer_bias_grad,
            row_product(mixer_low, query_low),
            row_product(mixer_low, key_low),
            row_product(mixer_low, value_low),
            row_product(mixer_low, logit_low),
            jnp.sum(logit_low.astype(jnp.float32), axis=0),
            output_grad,
            state_grad,
            norm_grad,
            feed_gain_grad,
            feed_bias_grad,
            jnp.sum(grad_out, axis=0),
        ),
        ("dp", "seq"),
    )
    sum_up, sum_up_bias, sum_down = (
        lax.psum(up_grad.astype(jnp.bfloat16), "dp").astype(jnp.float32),
        lax.psum(up_bias_grad.astype(jnp.bfloat16), "dp").astype(jnp.float32),
        lax.psum(down_grad.astype(jnp.bfloat16), "dp").astype(jnp.float32),
    )
    return (
        block_output.reshape(inputs.shape),
        input_grad,
        sum_mixer_gain,
        sum_mixer_bias,
        sum_query,
        sum_key,
        sum_value,
        sum_gate,
        sum_gate_bias,
        sum_output,
        sum_state,
        sum_norm,
        sum_feed_gain,
        sum_feed_bias,
        sum_up,
        sum_up_bias,
        sum_down,
        sum_down_bias,
    )


def solution(mesh):
    placed = (
        P("dp", "seq", None),
        P("dp", "seq", None),
        P(),
        P(),
        P(),
        P(),
        P(),
        P(),
        P(),
        P(),
        P(),
        P(),
        P(),
        P(),
        P(),
        P(None, "seq"),
        P("seq"),
        P(None, "seq"),
        P(),
    )
    return jax.shard_map(
        local,
        mesh=mesh,
        in_specs=placed,
        out_specs=(
            P("dp", "seq", None),
            P("dp", "seq", None),
            P(),
            P(),
            P(),
            P(),
            P(),
            P(),
            P(),
            P(),
            P(),
            P(),
            P(),
            P(),
            P(None, "seq"),
            P("seq"),
            P(None, "seq"),
            P(),
        ),
        check_vma=False,
    )
```

profile of v0, /device:TPU:0, one launch (start us, length us, event | category | flops | bytes accessed | tf_op | source)
XLA Modules:
  0.0 1146.8 jit_solution(16693976910965578052)
XLA Ops:
  72.8 29.6 %fusion.246 = (f32[8,32,32,128]{3,2,1,0:T(8,128)S(1)}, f32[8,32,32,128]{3,2,1,0:T(8,128)S(1)}) fusion(f32[8,64,128]{2,1,0:T(8,128)S(1)} %copy-done.46, f32[32,32,8,64]{3,2,1,0:T(8,128)} %reshape.1483, f32[32,32,8]{1,0,2:T(8,128)} %copy.612), kind=kOutput, calls=%fused_computation.363 | convolution fusion | flops 805830656 | bytes 10780672 | tf_op jit(solution)/shard_map/jvp(rnchd,hdf->rnchf)/dot_general | solution.py:87
  102.4 32.7 %fusion.247 = (f32[8,32,32,128]{3,2,1,0:T(8,128)S(1)}, f32[8,32,32,128]{3,2,1,0:T(8,128)S(1)}) fusion(f32[8,64,128]{2,1,0:T(8,128)S(1)} %copy-done.46, f32[32,32,8,64]{3,2,1,0:T(8,128)S(1)} %copy-done.18, f32[32,32,8]{1,0,2:T(8,128)S(1)} %copy-done.57), kind=kOutput, calls=%fused_computation.364 | convolution fusion | flops 805830656 | bytes 10780672 | tf_op jit(solution)/shard_map/jvp(rnchd,hdf->rnchf)/dot_general | solution.py:87
  136.4 8.7 convert_multiply_fusion.4
  145.1 8.2 fusion.89
  153.3 110.0 %fusion.24 = bf16[8,1,256,64]{1,2,3,0:T(8,128)(2,1)} fusion(f32[32,8,1,1]{0,2,3,1:T(1,128)S(1)} %bitcast.645, f32[32,8,256,64]{2,3,1,0:T(8,128)} %fusion.89), kind=kOutput, calls=%fused_computation.39 | convolution fusion | flops 50331648 | bytes 17040384 | tf_op jit(solution)/shard_map/jvp(rnh,rnhfd->rhfd)/dot_general | solution.py:119
  263.3 27.2 %copy.721 = bf16[8,1,256,64]{2,3,0,1:T(8,128)(2,1)S(1)} copy(bf16[8,1,256,64]{1,2,3,0:T(8,128)(2,1)} %fusion.24) | data formatting | bytes 524288 | tf_op jit(solution)/shard_map/jvp(rnh,rnhfd->rhfd)/dot_general | solution.py:119
  290.4 8.1 all-gather
  321.1 34.3 %fusion.8 = f32[32,8,256,64]{2,0,3,1:T(8,128)} fusion(f32[32,8,256,64]{2,3,1,0:T(8,128)} %fusion.89, f32[8,256,64]{1,2,0:T(8,128)} %copy.642, f32[32,8]{0,1:T(8,128)} %get-tuple-element.703, f32[8,32]{1,0:T(8,128)S(1)} %copy.636, f32[8,32]{1,0:T(8,128)S(1)} %subtract_bitcast_fusion, pred[32,32]{1,0:T(8,128)(4,1)} %iota_compare_fusion), kind=kOutput, calls=%fused_computation.19 | convolution fusion | flops 1619025920 | bytes 34082816 | tf_op jit(solution)/shard_map/jvp(rhcb,rbhfd->rchfd)/dot_general | solution.py:135
  355.5 9.3 fusion.53
  364.8 31.1 %fusion.21 = f32[32,8,64,32]{2,3,1,0:T(8,128)S(1)} fusion(f32[32,8,256,64]{2,0,3,1:T(8,128)} %fusion.8, f32[32,32,8,256]{3,1,0,2:T(8,128)} %get-tuple-element.681), kind=kOutput, calls=%fused_computation.35 | convolution fusion | flops 1610612736 | bytes 27262976 | tf_op jit(solution)/shard_map/jvp(rnthf,rnhfd->rnthd)/dot_general | solution.py:159
  411.3 33.8 %all-gather.8.cloned.1.call-done = bf16[2048,512]{0,1:T(8,128)(2,1)} async-done(((bf16[1024,512]{0,1:T(8,128)(2,1)}), bf16[2048,512]{0,1:T(8,128)(2,1)}) %all-gather.8.cloned.1.call-update) | async-done | bytes 2097168 | tf_op jit(solution)/shard_map/all_gather | solution.py:233
  445.2 23.3 %multiply_convert_fusion = (bf16[2048,1024]{1,0:T(8,128)(2,1)}, f32[2048,1024]{1,0:T(8,128)}, f32[2048,1024]{1,0:T(8,128)}) fusion(f32[1024]{0:T(1024)S(1)} %convert_element_type.533, bf16[2048,512]{0,1:T(8,128)(2,1)} %all-gather.8.cloned.1.call-done, bf16[512,1024]{1,0:T(8,128)(2,1)S(1)} %copy-done), kind=kOutput, calls=%fused_computation.69 | convolution fusion | flops 2285895680 | bytes 24121344 | tf_op jit(solution)/shard_map/dot_general | solution.py:234
  468.5 11.4 all-gather.10.cloned.1.call-done
  486.2 9.2 fusion.250
  513.5 33.5 %psum.125 = bf16[1024]{0:T(1024)(128)(2,1)S(1)} all-reduce(bf16[1024]{0:T(1024)(128)(2,1)S(1)} %get-tuple-element.724), channel_id=1, replica_groups=mesh['dp'=16,'seq'=2] {'dp'}, use_global_device_ids=true, to_apply=%region_60.61 | all-reduce | flops 1024 | bytes 4096 | tf_op jit(solution)/shard_map/psum | solution.py:328
  553.9 45.0 %all-reduce.13.cloned.1.call-done = (bf16[512,1024]{0,1:T(8,128)(2,1)}, bf16[512,1024]{1,0:T(8,128)(2,1)}) async-done(((bf16[512,1024]{0,1:T(8,128)(2,1)}, bf16[512,1024]{1,0:T(8,128)(2,1)}), (bf16[512,1024]{0,1:T(8,128)(2,1)}, bf16[512,1024]{1,0:T(8,128)(2,1)})) %all-reduce.13.cloned.1.call-update) | async-done | bytes 2097168 | tf_op jit(solution)/shard_map/psum | solution.py:329
  604.2 28.1 %reduce-scatter.5.cloned.1.call-done = bf16[1024,512]{0,1:T(8,128)(2,1)} async-done(((bf16[2048,512]{0,1:T(8,128)(2,1)}), bf16[1024,512]{0,1:T(8,128)(2,1)}) %reduce-scatter.5.cloned.1.call-update) | async-done | bytes 1048592 | tf_op jit(solution)/shard_map/reduce_scatter | solution.py:252
  653.3 18.0 %fusion.49 = f32[32,8,64,256]{3,2,1,0:T(8,128)S(1)} fusion(f32[32,8,64,32]{2,3,1,0:T(8,128)} %get-tuple-element.686, f32[32,32,8,256]{3,1,0,2:T(8,128)} %get-tuple-element.681), kind=kOutput, calls=%fused_computation.86 | convolution fusion | flops 1610612736 | bytes 27262976 | tf_op jit(solution)/shard_map/transpose(jvp(rnthf,rnhfd->rnthd))/dot_general | solution.py:159
  671.4 13.7 %fusion.14 = (f32[32,8]{0,1:T(8,128)}, f32[8,256,64]{1,2,0:T(8,128)S(1)}) fusion(f32[32,8,64,256]{3,2,1,0:T(8,128)S(1)} %fusion.49, f32[8,256,64]{1,2,0:T(8,128)S(1)} %copy-done.34, f32[32,8]{0,1:T(8,128)S(1)} %copy-done.93), kind=kLoop, calls=%fused_computation.27 | loop fusion | flops 16645888 | bytes 17827840 | tf_op jit(solution)/shard_map/transpose(jvp())/reduce_sum | solution.py:136
  686.0 8.8 all-gather.3
  707.9 9.6 while.37
  718.6 36.0 %add_bitcast_fusion = bf16[32,8,256,64]{2,0,3,1:T(8,128)(2,1)} fusion(f32[32,8,64,256]{3,2,1,0:T(8,128)} %copy-done.2, f32[8,32]{1,0:T(8,128)} %bitcast.647, f32[8,256,64]{1,2,0:T(8,128)} %copy.673, f32[8,32]{1,0:T(8,128)S(1)} %copy.636, f32[8,32]{1,0:T(8,128)S(1)} %subtract_bitcast_fusion, pred[32,32]{1,0:T(8,128)(4,1)} %iota_compare_fusion), kind=kOutput, calls=%fused_computation.37 | convolution fusion | flops 1623220224 | bytes 25694208 | tf_op jit(solution)/shard_map/transpose(jvp(rhcb,rbhfd->rchfd))/dot_general | solution.py:135
  755.2 13.3 %fusion.35 = (f32[32,32,8]{1,0,2:T(8,128)}, bf16[1,32,8,256,32]{3,4,1,2,0:T(8,128)(2,1)}) fusion(f32[1,32,32,8,128]{4,2,1,3,0:T(8,128)} %bitcast.628, f32[1,32,32,8,128]{4,2,1,3,0:T(8,128)S(1)} %bitcast.625, bf16[32,32,8,64]{3,1,2,0:T(8,128)(2,1)S(1)} %copy-done.33, bf16[32,8,256,64]{2,0,3,1:T(8,128)(2,1)} %add_bitcast_fusion, ...), kind=kOutput, calls=%fused_computation.49 | convolution fusion | flops 285204480 | bytes 22183936 | tf_op jit(solution)/shard_map/transpose(jvp(rnshf,rnshd->rnhfd))/dot_general | solution.py:106
  771.9 8.1 multiply_reduce_fusion
  782.5 43.0 %fusion.142 = f32[8,32,32]{2,1,0:T(8,128)} fusion(f32[32,8,256,64]{2,3,1,0:T(8,128)} %fusion.89, f32[32,8,64,256]{3,2,1,0:T(8,128)} %copy-done.2), kind=kOutput, calls=%fused_computation.211 | convolution fusion | flops 1610612736 | bytes 33587200 | tf_op jit(solution)/shard_map/transpose(jvp(rhcb,rbhfd->rchfd))/dot_general | solution.py:135
  831.2 31.1 %fusion.42 = (f32[32,32,8]{1,0,2:T(8,128)S(1)}, f32[32,8,32,256]{3,2,0,1:T(8,128)}) fusion(f32[1,32,32,8,128]{4,2,1,3,0:T(8,128)} %bitcast.621, f32[1,32,32,8,128]{4,2,1,3,0:T(8,128)} %bitcast.619, f32[32,8,256]{2,0,1:T(8,128)S(1)} %bitcast.632, f32[32,8,32]{2,0,1:T(8,128)S(1)} %copy.651, f32[32,8,256,64]{2,0,3,1:T(8,128)} %fusion.8, ...), kind=kOutput, calls=%fused_computation.62 | convolution fusion | flops 1627381760 | bytes 35979264 | tf_op jit(solution)/shard_map/transpose(jvp(rnthf,rnhfd->rnthd))/dot_general | solution.py:159
  887.5 15.9 %add_bitcast_fusion.2 = bf16[1,32,32,8,64]{4,2,3,1,0:T(8,128)(2,1)} fusion(bf16[32,8,64,32]{2,3,1,0:T(8,128)(2,1)} %fusion.260, bf16[32,32,8,256]{3,1,0,2:T(8,128)(2,1)} %copy-done.23, bf16[32,8,256,64]{2,0,3,1:T(8,128)(2,1)} %add_bitcast_fusion), kind=kOutput, calls=%fused_computation.190 | convolution fusion | flops 268959744 | bytes 14680064 | tf_op jit(solution)/shard_map/transpose(jvp(rnshf,rnshd->rnhfd))/dot_general | solution.py:106
  911.5 6.6 convert_multiply_fusion.3
  920.4 7.0 fusion.73
  947.5 7.4 fusion.72
  1002.8 40.7 %all-reduce.5 = (f32[512]{0:T(512)}, f32[512]{0:T(512)}, f32[512,8]{0,1:T(8,128)}, f32[8]{0:T(128)}, f32[8,256]{1,0:T(8,128)}, /*index=5*/f32[512]{0:T(512)}, f32[512]{0:T(512)}, f32[512]{0:T(512)}) all-reduce(f32[512]{0:T(512)S(1)} %get-tuple-element.614, ...), channel_id=1, replica_groups=mesh['dp'=16,'seq'=2] {'dp','seq'}, use_global_device_ids=true, to_apply=%region_42.43 | all-reduce | flops 8712 | bytes 69696 | tf_op jit(solution)/shard_map/psum | solution.py:308
  1043.5 88.9 %all-reduce.11.cloned.1.call-done = (f32[512,512]{1,0:T(8,128)}, f32[512,512]{1,0:T(8,128)}, f32[512,512]{1,0:T(8,128)}, f32[512,512]{1,0:T(8,128)}, f32[8,256,64]{1,2,0:T(8,128)}) async-done(((f32[512,512]{1,0:T(8,128)}, f32[512,512]{1,0:T(8,128)}, f32[512,512]{1,0:T(8,128)}, f32[512,512]{1,0:T(8,128)}, f32[8,256,64]{1,2,0:T(8,128)}), (f32[512,512]{1,0:T(8,128)}, f32[512,512]{1,0:T(8,128)}, ...) | async-done | bytes 4718608 | tf_op jit(solution)/shard_map/psum | solution.py:308
  (498 shorter events, 312.4 us)
Async XLA Ops:
  7.2 438.0 %copy-start = (bf16[512,1024]{1,0:T(8,128)(2,1)S(1)}, bf16[512,1024]{1,0:T(8,128)(2,1)}, u32[]{:S(2)}) copy-start(bf16[512,1024]{1,0:T(8,128)(2,1)} %param.38) | copy-start | bytes 3145732
  7.2 437.9 %all-gather.8.cloned.1.call-start = ((), (), s32[]{:S(2)}) async-start(), calls=%async_computation.2 | async-start | bytes 3145728 | tf_op jit(solution)/shard_map/all_gather | solution.py:233
  54.2 244.4 %copy-start.51 = (f32[32,32,8]{1,0,2:T(8,128)}, f32[32,32,8]{1,0,2:T(8,128)S(1)}, u32[]{:S(2)}) copy-start(f32[32,32,8]{1,0,2:T(8,128)S(1)} %copy.632) | copy-start | bytes 98308
  69.2 233.9 %copy-start.94 = (f32[32,8]{0,1:T(8,128)}, f32[32,8]{0,1:T(8,128)S(1)}, u32[]{:S(2)}) copy-start(f32[32,8]{0,1:T(8,128)S(1)} %get-tuple-element.704) | copy-start | bytes 3076
  72.7 63.7 %copy-start.60 = (f32[32,32,8]{1,0,2:T(8,128)}, f32[32,32,8]{1,0,2:T(8,128)S(1)}, u32[]{:S(2)}) copy-start(f32[32,32,8]{1,0,2:T(8,128)S(1)} %copy.643) | copy-start | bytes 98308
  102.4 34.0 %copy-start.5 = (f32[8,32,32,128]{3,2,1,0:T(8,128)}, f32[8,32,32,128]{3,2,1,0:T(8,128)S(1)}, u32[]{:S(2)}) copy-start(f32[8,32,32,128]{3,2,1,0:T(8,128)S(1)} %get-tuple-element.687) | copy-start | bytes 12582916
  102.4 34.0 %copy-start.7 = (f32[8,32,32,128]{3,2,1,0:T(8,128)}, f32[8,32,32,128]{3,2,1,0:T(8,128)S(1)}, u32[]{:S(2)}) copy-start(f32[8,32,32,128]{3,2,1,0:T(8,128)S(1)} %get-tuple-element.688) | copy-start | bytes 12582916
  311.3 44.1 %copy-start.16 = (f32[1,8,256,64]{3,2,1,0:T(8,128)}, f32[1,8,256,64]{3,2,1,0:T(8,128)S(1)}, u32[]{:S(2)}) copy-start(f32[1,8,256,64]{3,2,1,0:T(8,128)S(1)} %get-tuple-element.337) | copy-start | bytes 1572868
  311.3 44.1 %copy-start.88 = (f32[1,8,256]{2,1,0:T(8,128)}, f32[1,8,256]{2,1,0:T(8,128)S(1)}, u32[]{:S(2)}) copy-start(f32[1,8,256]{2,1,0:T(8,128)S(1)} %get-tuple-element.338) | copy-start | bytes 24580
  313.6 82.3 %copy-start.64 = (f32[32,8,32]{2,1,0:T(8,128)}, f32[32,8,32]{2,1,0:T(8,128)S(1)}, u32[]{:S(2)}) copy-start(f32[32,8,32]{2,1,0:T(8,128)S(1)} %copy.625) | copy-start | bytes 98308
  315.1 40.4 %copy-start.27 = (f32[8,256,64]{2,1,0:T(8,128)}, f32[8,256,64]{2,1,0:T(8,128)S(1)}, u32[]{:S(2)}) copy-start(f32[8,256,64]{2,1,0:T(8,128)S(1)} %copy.641) | copy-start | bytes 1572868
  320.0 35.4 %copy-start.105 = (f32[8,256]{1,0:T(8,128)}, f32[8,256]{1,0:T(8,128)S(1)}, u32[]{:S(2)}) copy-start(f32[8,256]{1,0:T(8,128)S(1)} %fusion.226) | copy-start | bytes 24580
  321.1 34.3 %copy-start.38 = (f32[1,32,8,256]{3,1,2,0:T(8,128)}, f32[1,32,8,256]{3,1,2,0:T(8,128)S(1)}, u32[]{:S(2)}) copy-start(f32[1,32,8,256]{3,1,2,0:T(8,128)S(1)} %fusion.136) | copy-start | bytes 786436
  408.8 229.1 %copy-start.98 = (f32[1024]{0:T(1024)}, f32[1024]{0:T(1024)S(1)}, u32[]{:S(2)}) copy-start(f32[1024]{0:T(1024)S(1)} %broadcast_multiply_fusion) | copy-start | bytes 12292
  409.2 228.8 %copy-start.103 = (f32[1024]{0:T(1024)}, f32[1024]{0:T(1024)S(1)}, u32[]{:S(2)}) copy-start(f32[1024]{0:T(1024)S(1)} %fusion.225) | copy-start | bytes 12292
  410.5 69.3 %all-gather.10.cloned.1.call-start = ((), (), s32[]{:S(2)}) async-start(), calls=%async_computation.5 | async-start | bytes 3145728 | tf_op jit(solution)/shard_map/all_gather | solution.py:246
  411.3 187.6 %all-reduce.13.cloned.1.call-start = ((), (), s32[]{:S(2)}) async-start(), calls=%async_computation.7 | async-start | bytes 4194304 | tf_op jit(solution)/shard_map/psum | solution.py:329
  500.7 131.7 %reduce-scatter.5.cloned.1.call-start = ((), (), s32[]{:S(2)}) async-start(), calls=%async_computation.4 | async-start | bytes 3145728 | tf_op jit(solution)/shard_map/reduce_scatter | solution.py:252
  507.1 485.2 %reduce-scatter.3.cloned.1.call-start = ((), (), s32[]{:S(2)}) async-start(), calls=%async_computation.3 | async-start | bytes 3145728 | tf_op jit(solution)/shard_map/reduce_scatter | solution.py:239
  553.8 578.6 %all-reduce.11.cloned.1.call-start = ((), (), s32[]{:S(2)}) async-start(), calls=%async_computation.6 | async-start | bytes 9437184 | tf_op jit(solution)/shard_map/psum | solution.py:308
  717.5 37.1 %copy-start.90 = (f32[1,8,256]{2,1,0:T(8,128)}, f32[1,8,256]{2,1,0:T(8,128)S(1)}, u32[]{:S(2)}) copy-start(f32[1,8,256]{2,1,0:T(8,128)S(1)} %get-tuple-element.339) | copy-start | bytes 24580
  718.6 36.0 %copy-start.49 = (f32[32,8,1,256]{3,2,1,0:T(1,128)S(1)}, f32[32,8,1,256]{3,2,1,0:T(1,128)}, u32[]{:S(2)}) copy-start(f32[32,8,1,256]{3,2,1,0:T(1,128)} %copy-done.48) | copy-start | bytes 786436
  718.6 36.0 %copy-start.95 = (f32[32,8]{0,1:T(8,128)S(1)}, f32[32,8]{0,1:T(8,128)}, u32[]{:S(2)}) copy-start(f32[32,8]{0,1:T(8,128)} %copy-done.94) | copy-start | bytes 3076
  718.6 36.0 %copy-start.100 = (pred[32,32]{1,0:T(8,128)(4,1)S(1)}, pred[32,32]{1,0:T(8,128)(4,1)}, u32[]{:S(2)}) copy-start(pred[32,32]{1,0:T(8,128)(4,1)} %iota_compare_fusion) | copy-start | bytes 3076
  718.6 36.6 %copy-start.10 = (f32[8,32,32,128]{3,2,1,0:T(8,128)S(1)}, f32[8,32,32,128]{3,2,1,0:T(8,128)}, u32[]{:S(2)}) copy-start(f32[8,32,32,128]{3,2,1,0:T(8,128)} %copy-done.9) | copy-start | bytes 12582916
  718.6 36.6 %copy-start.33 = (bf16[32,32,8,64]{3,1,2,0:T(8,128)(2,1)S(1)}, bf16[32,32,8,64]{3,1,2,0:T(8,128)(2,1)}, u32[]{:S(2)}) copy-start(bf16[32,32,8,64]{3,1,2,0:T(8,128)(2,1)} %copy-done.31) | copy-start | bytes 3145732
  782.5 43.0 %copy-start.29 = (bf16[32,8,32,32]{3,2,1,0:T(8,128)(2,1)S(1)}, bf16[32,8,32,32]{3,2,1,0:T(8,128)(2,1)}, u32[]{:S(2)}) copy-start(bf16[32,8,32,32]{3,2,1,0:T(8,128)(2,1)} %copy-done.28) | copy-start | bytes 1572868
  831.1 35.1 %copy-start.89 = (f32[1,8,256]{2,1,0:T(8,128)S(1)}, f32[1,8,256]{2,1,0:T(8,128)}, u32[]{:S(2)}) copy-start(f32[1,8,256]{2,1,0:T(8,128)} %copy-done.88) | copy-start | bytes 24580
  831.1 37.5 %copy-start.50 = (f32[32,8,1,256]{3,2,1,0:T(1,128)S(1)}, f32[32,8,1,256]{3,2,1,0:T(1,128)}, u32[]{:S(2)}) copy-start(f32[32,8,1,256]{3,2,1,0:T(1,128)} %copy-done.48) | copy-start | bytes 786436
  831.1 37.5 %copy-start.81 = (f32[8,32,32]{2,1,0:T(8,128)S(1)}, f32[8,32,32]{2,1,0:T(8,128)}, u32[]{:S(2)}) copy-start(f32[8,32,32]{2,1,0:T(8,128)} %fusion.142) | copy-start | bytes 98308
  831.1 38.7 %copy-start.56 = (f32[1,32,32,8]{1,3,2,0:T(8,128)S(1)}, f32[1,32,32,8]{1,3,2,0:T(8,128)}, u32[]{:S(2)}) copy-start(f32[1,32,32,8]{1,3,2,0:T(8,128)} %copy-done.55) | copy-start | bytes 98308
  831.2 40.3 %copy-start.65 = (f32[32,8,32]{2,1,0:T(8,128)S(1)}, f32[32,8,32]{2,1,0:T(8,128)}, u32[]{:S(2)}) copy-start(f32[32,8,32]{2,1,0:T(8,128)} %copy-done.64) | copy-start | bytes 98308
  (119 other events, 1087.7 us)
Sparse Core Ops, SparseCore 0:
  410.6 34.4 all-gather.7
  446.7 33.1 all-gather.9
  500.8 98.0 all-reduce.12
  601.1 31.2 reduce-scatter.4
  634.5 31.8 reduce-scatter.2
  985.0 147.3 all-reduce.10
where the time goes:
time: 1160 us; the launch traced here: 1150 us
  matrix products  554 us (48%)
  waiting for transfers between devices  208 us (18%)
  local copies, waits for them, and re-layouts  145 us (12%)
  other arithmetic  119 us (10%)
  blocking collectives  105 us (9%)
  between operations  15.9 us (1%)
    dot_general x3, matrix products, mix_output(): jnp.einsum('rhcb,rbhfd->rchfd', carry_weights, group_state, precision=HIGH)  113 us
    dot_general x1, matrix products, summarize(): jnp.einsum('rnh,rnhfd->rhfd', to_end, group_state, precision=HIGH)  110 us
    psum x1, waiting for transfers between devices, local(): lax.psum((mixer_gain_grad, mixer_bias_grad, row_product(mixer_low, query_...  88.9 us
    dot_general x3, matrix products, mix_output(): jnp.einsum('rnthf,rnhfd->rnthd', lifted, starts, precision=HIGH)  80.3 us
    dot_general x4, matrix products, unit_features(): jnp.einsum('rnchd,hdf->rnchf', unit_rows, projections, precision=HIGH)  76.7 us
    psum x1, waiting for transfers between devices, local(): lax.psum(down_grad.astype(jnp.bfloat16), 'dp').astype(jnp.float32)  45 us
    psum x1, blocking collectives, local(): lax.psum((mixer_gain_grad, mixer_bias_grad, row_product(mixer_low, query_...  40.7 us
    dot_general x3, matrix products, prepare(): jnp.einsum('rnshf,rnshd->rnhfd', weighted, value_rows, preferred_element_...  37.3 us
  transfers between devices with their start and end apart: 6, of which 5 were waited for; matrix products, arithmetic and copies ran while one was open for 34% of the time, Pallas kernels for 0%

commit v1 on v0

v1 whole, which is shorter than its diff:
```python
from functools import partial
import math

import jax
import jax.numpy as jnp
from jax import lax
from jax.experimental import pallas as pl
from jax.experimental.pallas import tpu as pltpu
from jax.sharding import PartitionSpec as P

F32 = jnp.float32
BF16 = jnp.bfloat16
EPS_NORM = 1e-05
EPS_UNIT = 1e-06
GUARD = 0.0625
HIGH = lax.Precision.HIGHEST
VMEM = 56 * 1024 * 1024

C = 128
T = 256
HB = 512
LANES = 128
PAY = 80

SIN = (3.14158202, -5.16714278, 2.54189892, -0.55463591)
COS = (0.99999995, -4.93479286, 4.05841191, -1.33188012, 0.21969671)
ERF = (0.319381530, -0.356563782, 1.781477937, -1.821255978, 1.330274429)
ERF_P = 0.2316419
INV_SQRT_2PI = 0.3989422804014327


def nn(a, b):
    return lax.dot_general(a, b, (((1,), (0,)), ((), ())), preferred_element_type=F32)


def nt(a, b):
    return lax.dot_general(a, b, (((1,), (1,)), ((), ())), preferred_element_type=F32)


def tn(a, b):
    return lax.dot_general(a, b, (((0,), (0,)), ((), ())), preferred_element_type=F32)


def exact(a, b):
    return lax.dot_general(
        a, b, (((1,), (0,)), ((), ())), precision=HIGH, preferred_element_type=F32
    )


def iota(shape, dim):
    return lax.broadcasted_iota(jnp.int32, shape, dim)


def log_sigmoid(x):
    return jnp.minimum(x, 0.0) - jnp.log(1.0 + jnp.exp(-jnp.abs(x)))


def normalize(x):
    centred = x - jnp.mean(x, axis=-1, keepdims=True)
    scale = lax.rsqrt(jnp.mean(centred * centred, axis=-1, keepdims=True) + EPS_NORM)
    return centred * scale, scale


def normalize_back(grad, gain, xhat, scale):
    inner = grad * gain
    mean_inner = jnp.mean(inner, axis=-1, keepdims=True)
    mean_both = jnp.mean(inner * xhat, axis=-1, keepdims=True)
    return scale * (inner - mean_inner - xhat * mean_both)


def fold_rows(x):
    return jnp.sum(x.reshape(x.shape[0] // 8, 8, x.shape[1]), axis=0)


def block_ones():
    return jnp.where(
        iota((LANES, LANES), 0) // 64 == iota((LANES, LANES), 1) // 64, 1.0, 0.0
    ).astype(BF16)


def head_sums(x):
    high = x.astype(BF16)
    rest = (x - high.astype(F32)).astype(BF16)
    ones = block_ones()
    return nn(jnp.concatenate([high, rest], axis=1), jnp.concatenate([ones, ones], axis=0))


def lower_half(shape):
    return iota(shape, 1) < 64


def mine(h, lower):
    return lower if h % 2 == 0 else jnp.logical_not(lower)


def column(block, index, rows, width):
    return jnp.broadcast_to(block[:, index : index + 1], (rows, width))


def sin_cos(turns, scale):
    r = turns - jnp.floor(turns + 0.5)
    r2 = r * r
    s = (((SIN[3] * r2 + SIN[2]) * r2 + SIN[1]) * r2 + SIN[0]) * r
    k = 2.0 * scale
    c = (((k * COS[4] * r2 + k * COS[3]) * r2 + k * COS[2]) * r2 + k * COS[1]) * r2 + k * COS[0]
    return s * c, scale - (k * s) * s


def grow_state(payload, h):
    state = payload[h, 0:64, :]
    norm = jnp.broadcast_to(payload[h, 64:65, :].astype(F32), (64, state.shape[1]))
    state = state.astype(F32)
    return jnp.concatenate([state, norm] if h % 2 == 0 else [norm, state], axis=0)


def shrink_state(state, h):
    if h % 2 == 0:
        return state[0:PAY].astype(BF16)
    return jnp.concatenate([state[64:128], state[0 : PAY - 64]], axis=0).astype(BF16)


def features_kernel(
    heads,
    x_ref,
    gain_ref,
    bias_ref,
    wq_ref,
    wk_ref,
    wv_ref,
    wg_ref,
    wgt_ref,
    gb_ref,
    gbt_ref,
    pcat_ref,
    start_ref,
    ml_ref,
    uq_ref,
    uk_ref,
    rq_ref,
    rk_ref,
    qf_ref,
    kf_ref,
    v_ref,
    gcol_ref,
    grow_ref,
    before_ref,
    final_ref,
    total_ref,
    state,
    carry,
):
    step = pl.program_id(0)

    @pl.when(step == 0)
    def _():
        state[...] = start_ref[...]
        carry[...] = jnp.zeros_like(carry)

    xhat, _ = normalize(x_ref[...].astype(F32))
    ml = (xhat * gain_ref[...] + bias_ref[...]).astype(BF16)
    ml_ref[...] = ml
    q = nn(ml, wq_ref[...])
    k = nn(ml, wk_ref[...])
    v = nn(ml, wv_ref[...])
    v_ref[...] = v.astype(BF16)
    logit = nn(ml, wg_ref[...]) + gb_ref[...]
    keep = log_sigmoid(logit)
    gain_in = keep - logit
    tri = jnp.where(iota((C, C), 0) >= iota((C, C), 1), 1.0, 0.0)
    decay = exact(tri, keep)
    total = decay[C - 1 : C, :]
    group = iota((C, LANES), 1) // 8
    everywhere = carry[...] + decay
    coef = total - decay + gain_in
    packed = jnp.where(group == 0, decay, coef)
    packed = jnp.where(group == 2, everywhere, packed)
    packed = jnp.where(group == 3, jax.nn.sigmoid(logit), packed)
    packed = jnp.where(group == 4, gain_in - decay, packed)
    packed = jnp.where(group == 5, jax.nn.sigmoid(-logit), packed)
    packed = jnp.where(group == 6, jnp.broadcast_to(carry[...], (C, LANES)), packed)
    packed = jnp.where(group == 7, jnp.broadcast_to(total, (C, LANES)), packed)
    gcol_ref[...] = packed
    carry[...] = carry[...] + total
    total_ref[...] = jnp.broadcast_to(carry[...], total_ref.shape)
    logit_row = nt(wgt_ref[...], ml) + gbt_ref[...][:, 0:1]
    keep_row = log_sigmoid(logit_row)
    upper = jnp.where(iota((C, C), 0) <= iota((C, C), 1), 1.0, 0.0)
    decay_row = exact(keep_row, upper)
    grow_ref[...] = jnp.concatenate([keep_row - logit_row - decay_row, decay_row], axis=0)

    lower = lower_half((C, LANES))
    ftr_scale = 1.0 / math.sqrt(LANES)
    for p in range(heads // 2):
        lanes = slice(LANES * p, LANES * (p + 1))
        both = jnp.concatenate([q[:, lanes], k[:, lanes]], axis=0)
        scale = lax.rsqrt(head_sums(both * both) + EPS_UNIT)
        unit = both * scale
        high = unit.astype(BF16)
        rest = (unit - high.astype(F32)).astype(BF16)
        uq_ref[:, lanes] = high[:C]
        uk_ref[:, lanes] = high[C:]
        rq_ref[:, lanes] = scale[:C]
        rk_ref[:, lanes] = scale[C:]
        turns = nn(jnp.concatenate([high, rest, high], axis=1), pcat_ref[p])
        s, c = sin_cos(turns, ftr_scale)
        s = s.astype(BF16)
        c = c.astype(BF16)
        for j in range(2):
            h = 2 * p + j
            half = slice(LANES * j, LANES * (j + 1))
            feats = jnp.concatenate([s[:, half], c[:, half]], axis=1)
            qf_ref[:, 256 * h : 256 * (h + 1)] = feats[:C]
            kf = feats[C:]
            kf_ref[:, 256 * h : 256 * (h + 1)] = kf
            values = jnp.where(mine(h, lower), v[:, lanes], 1.0)
            weighted = (values * jnp.exp(column(coef, h, C, LANES))).astype(BF16)
            now = state[h]
            before_ref[0, h] = now.astype(BF16)
            state[h] = jnp.exp(total[:, h : h + 1]) * now + tn(weighted, kf)

    @pl.when(step == pl.num_programs(0) - 1)
    def _():
        for h in range(heads):
            final_ref[h] = shrink_state(state[h], h)


def inner_kernel(heads, qf_ref, kf_ref, v_ref, gcol_ref, grow_ref, before_ref, n_ref):
    causal = iota((C, C), 0) >= iota((C, C), 1)
    lower = lower_half((C, LANES))
    gcol = gcol_ref[...]
    for h in range(heads):
        qf = qf_ref[:, 256 * h : 256 * (h + 1)]
        kf = kf_ref[:, 256 * h : 256 * (h + 1)]
        p = h // 2
        v = v_ref[:, LANES * p : LANES * (p + 1)].astype(F32)
        values = jnp.where(mine(h, lower), v, 1.0).astype(BF16)
        decay = column(gcol, h, C, LANES)
        pairs = jnp.where(causal, jnp.exp(decay + grow_ref[h : h + 1, :]), 0.0)
        weights = (nt(qf, kf) * pairs).astype(BF16)
        n_ref[:, LANES * h : LANES * (h + 1)] = nn(weights, values) + jnp.exp(decay) * nt(
            qf, before_ref[0, h]
        )


def feed_kernel(
    heads,
    shards,
    x_ref,
    dout_ref,
    qf_ref,
    n_ref,
    gcol_ref,
    entry_ref,
    wo_ref,
    gain_ref,
    bias_ref,
    up_ref,
    upb_ref,
    down_ref,
    downb_ref,
    out_ref,
    mg_ref,
    fl_ref,
    hl_ref,
    pre_ref,
    mix_ref,
    br_ref,
    a_ref,
    final_ref,
    sums_ref,
    upbg_ref,
    adj,
    entry,
):
    step = pl.program_id(0)
    rows = x_ref.shape[0]

    @pl.when(step == 0)
    def _():
        adj[...] = jnp.zeros_like(adj)
        sums_ref[...] = jnp.zeros_like(sums_ref)
        upbg_ref[...] = jnp.zeros_like(upbg_ref)
        for h in range(heads):
            entry[h] = grow_state(entry_ref, h).astype(BF16)

    lower = lower_half((rows, LANES))
    gcol = gcol_ref[...]
    parts = []
    for p in range(heads // 2):
        both = []
        for h in (2 * p, 2 * p + 1):
            far = nt(qf_ref[:, 256 * h : 256 * (h + 1)], entry[h])
            far = far * jnp.exp(column(gcol, 16 + h, rows, LANES))
            both.append(n_ref[:, LANES * h : LANES * (h + 1)] + far)
        num = jnp.where(lower, both[0], both[1])
        den = pltpu.roll(jnp.where(lower, both[1], both[0]), 64, 1)
        inv = lax.rsqrt(den * den + GUARD)
        parts.append((num, den, inv))
    mixed = jnp.concatenate([num * inv for num, den, inv in parts], axis=1).astype(BF16)
    mix_ref[...] = mixed
    middle = x_ref[...].astype(F32) + nn(mixed, wo_ref[...])
    xhat, scale = normalize(middle)
    gain = gain_ref[...]
    feed_low = (xhat * gain + bias_ref[...]).astype(BF16)
    fl_ref[...] = feed_low
    dout_low = dout_ref[...]
    dout = dout_low.astype(F32)
    out = middle + downb_ref[...]
    feed_grad = jnp.zeros_like(middle)
    width = up_ref.shape[2]
    block = min(HB, width)
    for s in range(shards):
        for b in range(width // block):
            cols = slice(block * b, block * (b + 1))
            place = slice(width * s + block * b, width * s + block * (b + 1))
            up = up_ref[s, :, cols]
            down = down_ref[s, :, cols]
            pre = nn(feed_low, up) + upb_ref[:, place]
            t = 1.0 / (1.0 + ERF_P * jnp.abs(pre))
            bell = INV_SQRT_2PI * jnp.exp(-0.5 * pre * pre)
            tail = ((((ERF[4] * t + ERF[3]) * t + ERF[2]) * t + ERF[1]) * t + ERF[0]) * t * bell
            phi = jnp.where(pre >= 0.0, 1.0 - tail, tail)
            hidden = (pre * phi).astype(BF16)
            hl_ref[:, place] = hidden
            out = out + nt(hidden, down)
            pre_grad = nn(dout_low, down) * (phi + pre * bell)
            pre_low = pre_grad.astype(BF16)
            pre_ref[:, place] = pre_low
            upbg_ref[:, place] += fold_rows(pre_low.astype(F32))
            feed_grad = feed_grad + nt(pre_low, up)
    out_ref[...] = out.astype(BF16)
    sums_ref[0:8, :] += fold_rows(feed_grad * xhat)
    sums_ref[8:16, :] += fold_rows(feed_grad)
    sums_ref[16:24, :] += fold_rows(dout)
    middle_grad = dout + normalize_back(feed_grad, gain, xhat, scale)
    mg_ref[...] = middle_grad
    branch = middle_grad.astype(BF16)
    br_ref[...] = branch
    mixed_grad = nt(branch, wo_ref[...])
    for p in range(heads // 2):
        num, den, inv = parts[p]
        mg = mixed_grad[:, LANES * p : LANES * (p + 1)]
        a = mg * inv
        b = head_sums(mg * num) * den * (inv * inv * inv) * (-1.0 / 64)
        b = pltpu.roll(b, 64, 1)
        for h in (2 * p, 2 * p + 1):
            a_low = jnp.where(mine(h, lower), a, b)
            a_ref[:, LANES * h : LANES * (h + 1)] = a_low.astype(BF16)
            lifted = (a_low * jnp.exp(column(gcol, 16 + h, rows, LANES))).astype(BF16)
            adj[h] += tn(lifted, qf_ref[:, 256 * h : 256 * (h + 1)])

    @pl.when(step == pl.num_programs(0) - 1)
    def _():
        for h in range(heads):
            final_ref[h] = shrink_state(adj[h], h)


def back_kernel(
    heads,
    x_ref,
    mg_ref,
    ml_ref,
    uq_ref,
    uk_ref,
    rq_ref,
    rk_ref,
    qf_ref,
    kf_ref,
    v_ref,
    a_ref,
    gcol_ref,
    grow_ref,
    before_ref,
    entry_ref,
    after_ref,
    gain_ref,
    wq_ref,
    wk_ref,
    wv_ref,
    wgt_ref,
    pcat_ref,
    dx_ref,
    dwq_ref,
    dwk_ref,
    dwv_ref,
    dwg_ref,
    adj_ref,
    sums_ref,
):
    step = pl.program_id(0)

    @pl.when(step == 0)
    def _():
        for h in range(heads):
            adj_ref[h] = grow_state(after_ref, h)
        for ref in (dwq_ref, dwk_ref, dwv_ref, dwg_ref, sums_ref):
            ref[...] = jnp.zeros_like(ref)

    row = iota((C, C), 0)
    col = iota((C, C), 1)
    causal = row >= col
    strict = row > col
    from_here = jnp.where(row <= col, 1.0, 0.0).astype(BF16)
    until_here = jnp.where(strict, 1.0, 0.0).astype(BF16)
    both_sums = jnp.concatenate([from_here, until_here], axis=1)
    lower = lower_half((C, LANES))
    gcol = gcol_ref[...]
    grads = {"q": [], "k": [], "v": []}
    logit_parts = []
    for p in range(heads // 2):
        lanes = slice(LANES * p, LANES * (p + 1))
        angle_q, angle_k, dvs = [], [], []
        v_pair = v_ref[:, lanes].astype(F32)
        for h in (2 * p, 2 * p + 1):
            qf = qf_ref[:, 256 * h : 256 * (h + 1)]
            kf = kf_ref[:, 256 * h : 256 * (h + 1)]
            values = jnp.where(mine(h, lower), v_pair, 1.0)
            values_low = values.astype(BF16)
            a_low = a_ref[:, LANES * h : LANES * (h + 1)]
            a = a_low.astype(F32)
            decay = column(gcol, h, C, LANES)
            lift = jnp.exp(decay)
            coef = jnp.exp(column(gcol, 8 + h, C, LANES))
            carried = jnp.exp(gcol[0:1, 48 + h : 49 + h])
            total = jnp.exp(gcol[0:1, 56 + h : 57 + h])
            entry = grow_state(entry_ref, h)
            before = before_ref[0, h].astype(F32) + carried * entry
            before_low = before.astype(BF16)
            adj = adj_ref[h]
            adj_low = adj.astype(BF16)
            pairs = jnp.where(causal, jnp.exp(decay + grow_ref[h : h + 1, :]), 0.0)
            raw = nt(qf, kf)
            weights = (raw * pairs).astype(BF16)
            dweights = nt(a_low, values_low).astype(BF16).astype(F32)
            draw = dweights * pairs
            draw_low = draw.astype(BF16)
            both = (raw * draw).astype(BF16)
            a_lift = (a * lift).astype(BF16)
            v_coef = (values * coef).astype(BF16)
            dq = nn(
                jnp.concatenate([draw_low, a_lift], axis=1),
                jnp.concatenate([kf, before_low], axis=0),
            )
            dk = tn(draw_low, qf) + nn(v_coef, adj_low)
            dv_far = coef * nt(kf, adj_low)
            dv = tn(weights, a_low) + dv_far
            n_far = lift * nt(qf, before_low)
            near = jnp.concatenate([a * n_far, values * dv_far], axis=0).astype(BF16)
            through = jnp.sum(total * adj * before, axis=0, keepdims=True)
            through = through[:, :LANES] + through[:, LANES:]
            flow = nn(both_sums, near) + jnp.where(strict, nn(from_here, both), 0.0) + through
            stay = column(gcol, 24 + h, C, LANES)
            leave = column(gcol, 40 + h, C, LANES)
            logit_parts.append((leave * flow - stay * (values * dv)).astype(BF16))
            adj_ref[h] = total * adj + tn(a_lift, qf)
            for feats, grad, angle in ((qf, dq, angle_q), (kf, dk, angle_k)):
                f = feats.astype(F32)
                angle.append(grad[:, :LANES] * f[:, LANES:] - grad[:, LANES:] * f[:, :LANES])
            dvs.append(dv)
        proj = pcat_ref[p, 0:LANES, :]
        for name, angle, u_ref, r_ref in (
            ("q", angle_q, uq_ref, rq_ref),
            ("k", angle_k, uk_ref, rk_ref),
        ):
            du = nt(jnp.concatenate(angle, axis=1).astype(BF16), proj)
            u = u_ref[:, lanes].astype(F32)
            along = nn((u * du).astype(BF16), block_ones())
            grads[name].append((2.0 * math.pi) * r_ref[:, lanes] * (du - u * along))
        grads["v"].append(jnp.where(lower, dvs[0], dvs[1]))
    dq, dk, dv = (jnp.concatenate(grads[name], axis=1).astype(BF16) for name in "qkv")
    select = jnp.where(
        iota((LANES * heads, LANES), 0) // LANES == iota((LANES * heads, LANES), 1), 1.0, 0.0
    ).astype(BF16)
    dlogit = nn(jnp.concatenate(logit_parts, axis=1), select).astype(BF16)
    ml = ml_ref[...]
    dwq_ref[...] += tn(ml, dq)
    dwk_ref[...] += tn(ml, dk)
    dwv_ref[...] += tn(ml, dv)
    dwg_ref[...] += tn(ml, dlogit)
    mixer_grad = (
        nt(dq, wq_ref[...])
        + nt(dk, wk_ref[...])
        + nt(dv, wv_ref[...])
        + nn(dlogit, wgt_ref[...])
    )
    xhat, scale = normalize(x_ref[...].astype(F32))
    sums_ref[0:8, :] += fold_rows(mixer_grad * xhat)
    sums_ref[8:16, :] += fold_rows(mixer_grad)
    sums_ref[16:24, 0:LANES] += fold_rows(dlogit.astype(F32))
    dx_ref[...] = mg_ref[...] + normalize_back(mixer_grad, gain_ref[...], xhat, scale)


def whole(shape):
    zeros = (0,) * len(shape)
    return pl.BlockSpec(shape, lambda i: zeros)


def call(kernel, steps, ins, outs, scratch, name):
    in_specs = [
        whole(array.shape) if block is None else pl.BlockSpec(block, index)
        for array, block, index in ins
    ]
    out_specs = [
        whole(shape) if block is None else pl.BlockSpec(block, index)
        for shape, dtype, block, index in outs
    ]
    return pl.pallas_call(
        kernel,
        grid=(steps,),
        in_specs=in_specs,
        out_specs=out_specs,
        out_shape=[jax.ShapeDtypeStruct(shape, dtype) for shape, dtype, _, _ in outs],
        scratch_shapes=scratch,
        compiler_params=pltpu.CompilerParams(
            dimension_semantics=("arbitrary",), vmem_limit_bytes=VMEM
        ),
        name=name,
    )(*[array for array, _, _ in ins])


def carry_over(payload, logs, forward):
    n, index = lax.axis_size("seq"), lax.axis_index("seq")
    if n == 2:
        return lax.ppermute(payload, "seq", [(0, 1)] if forward else [(1, 0)])
    everything = lax.all_gather(payload, "seq")
    every_log = lax.all_gather(logs, "seq")
    total = jnp.zeros(payload.shape, F32)
    for k in range(n) if forward else reversed(range(n)):
        ahead = (k < index) if forward else (k > index)
        new = jnp.exp(every_log[k])[:, None, None] * total + everything[k].astype(F32)
        total = jnp.where(ahead, new, total)
    return total.astype(BF16)


def local(
    inputs,
    cotangent,
    mixer_gain,
    mixer_bias,
    query_weight,
    key_weight,
    value_weight,
    gate_weight,
    gate_bias,
    output_weight,
    projections,
    start_state,
    start_norm,
    feed_gain,
    feed_bias,
    up_weight,
    up_bias,
    down_weight,
    down_bias,
):
    _, tokens, width = inputs.shape
    heads, size, feats = projections.shape
    chunks = tokens // C
    tile = min(T, tokens)
    tiles = tokens // tile
    shards = lax.axis_size("seq")
    first = lax.axis_index("seq") == 0
    x = inputs.reshape(tokens, width)
    dout = cotangent.reshape(tokens, width)

    every_up = lax.all_gather(up_weight, "seq")
    every_down = lax.all_gather(down_weight, "seq")
    every_upb = lax.all_gather(up_bias.astype(F32), "seq").reshape(1, -1)
    hidden = every_upb.shape[1]

    turns = projections * (1.0 / (2.0 * math.pi))
    high = lax.reduce_precision(turns, 8, 7)
    rest = turns - high
    zeros = jnp.zeros_like(turns)

    def pair_blocks(part):
        left = jnp.concatenate([part[0::2], zeros[0::2]], axis=2)
        right = jnp.concatenate([zeros[0::2], part[1::2]], axis=2)
        return jnp.concatenate([left, right], axis=1)

    pcat = jnp.concatenate(
        [pair_blocks(high), pair_blocks(high), pair_blocks(rest)], axis=1
    ).astype(BF16)
    wg = jnp.tile(gate_weight, (1, LANES // heads))
    wgt = gate_weight.T
    gb = jnp.tile(gate_bias, LANES // heads)[None]
    gbt = jnp.broadcast_to(gate_bias[:, None], (heads, LANES))
    start_rows = start_state.transpose(0, 2, 1)
    norm_rows = jnp.broadcast_to(start_norm[:, None, :], start_rows.shape)
    even = (jnp.arange(heads) % 2 == 0)[:, None, None]
    start = jnp.concatenate(
        [jnp.where(even, start_rows, norm_rows), jnp.where(even, norm_rows, start_rows)], axis=1
    )
    start = jnp.where(first, start, 0.0)

    def rows(n, block_rows=C):
        return (block_rows, n), lambda i: (i, 0)

    def out_rows(n, dtype, block_rows=C):
        return ((tokens, n), dtype) + rows(n, block_rows)

    def const(array):
        return (array if array.ndim > 1 else array[None], None, None)

    def keep(shape, dtype):
        return (shape, dtype, None, None)

    wide = heads * LANES
    wider = heads * 2 * feats
    ml, uq, uk, rq, rk, qf, kf, v, gcol, grow, before, final, total = call(
        partial(features_kernel, heads),
        chunks,
        [
            (x,) + rows(width),
            const(mixer_gain),
            const(mixer_bias),
            const(query_weight),
            const(key_weight),
            const(value_weight),
            const(wg),
            const(wgt),
            const(gb),
            const(gbt),
            const(pcat),
            const(start),
        ],
        [
            out_rows(width, BF16),
            out_rows(width, BF16),
            out_rows(width, BF16),
            out_rows(width, F32),
            out_rows(width, F32),
            out_rows(wider, BF16),
            out_rows(wider, BF16),
            out_rows(width, BF16),
            out_rows(LANES, F32),
            ((2 * heads, tokens), F32, (2 * heads, C), lambda i: (0, i)),
            (
                (chunks, heads, LANES, 2 * feats),
                BF16,
                (1, heads, LANES, 2 * feats),
                lambda i: (i, 0, 0, 0),
            ),
            keep((heads, PAY, 2 * feats), BF16),
            keep((8, LANES), F32),
        ],
        [pltpu.VMEM((heads, LANES, 2 * feats), F32), pltpu.VMEM((1, LANES), F32)],
        "features",
    )
    logs = total[0, :heads]
    entry = carry_over(final, logs, True)
    state_block = (1, heads, LANES, 2 * feats)
    (num,) = call(
        partial(inner_kernel, heads),
        chunks,
        [
            (qf,) + rows(wider),
            (kf,) + rows(wider),
            (v,) + rows(width),
            (gcol,) + rows(LANES),
            (grow, (2 * heads, C), lambda i: (0, i)),
            (before, state_block, lambda i: (i, 0, 0, 0)),
        ],
        [out_rows(wide, F32)],
        [],
        "inner",
    )
    out, mg, fl, hl, pre, mix, br, a, adj_final, feed_sums, upbg = call(
        partial(feed_kernel, heads, shards),
        tiles,
        [
            (x,) + rows(width, tile),
            (dout,) + rows(width, tile),
            (qf,) + rows(wider, tile),
            (num,) + rows(wide, tile),
            (gcol,) + rows(LANES, tile),
            const(entry),
            const(output_weight),
            const(feed_gain),
            const(feed_bias),
            const(every_up),
            const(every_upb),
            const(every_down),
            const(down_bias),
        ],
        [
            out_rows(width, BF16, tile),
            out_rows(width, F32, tile),
            out_rows(width, BF16, tile),
            out_rows(hidden, BF16, tile),
            out_rows(hidden, BF16, tile),
            out_rows(width, BF16, tile),
            out_rows(width, BF16, tile),
            out_rows(wide, BF16, tile),
            keep((heads, PAY, 2 * feats), BF16),
            keep((24, width), F32),
            keep((8, hidden), F32),
        ],
        [
            pltpu.VMEM((heads, LANES, 2 * feats), F32),
            pltpu.VMEM((heads, LANES, 2 * feats), BF16),
        ],
        "feed",
    )
    after = carry_over(adj_final, logs, False)
    down_grad = tn(dout, hl).astype(BF16)
    up_grad = tn(fl, pre).astype(BF16)
    output_grad = tn(mix, br).astype(BF16)

    def back_rows(n):
        return (C, n), lambda i: (chunks - 1 - i, 0)

    dx, dwq, dwk, dwv, dwg, adj, mixer_sums = call(
        partial(back_kernel, heads),
        chunks,
        [
            (x,) + back_rows(width),
            (mg,) + back_rows(width),
            (ml,) + back_rows(width),
            (uq,) + back_rows(width),
            (uk,) + back_rows(width),
            (rq,) + back_rows(width),
            (rk,) + back_rows(width),
            (qf,) + back_rows(wider),
            (kf,) + back_rows(wider),
            (v,) + back_rows(width),
            (a,) + back_rows(wide),
            (gcol,) + back_rows(LANES),
            (grow, (2 * heads, C), lambda i: (0, chunks - 1 - i)),
            (before, state_block, lambda i: (chunks - 1 - i, 0, 0, 0)),
            const(entry),
            const(after),
            const(mixer_gain),
            const(query_weight),
            const(key_weight),
            const(value_weight),
            const(jnp.pad(wgt, ((0, LANES - heads), (0, 0)))),
            const(pcat),
        ],
        [
            ((tokens, width), F32) + back_rows(width),
            keep((width, width), F32),
            keep((width, width), F32),
            keep((width, width), F32),
            keep((width, LANES), F32),
            keep((heads, LANES, 2 * feats), F32),
            keep((24, width), F32),
        ],
        [],
        "back",
    )
    adj = jnp.where(first, adj, 0.0)
    state_grad = jnp.where(even, adj[:, :64], adj[:, 64:])
    norm_grad = jnp.sum(jnp.where(even, adj[:, 64:], adj[:, :64]), axis=1)

    up_half = lax.psum_scatter(
        jnp.stack([up_grad, down_grad]), "seq", scatter_dimension=2, tiled=True
    )
    upb_half = lax.psum_scatter(jnp.sum(upbg, axis=0), "seq", scatter_dimension=0, tiled=True)
    sum_up_down, sum_upb = lax.psum((up_half, upb_half), "dp")
    sum_up, sum_down = (part.astype(F32) for part in sum_up_down)
    wide_sums = lax.psum(
        (
            dwq.astype(BF16),
            dwk.astype(BF16),
            dwv.astype(BF16),
            output_grad,
            state_grad.astype(BF16),
        ),
        ("dp", "seq"),
    )
    sum_q, sum_k, sum_v, sum_o, sum_state = (part.astype(F32) for part in wide_sums)
    feed_three = jnp.sum(feed_sums.reshape(3, 8, width), axis=1)
    mixer_three = jnp.sum(mixer_sums.reshape(3, 8, width), axis=1)
    sum_g, sum_norm, sum_feed, sum_mixer = lax.psum(
        (dwg[:, :heads], norm_grad, feed_three, mixer_three), ("dp", "seq")
    )
    return (
        out.reshape(inputs.shape),
        dx.reshape(inputs.shape),
        sum_mixer[0],
        sum_mixer[1],
        sum_q,
        sum_k,
        sum_v,
        sum_g,
        sum_mixer[2, :heads],
        sum_o,
        sum_state.transpose(0, 2, 1),
        sum_norm,
        sum_feed[0],
        sum_feed[1],
        sum_up,
        sum_upb,
        sum_down,
        sum_feed[2],
    )


def solution(mesh):
    tokens = P("dp", "seq", None)
    columns = P(None, "seq")
    return jax.shard_map(
        local,
        mesh=mesh,
        in_specs=(tokens, tokens) + (P(),) * 13 + (columns, P("seq"), columns, P()),
        out_specs=(tokens, tokens) + (P(),) * 12 + (columns, P("seq"), columns, P()),
        check_vma=False,
    )
```

time: 1160 us -> 438 us (0.38); the launches traced: 1150 us -> 437 us
  matrix products: 554 us -> 8.73 us
  local copies, waits for them, and re-layouts: 145 us -> 6.95 us
  Pallas kernels: 0 us -> 117 us
  other arithmetic: 119 us -> 21.4 us
  waiting for transfers between devices: 208 us -> 179 us
  blocking collectives: 105 us -> 82.1 us
    dot_general x48 -> x3, matrix products: 554 us -> 8.73 us  [tn(): lax.dot_general(a, b, (((0,), (0,)), ((), ())), preferred_element_type=F32)]
    pallas_call x0 -> x4, Pallas kernels: none -> 117 us  [call(): pl.pallas_call(kernel, grid=(steps,), in_specs=in_specs, out_specs=out_sp...]
    reduce_sum x18 -> x4, other arithmetic: 53.7 us -> 0.2 us  [the longest x1 0.13 us: local(): norm_grad = jnp.sum(jnp.where(even, adj[:, 64:], adj[:, :64]), axis=1)]
    unnamed x302 -> x60, local copies, waits for them, and re-layouts: 33.1 us -> 3.11 us
    all_gather x2, waiting for transfers between devices: 45.2 us -> 15.7 us  [the longest x1 15.7 us: local(): every_down = lax.all_gather(down_weight, 'seq')]
    reduce_scatter x2 -> x1, waiting for transfers between devices: 28.2 us -> 0.02 us  [local(): lax.psum_scatter(jnp.stack([up_grad, down_grad]), 'seq', scatter_dimensio...]
    dot_general x3 -> x0, local copies, waits for them, and re-layouts: 27.2 us -> none  [the longest x1 27.2 us: summarize(): jnp.einsum('rnh,rnhfd->rhfd', to_end, group_state, precision=HIGH)]
    all_gather x5 -> x1, blocking collectives: 31 us -> 4.67 us  [local(): every_upb = lax.all_gather(up_bias.astype(F32), 'seq').reshape(1, -1)]
  transfers between devices with their start and end apart: 6 -> 7, of which waited for: 5 -> 4; matrix products, arithmetic and copies ran while one was open for 34% -> 5% of each run, Pallas kernels for 0% -> 20%
where the time goes in v1:
time: 438 us; the launch traced here: 437 us
  waiting for transfers between devices  179 us (41%)
  Pallas kernels  117 us (27%)
  blocking collectives  82.1 us (19%)
  other arithmetic  21.4 us (5%)
  between operations  14.9 us (3%)
  matrix products  8.73 us (2%)
  local copies, waits for them, and re-layouts  6.95 us (2%)
  starting transfers between devices  6.56 us (1%)
    pallas_call x4, Pallas kernels, call(): pl.pallas_call(kernel, grid=(steps,), in_specs=in_specs, out_specs=out_sp...  117 us
    psum x1, waiting for transfers between devices, local(): sum_up_down, sum_upb = lax.psum((up_half, upb_half), 'dp')  92.6 us
    psum x1, waiting for transfers between devices, local(): lax.psum((dwq.astype(BF16), dwk.astype(BF16), dwv.astype(BF16), output_gr...  56.4 us
    psum x1, blocking collectives, local(): lax.psum((dwg[:, :heads], norm_grad, feed_three, mixer_three), ('dp', 'se...  42 us
    psum x1, blocking collectives, local(): sum_up_down, sum_upb = lax.psum((up_half, upb_half), 'dp')  30.5 us
    all_gather x1, waiting for transfers between devices, local(): every_down = lax.all_gather(down_weight, 'seq')  15.7 us
    ppermute x2, waiting for transfers between devices, carry_over(): return lax.ppermute(payload, 'seq', [(0, 1)] if forward else [(1, 0)])  12.8 us
  transfers between devices with their start and end apart: 7, of which 4 were waited for; matrix products, arithmetic and copies ran while one was open for 5% of the time, Pallas kernels for 20%

profile of v1, /device:TPU:0, one launch (start us, length us, event | category | flops | bytes accessed | tf_op | source)
XLA Modules:
  0.0 437.5 jit_solution(8622384076949037046)
XLA Ops:
  8.9 0.8 copy.43.wg_ref
  10.7 1.1 maximum_select_fusion.start_ref
  12.4 30.1 %features.1 = (bf16[1024,512]{1,0:T(8,128)(2,1)}, bf16[1024,512]{1,0:T(8,128)(2,1)}, bf16[1024,512]{1,0:T(8,128)(2,1)}, f32[1024,512]{1,0:T(8,128)}, f32[1024,51...) custom-call(bf16[1024,512]{1,0:T(8,128)(2,1)} %bitcast.57, ...), custom_call_target="tpu_custom_call" | custom-call | tf_op jit(solution)/shard_map/features/pallas_call | solution.py:507
  42.5 4.9 %collective-permute-start = (bf16[8,80,256]{2,1,0:T(8,128)(2,1)}, bf16[8,80,256]{2,1,0:T(8,128)(2,1)S(1)}, u32[]{:S(2)}, u32[]{:S(2)}) collective-permute-start(bf16[8,80,256]{2,1,0:T(8,128)(2,1)} %get-tuple-element.54), channel_id=1, source_target_pairs={{0,1},{2,3},{4,5},{6,7},{8,9},{10,11},{12,13},{14,15},{16,17},{18,... | collective-permute-start | bytes 983048 | tf_op jit(solution)/shard_map/ppermute | solution.py:524
  47.4 12.5 %inner.1.n_ref = f32[1024,1024]{1,0:T(8,128)} custom-call(bf16[1024,2048]{1,0:T(8,128)(2,1)} %get-tuple-element.48.qf_ref, bf16[1024,2048]{1,0:T(8,128)(2,1)} %get-tuple-element.49.kf_ref, bf16[1024,512]{1,0:T(8,128)(2,1)} %get-tuple-element.50.v_ref, f32[1024,128]{1,0:T(8,128)} %get-tuple-element.51.gcol_ref, f32[16,1024]{1,0:T(8,128)} %get-tuple-element.52.grow_ref, ...), custom_call_target="tpu_custom_call" | custom-call | tf_op jit(solution)/shard_map/inner/pallas_call | solution.py:507
  59.8 4.7 %all-gather.1 = f32[2048]{0:T(1024)} all-gather(f32[1024]{0:T(1024)S(1)} %all_gather.28), channel_id=3, replica_groups=mesh['dp'=16,'seq'=2] {'seq'}, dimensions={0}, use_global_device_ids=true | all-gather | bytes 12288 | tf_op jit(solution)/shard_map/all_gather | solution.py:568
  64.5 15.7 %all-gather.8.cloned.1.call-done = bf16[1024,1024]{1,0:T(8,128)(2,1)} async-done(((bf16[512,1024]{1,0:T(8,128)(2,1)}), bf16[1024,1024]{1,0:T(8,128)(2,1)}) %all-gather.8.cloned.1.call-update) | async-done | bytes 2097168 | tf_op jit(solution)/shard_map/all_gather | solution.py:567
  80.2 31.9 %feed.1 = (bf16[1024,512]{1,0:T(8,128)(2,1)}, f32[1024,512]{1,0:T(8,128)}, bf16[1024,512]{1,0:T(8,128)(2,1)}, bf16[1024,2048]{1,0:T(8,128)(2,1)}, bf16[1024,2048...) custom-call(bf16[1024,512]{1,0:T(8,128)(2,1)} %bitcast.58, ...), custom_call_target="tpu_custom_call" | custom-call | tf_op jit(solution)/shard_map/feed/pallas_call | solution.py:507
  112.2 4.8 %fusion.1 = bf16[1,512,2048]{2,1,0:T(8,128)(2,1)S(1)} fusion(bf16[1024,2048]{1,0:T(8,128)(2,1)} %get-tuple-element.76, bf16[1,1024,512]{2,1,0:T(8,128)(2,1)S(1)} %copy-done.2), kind=kOutput, calls=%fused_computation.4 | convolution fusion | flops 2148532224 | bytes 7340032 | tf_op jit(solution)/shard_map/dot_general | solution.py:41
  117.0 2.4 fusion
  119.4 2.3 pad_maximum_fusion
  121.8 0.9 copy-done.24
  122.7 1.5 collective-permute-start.1
  124.9 1.5 convolution_convert_fusion.2
  126.4 12.8 %collective-permute-done.1.after_ref = bf16[8,80,256]{2,1,0:T(8,128)(2,1)S(1)} collective-permute-done((bf16[8,80,256]{2,1,0:T(8,128)(2,1)S(1)}, bf16[8,80,256]{2,1,0:T(8,128)(2,1)S(1)}, u32[]{:S(2)}, u32[]{:S(2)}) %collective-permute-start.1) | collective-permute-done | bytes 327712 | tf_op jit(solution)/shard_map/ppermute | solution.py:524
  139.2 0.7 copy-done.9
  139.9 43.0 %back.1 = (f32[1024,512]{1,0:T(8,128)}, f32[512,512]{1,0:T(8,128)}, f32[512,512]{1,0:T(8,128)}, f32[512,512]{1,0:T(8,128)}, f32[512,128]{1,0:T(8,128)}, /*index=5*/f32[8,128,256]{2,1,0:T(8,128)}, f32[24,512]{1,0:T(8,128)}) custom-call(bf16[1024,512]{1,0:T(8,128)(2,1)} %bitcast.59, f32[1024,512]{1,0:T(8,128)} %get-tuple-element.56.mg_ref, ...), custom_call_target="tpu_custom_call" | custom-call | tf_op jit(solution)/shard_map/back/pallas_call | solution.py:507
  183.0 2.2 convert_element_type.53
  185.2 2.1 convert_element_type.55
  187.3 0.9 convert_element_type.57
  188.3 0.8 fusion.4
  191.0 5.0 %all-reduce.5 = f32[2048]{0:T(1024)S(1)} all-reduce(f32[2048]{0:T(1024)S(1)} %reduce_sum.39), channel_id=6, replica_groups=mesh['dp'=16,'seq'=2] {'seq'}, use_global_device_ids=true, to_apply=%region_15.16.clone | all-reduce | flops 2048 | bytes 16384
  196.1 30.5 %psum.87 = f32[1024]{0:T(1024)} all-reduce(f32[1024]{0:T(1024)S(1)} %dynamic-slice.1), channel_id=1, replica_groups=mesh['dp'=16,'seq'=2] {'dp'}, use_global_device_ids=true, to_apply=%region_16.17 | all-reduce | flops 1024 | bytes 8192 | tf_op jit(solution)/shard_map/psum | solution.py:760
  226.7 42.0 %all-reduce.6 = (f32[3,512]{1,0:T(4,128)S(1)}, f32[512,8]{1,0:T(8,128)S(1)}, f32[8,256]{1,0:T(8,128)}, f32[3,512]{1,0:T(4,128)S(1)}) all-reduce(f32[3,512]{1,0:T(4,128)S(1)} %bitcast_reduce_fusion.1, f32[512,8]{1,0:T(8,128)S(1)} %bitcast.63, f32[8,256]{1,0:T(8,128)S(1)} %select_reduce_fusion, ...), channel_id=1, replica_groups=mesh['dp'=16,'seq'=2] {'dp','seq'}, use_global_device_ids=true, to_apply=%region_1.2 | all-reduce | flops 9216 | bytes 73728 | tf_op jit(solution)/shard_map/psum | solution.py:775
  270.5 56.4 %all-reduce.13.cloned.1.call-done = (bf16[512,512]{1,0:T(8,128)(2,1)}, bf16[512,512]{1,0:T(8,128)(2,1)}, bf16[512,512]{1,0:T(8,128)(2,1)}, bf16[512,512]{1,0:T(8,128)(2,1)}, bf16[8,256,64]{1,2,0:T(8,128)(2,1)}) async-done(((bf16[512,512]{1,0:T(8,128)(2,1)}, bf16[512,512]{1,0:T(8,128)(2,1)}, bf16[512,512]{1,0:T(8,128)(2,1)}, bf16[512,512]{1,0:T(8,128)(2,1)}, bf16[8,256,64]{1,2,0:T(8,128)(2,1)}), ...) | async-done | bytes 2359312 | tf_op jit(solution)/shard_map/psum | solution.py:762
  326.9 2.2 convert_element_type.54
  329.1 2.2 convert_element_type.56
  331.3 1.1 convert_element_type.58
  332.4 1.1 convert_element_type.60
  333.5 0.8 transpose.31
  334.4 92.6 %all-reduce.11.cloned.1.call-done = bf16[2,512,1024]{2,1,0:T(8,128)(2,1)} async-done(((bf16[2,512,1024]{2,1,0:T(8,128)(2,1)}), bf16[2,512,1024]{2,1,0:T(8,128)(2,1)}) %all-reduce.11.cloned.1.call-update) | async-done | bytes 2097168 | tf_op jit(solution)/shard_map/psum | solution.py:760
  426.9 4.0 fusion.2
  (91 shorter events, 7.3 us)
Async XLA Ops:
  7.2 1.6 copy-start.5
  7.2 1.6 copy-start.12
  7.2 2.4 copy-start.19
  7.2 57.3 %all-gather.6.cloned.1.call-start = ((), (), s32[]{:S(2)}) async-start(), calls=%async_computation.3 | async-start | bytes 3145728 | tf_op jit(solution)/shard_map/all_gather | solution.py:566
  8.0 2.5 copy-start.8
  8.0 2.5 copy-start.17
  8.0 72.3 %all-gather.8.cloned.1.call-start = ((), (), s32[]{:S(2)}) async-start(), calls=%async_computation.4 | async-start | bytes 3145728 | tf_op jit(solution)/shard_map/all_gather | solution.py:567
  8.7 180.5 %reduce-scatter.2.cloned.1.call-start = ((), (), s32[]{:S(2)}) async-start(), calls=%async_computation.1 | async-start | bytes 6291456 | tf_op jit(solution)/shard_map/reduce_scatter | solution.py:756
  10.5 1.9 copy-start
  12.4 34.9 %copy-start.18 = (bf16[1024]{0:T(1024)(128)(2,1)S(1)}, bf16[1024]{0:T(1024)(128)(2,1)}, u32[]{:S(2)}) copy-start(bf16[1024]{0:T(1024)(128)(2,1)} %param.35) | copy-start | bytes 6148
  42.5 22.0 %collective-permute-start = (bf16[8,80,256]{2,1,0:T(8,128)(2,1)}, bf16[8,80,256]{2,1,0:T(8,128)(2,1)S(1)}, u32[]{:S(2)}, u32[]{:S(2)}) collective-permute-start(bf16[8,80,256]{2,1,0:T(8,128)(2,1)} %get-tuple-element.54), channel_id=1, source_target_pairs={{0,1},{2,3},{4,5},{6,7},{8,9},{10,11},{12,13},{14,15},{16,17},{18,... | collective-permute-start | bytes 983048 | tf_op jit(solution)/shard_map/ppermute | solution.py:524
  64.5 15.7 %copy-start.1 = (bf16[8,80,256]{2,1,0:T(8,128)(2,1)}, bf16[8,80,256]{2,1,0:T(8,128)(2,1)S(1)}, u32[]{:S(2)}) copy-start(bf16[8,80,256]{2,1,0:T(8,128)(2,1)S(1)} %collective-permute-done.entry_ref) | copy-start | bytes 983044
  80.2 31.9 %copy-start.2 = (bf16[1,1024,512]{2,1,0:T(8,128)(2,1)S(1)}, bf16[1,1024,512]{2,1,0:T(8,128)(2,1)}, u32[]{:S(2)}) copy-start(bf16[1,1024,512]{2,1,0:T(8,128)(2,1)} %param.20) | copy-start | bytes 3145732
  112.1 4.8 %copy-start.20 = (bf16[1024,2048]{1,0:T(8,128)(2,1)S(1)}, bf16[1024,2048]{1,0:T(8,128)(2,1)}, u32[]{:S(2)}) copy-start(bf16[1024,2048]{1,0:T(8,128)(2,1)} %get-tuple-element.75) | copy-start | bytes 12582916
  112.2 4.8 %copy-start.23 = (bf16[1024,512]{1,0:T(8,128)(2,1)S(1)}, bf16[1024,512]{1,0:T(8,128)(2,1)}, u32[]{:S(2)}) copy-start(bf16[1024,512]{1,0:T(8,128)(2,1)} %get-tuple-element.74) | copy-start | bytes 3145732
  121.7 1.0 copy-start.24
  121.7 2.5 copy-start.13
  121.7 3.1 copy-start.21
  121.7 3.1 copy-start.22
  121.7 205.2 %all-reduce.13.cloned.1.call-start = ((), (), s32[]{:S(2)}) async-start(), calls=%async_computation.5 | async-start | bytes 4718592 | tf_op jit(solution)/shard_map/psum | solution.py:762
  122.7 16.5 %collective-permute-start.1 = (bf16[8,80,256]{2,1,0:T(8,128)(2,1)S(1)}, bf16[8,80,256]{2,1,0:T(8,128)(2,1)S(1)}, u32[]{:S(2)}, u32[]{:S(2)}) collective-permute-start(bf16[8,80,256]{2,1,0:T(8,128)(2,1)S(1)} %copy-done.24), channel_id=1, source_target_pairs={{1,0},{3,2},{5,4},{7,6},{9,8},{11,10},{13,12},{15,14},{17,16},{19,... | collective-permute-start | bytes 983048 | tf_op jit(solution)/shard_map/ppermute | solution.py:524
  139.2 0.7 copy-start.9
  183.0 4.3 copy-start.4
  183.0 5.2 %copy-start.3 = (f32[8,128,256]{2,1,0:T(8,128)S(1)}, f32[8,128,256]{2,1,0:T(8,128)}, u32[]{:S(2)}) copy-start(f32[8,128,256]{2,1,0:T(8,128)} %get-tuple-element.72) | copy-start | bytes 3145732
  189.1 1.9 copy-start.14
  189.1 37.4 %copy-start.15 = (f32[24,512]{1,0:T(8,128)S(1)}, f32[24,512]{1,0:T(8,128)}, u32[]{:S(2)}) copy-start(f32[24,512]{1,0:T(8,128)} %get-tuple-element.73) | copy-start | bytes 147460
  189.1 37.4 %copy-start.16 = (f32[24,512]{1,0:T(8,128)S(1)}, f32[24,512]{1,0:T(8,128)}, u32[]{:S(2)}) copy-start(f32[24,512]{1,0:T(8,128)} %get-tuple-element.65) | copy-start | bytes 147460
  189.1 37.6 %copy-start.11 = (f32[512,128]{1,0:T(8,128)S(1)}, f32[512,128]{1,0:T(8,128)}, u32[]{:S(2)}) copy-start(f32[512,128]{1,0:T(8,128)} %get-tuple-element.69) | copy-start | bytes 786436
  189.2 237.8 %all-reduce.11.cloned.1.call-start = ((), (), s32[]{:S(2)}) async-start(), calls=%async_computation.2 | async-start | bytes 4194304 | tf_op jit(solution)/shard_map/psum | solution.py:760
  326.9 4.4 %copy-start.7 = (bf16[512,512]{1,0:T(8,128)(2,1)S(1)}, bf16[512,512]{1,0:T(8,128)(2,1)}, u32[]{:S(2)}) copy-start(bf16[512,512]{1,0:T(8,128)(2,1)} %get-tuple-element.138) | copy-start | bytes 1572868
  326.9 5.5 %copy-start.6 = (bf16[512,512]{1,0:T(8,128)(2,1)S(1)}, bf16[512,512]{1,0:T(8,128)(2,1)}, u32[]{:S(2)}) copy-start(bf16[512,512]{1,0:T(8,128)(2,1)} %get-tuple-element.139) | copy-start | bytes 1572868
  329.1 4.4 %copy-start.10 = (bf16[8,256,64]{1,2,0:T(8,128)(2,1)S(1)}, bf16[8,256,64]{1,2,0:T(8,128)(2,1)}, u32[]{:S(2)}) copy-start(bf16[8,256,64]{1,2,0:T(8,128)(2,1)} %get-tuple-element.140) | copy-start | bytes 786436
  (1 other events, 0.7 us)
Sparse Core Ops, SparseCore 0:
  9.6 35.8 all-gather.5
  47.0 33.1 all-gather.7
  121.9 58.4 reduce-scatter.1
  189.3 137.5 all-reduce.12
  330.3 96.5 all-reduce.10

commit v2 on v1

--- a/solution.py
+++ b/solution.py
@@ -13,6 +13,7 @@
 EPS_NORM = 1e-05
 EPS_UNIT = 1e-06
 GUARD = 0.0625
+MESH = pl.DeviceIdType.MESH
 HIGH = lax.Precision.HIGHEST
 VMEM = 56 * 1024 * 1024
 
@@ -753,48 +754,256 @@
     state_grad = jnp.where(even, adj[:, :64], adj[:, 64:])
     norm_grad = jnp.sum(jnp.where(even, adj[:, 64:], adj[:, :64]), axis=1)
 
-    up_half = lax.psum_scatter(
-        jnp.stack([up_grad, down_grad]), "seq", scatter_dimension=2, tiled=True
-    )
-    upb_half = lax.psum_scatter(jnp.sum(upbg, axis=0), "seq", scatter_dimension=0, tiled=True)
-    sum_up_down, sum_upb = lax.psum((up_half, upb_half), "dp")
-    sum_up, sum_down = (part.astype(F32) for part in sum_up_down)
-    wide_sums = lax.psum(
-        (
-            dwq.astype(BF16),
-            dwk.astype(BF16),
-            dwv.astype(BF16),
-            output_grad,
-            state_grad.astype(BF16),
-        ),
-        ("dp", "seq"),
-    )
-    sum_q, sum_k, sum_v, sum_o, sum_state = (part.astype(F32) for part in wide_sums)
     feed_three = jnp.sum(feed_sums.reshape(3, 8, width), axis=1)
     mixer_three = jnp.sum(mixer_sums.reshape(3, 8, width), axis=1)
-    sum_g, sum_norm, sum_feed, sum_mixer = lax.psum(
-        (dwg[:, :heads], norm_grad, feed_three, mixer_three), ("dp", "seq")
-    )
+    upb_grad = jnp.sum(upbg, axis=0)
+    weight_grads = (dwq.astype(BF16), dwk.astype(BF16), dwv.astype(BF16), output_grad)
+    small = (dwg[:, :heads].T, norm_grad, feed_three, mixer_three)
+    if (lax.axis_size("dp"), lax.axis_size("seq")) == (16, 2):
+        half = hidden // 2
+        up_down = jnp.concatenate(
+            [up_grad[:, :half], up_grad[:, half:], down_grad[:, :half], down_grad[:, half:]]
+        )
+        flat = jnp.concatenate([part.reshape(-1) for part in small + (upb_grad,)])
+        flat = jnp.pad(flat, (0, 256 * LANES - flat.shape[0])).reshape(256, LANES)
+        state_rows = state_grad.astype(BF16).reshape(heads * 64, 2 * feats)
+        sum_up_down, sum_q, sum_k, sum_v, sum_o, sum_state, flat = sum_devices(
+            (up_down,) + weight_grads + (state_rows, flat),
+            ("half", "all", "all", "all", "all", "all", "all"),
+            (4, 1, 1, 1, 1, 1, 1),
+        )
+        sum_up, sum_down = sum_up_down[:width], sum_up_down[width:]
+        flat = flat.reshape(-1)
+        sums, at = [], 0
+        for part in small + (upb_grad,):
+            sums.append(flat[at : at + part.size].reshape(part.shape))
+            at += part.size
+        sum_g, sum_norm, sum_feed, sum_mixer, sum_upb = sums
+        sum_upb = jnp.where(first, sum_upb[:half], sum_upb[half:])
+        sum_state = sum_state.reshape(heads, 64, 2 * feats)
+    else:
+        halves = lax.psum_scatter(
+            jnp.stack([up_grad, down_grad]), "seq", scatter_dimension=2, tiled=True
+        )
+        upb_half = lax.psum_scatter(upb_grad, "seq", scatter_dimension=0, tiled=True)
+        (sum_up, sum_down), sum_upb = lax.psum((halves, upb_half), "dp")
+        sum_q, sum_k, sum_v, sum_o, sum_state = lax.psum(
+            weight_grads + (state_grad.astype(BF16),), ("dp", "seq")
+        )
+        sum_g, sum_norm, sum_feed, sum_mixer = lax.psum(small, ("dp", "seq"))
     return (
         out.reshape(inputs.shape),
         dx.reshape(inputs.shape),
         sum_mixer[0],
         sum_mixer[1],
-        sum_q,
-        sum_k,
-        sum_v,
-        sum_g,
+        sum_q.astype(F32),
+        sum_k.astype(F32),
+        sum_v.astype(F32),
+        sum_g.T,
         sum_mixer[2, :heads],
-        sum_o,
-        sum_state.transpose(0, 2, 1),
+        sum_o.astype(F32),
+        sum_state.astype(F32).transpose(0, 2, 1),
         sum_norm,
         sum_feed[0],
         sum_feed[1],
-        sum_up,
+        sum_up.astype(F32),
         sum_upb,
-        sum_down,
+        sum_down.astype(F32),
         sum_feed[2],
     )
+
+
+class Links:
+    def __init__(self):
+        self.dp, self.seq = lax.axis_index("dp"), lax.axis_index("seq")
+        core, y, z = self.dp % 2, (self.dp // 2) % 2, self.dp // 4
+        self.y = y
+        self.at = {"core": core, "x": self.seq, "y": y, "z": z, "plane": self.seq * 2 + y}
+
+    size = {"core": 2, "x": 2, "y": 2, "z": 4, "plane": 4}
+
+    def partner(self, group, step):
+        dp, seq = self.dp, self.seq
+        if group == "core":
+            return (dp + 1 - 2 * self.at["core"], seq)
+        if group == "x":
+            return (dp, 1 - seq)
+        if group == "y":
+            return (dp + 2 - 4 * self.y, seq)
+        target = (self.at[group] + step) % 4
+        if group == "z":
+            return (dp % 4 + 4 * target, seq)
+        return (dp + 2 * (target % 2 - self.y), target // 2)
+
+    def greet(self, groups):
+        barrier = pltpu.get_barrier_semaphore()
+        count = 0
+        for group in groups:
+            for step in range(1, self.size[group]):
+                pl.semaphore_signal(
+                    barrier, inc=1, device_id=self.partner(group, step), device_id_type=MESH
+                )
+                count += 1
+        pl.semaphore_wait(barrier, count)
+
+
+class Plan:
+    def __init__(self, rows, lanes, dtype, scatter, gather):
+        self.scatter, self.gather, self.lanes, self.dtype = scatter, gather, lanes, dtype
+        self.rows = rows
+        self.stages = len(scatter) + len(gather)
+
+    def scratch(self):
+        shapes = []
+        rows = self.rows
+        for i, group in enumerate(self.scatter):
+            n = Links.size[group]
+            rows //= n
+            shapes.append(pltpu.VMEM((n - 1, rows, self.lanes), self.dtype))
+            if i < len(self.scatter) - 1:
+                shapes.append(pltpu.VMEM((rows, self.lanes), self.dtype))
+        for group in self.scatter + self.gather:
+            n = Links.size[group]
+            shapes.append(pltpu.SemaphoreType.DMA((n - 1,)))
+            shapes.append(pltpu.SemaphoreType.DMA((n - 1,)))
+        return shapes
+
+
+class Stream:
+    def __init__(self, plan, links, source, out, scratch):
+        self.plan, self.links, self.source, self.out = plan, links, source, out
+        scratch = list(scratch)
+        self.landing, self.parts = [], [source]
+        for i in range(len(plan.scatter)):
+            self.landing.append(scratch.pop(0))
+            if i < len(plan.scatter) - 1:
+                self.parts.append(scratch.pop(0))
+        self.sems = [(scratch.pop(0), scratch.pop(0)) for _ in range(plan.stages)]
+        self.places = {}
+        rows, start = out.shape[0], 0
+        for group in plan.scatter:
+            if group in plan.gather:
+                rows //= Links.size[group]
+                self.places[group] = (start, rows)
+                start = start + links.at[group] * rows
+        self.final = (start, rows)
+
+    def copies(self, stage, sending):
+        plan, links = self.plan, self.links
+        scattering = stage < len(plan.scatter)
+        group = (plan.scatter + plan.gather)[stage]
+        n, me = Links.size[group], links.at[group]
+        sends, recvs = self.sems[stage]
+        made = []
+        for step in range(1, n):
+            if scattering:
+                landing = self.landing[stage]
+                rows = landing.shape[1]
+                target = (me + step) % n
+                source = self.parts[stage].at[pl.ds(pl.multiple_of(target * rows, 8), rows)]
+                arrives = lands = landing.at[step - 1]
+            else:
+                start, rows = self.places[group]
+                mine_at = pl.multiple_of(start + me * rows, 8)
+                theirs_at = pl.multiple_of(start + ((me + n - step) % n) * rows, 8)
+                source = lands = self.out.at[pl.ds(mine_at, rows)]
+                arrives = self.out.at[pl.ds(theirs_at, rows)]
+            device = links.partner(group, step)
+
+            def copy(src, dst):
+                return pltpu.make_async_remote_copy(
+                    src_ref=src,
+                    dst_ref=dst,
+                    send_sem=sends.at[step - 1],
+                    recv_sem=recvs.at[step - 1],
+                    device_id=device,
+                    device_id_type=MESH,
+                )
+
+            made.append(copy(source, lands) if sending else copy(arrives, arrives))
+        return made
+
+    def start(self, stage):
+        for copy in self.copies(stage, True):
+            copy.start()
+
+    def finish(self, stage):
+        for copy in self.copies(stage, False):
+            copy.wait_recv()
+        if stage >= len(self.plan.scatter):
+            return
+        group = self.plan.scatter[stage]
+        landing = self.landing[stage]
+        arrivals, rows, _ = landing.shape
+        own = pl.multiple_of(self.links.at[group] * rows, 8)
+        total = self.parts[stage][pl.ds(own, rows), :].astype(F32)
+        for step in range(arrivals):
+            total = total + landing[step].astype(F32)
+        total = total.astype(landing.dtype)
+        if stage + 1 < len(self.plan.scatter):
+            self.parts[stage + 1][...] = total
+        else:
+            start, rows = self.final
+            self.out[pl.ds(pl.multiple_of(start, 8), rows), :] = total
+
+    def drain(self):
+        for stage in range(self.plan.stages):
+            for copy in self.copies(stage, True):
+                copy.wait_send()
+
+
+def run_streams(streams):
+    stages = max(stream.plan.stages for stream in streams)
+    for tick in range(stages + len(streams)):
+        for i, stream in enumerate(streams):
+            stage = tick - i
+            if 0 < stage <= stream.plan.stages:
+                stream.finish(stage - 1)
+            if 0 <= stage < stream.plan.stages:
+                stream.start(stage)
+    for stream in streams:
+        stream.drain()
+
+
+UP_PLAN = (("core", "x", "y", "z"), ("z", "y", "core"))
+ALL_PLAN = (("core", "plane", "z"), ("z", "plane", "core"))
+
+
+def sum_kernel(plans, splits, n_in, *refs):
+    sources, outs, scratch = refs[:n_in], refs[n_in : 2 * n_in], list(refs[2 * n_in :])
+    links = Links()
+    links.greet(("core", "plane", "z"))
+    streams = []
+    for source, out, plan, split in zip(sources, outs, plans, splits):
+        for part in range(split):
+            own = [scratch.pop(0) for _ in plan.scratch()]
+            lanes = pl.ds(part * plan.lanes, plan.lanes)
+            streams.append(Stream(plan, links, source.at[:, lanes], out.at[:, lanes], own))
+    run_streams(streams)
+
+
+def sum_devices(arrays, kinds, splits):
+    plans, shapes, scratch = [], [], []
+    for array, kind, split in zip(arrays, kinds, splits):
+        rows, lanes = array.shape
+        scatter, gather = UP_PLAN if kind == "half" else ALL_PLAN
+        plan = Plan(rows, lanes // split, array.dtype, scatter, gather)
+        plans.append(plan)
+        for _ in range(split):
+            scratch.extend(plan.scratch())
+        out_rows = rows // 2 if kind == "half" else rows
+        shapes.append(jax.ShapeDtypeStruct((out_rows, lanes), array.dtype))
+    return pl.pallas_call(
+        partial(sum_kernel, plans, splits, len(arrays)),
+        in_specs=[pl.BlockSpec(memory_space=pltpu.VMEM)] * len(arrays),
+        out_specs=[pl.BlockSpec(memory_space=pltpu.VMEM)] * len(arrays),
+        out_shape=shapes,
+        scratch_shapes=scratch,
+        compiler_params=pltpu.CompilerParams(
+            collective_id=1, has_side_effects=True, vmem_limit_bytes=VMEM
+        ),
+        name="sums",
+    )(*arrays)
 
 
 def solution(mesh):

time: 438 us -> 293 us (0.67)
  waiting for transfers between devices: 179 us -> 13.4 us
  Pallas kernels: 117 us -> 210 us
  blocking collectives: 82.1 us -> 4.49 us
  local copies, waits for them, and re-layouts: 6.95 us -> 13.6 us
    psum x2 -> x0, waiting for transfers between devices: 149 us -> none  [the longest x1 92.6 us: local(): sum_up_down, sum_upb = lax.psum((up_half, upb_half), 'dp')]
    pallas_call x0 -> x1, Pallas kernels: none -> 92.6 us  [sum_devices(): pl.pallas_call(partial(sum_kernel, plans, splits, len(arrays)), in_specs=...]
    psum x2 -> x0, blocking collectives: 72.4 us -> none  [the longest x1 42 us: local(): lax.psum((dwg[:, :heads], norm_grad, feed_three, mixer_three), ('dp', 'se...]
    ppermute x2, waiting for transfers between devices: 12.8 us -> 0.01 us  [carry_over(): return lax.ppermute(payload, 'seq', [(0, 1)] if forward else [(1, 0)])]
    unnamed x1 -> x0, blocking collectives: 5.01 us -> none
    convert_element_type x5 -> x6, other arithmetic: 10.6 us -> 9.35 us  [the longest x1 4.1 us: local(): sum_down.astype(F32)]
  transfers between devices with their start and end apart: 7 -> 4, of which waited for: 4 -> 1; matrix products, arithmetic and copies ran while one was open for 5% -> 7% of each run, Pallas kernels for 20% -> 15%
where the time goes in v2:
time: 293 us
  Pallas kernels  210 us (72%)
  other arithmetic  21.2 us (7%)
  between operations  14.5 us (5%)
  local copies, waits for them, and re-layouts  13.6 us (5%)
  waiting for transfers between devices  13.4 us (5%)
  matrix products  9 us (3%)
  starting transfers between devices  6.65 us (2%)
  blocking collectives  4.49 us (2%)
    pallas_call x4, Pallas kernels, call(): pl.pallas_call(kernel, grid=(steps,), in_specs=in_specs, out_specs=out_sp...  117 us
    pallas_call x1, Pallas kernels, sum_devices(): pl.pallas_call(partial(sum_kernel, plans, splits, len(arrays)), in_specs=...  92.6 us
    all_gather x1, waiting for transfers between devices, local(): every_down = lax.all_gather(down_weight, 'seq')  12 us
    dot_general x3, matrix products, tn(): lax.dot_general(a, b, (((0,), (0,)), ((), ())), preferred_element_type=F32)  9 us
    ppermute x2, starting transfers between devices, carry_over(): return lax.ppermute(payload, 'seq', [(0, 1)] if forward else [(1, 0)])  6.57 us
  transfers between devices with their start and end apart: 4, of which 1 were waited for; matrix products, arithmetic and copies ran while one was open for 7% of the time, Pallas kernels for 15%

profile of v2, /device:TPU:0, one launch (start us, length us, event | category | flops | bytes accessed | tf_op | source)
XLA Modules:
  0.0 292.6 jit_solution(9197579291287147082)
XLA Ops:
  8.7 1.0 multiply_reduce-precision_fusion
  12.5 1.0 subtract_convert_fusion
  13.8 1.1 maximum_select_fusion.start_ref
  15.6 30.1 %features.1 = (bf16[1024,512]{1,0:T(8,128)(2,1)}, bf16[1024,512]{1,0:T(8,128)(2,1)}, bf16[1024,512]{1,0:T(8,128)(2,1)}, f32[1024,512]{1,0:T(8,128)}, f32[1024,51...) custom-call(bf16[1024,512]{1,0:T(8,128)(2,1)} %bitcast.60, ...), custom_call_target="tpu_custom_call" | custom-call | tf_op jit(solution)/shard_map/features/pallas_call | solution.py:508
  45.6 5.1 %collective-permute-start = (bf16[8,80,256]{2,1,0:T(8,128)(2,1)}, bf16[8,80,256]{2,1,0:T(8,128)(2,1)S(1)}, u32[]{:S(2)}, u32[]{:S(2)}) collective-permute-start(bf16[8,80,256]{2,1,0:T(8,128)(2,1)} %get-tuple-element.61), channel_id=1, source_target_pairs={{0,1},{2,3},{4,5},{6,7},{8,9},{10,11},{12,13},{14,15},{16,17},{18,... | collective-permute-start | bytes 983048 | tf_op jit(solution)/shard_map/ppermute | solution.py:525
  51.5 12.5 %inner.1.n_ref = f32[1024,1024]{1,0:T(8,128)} custom-call(bf16[1024,2048]{1,0:T(8,128)(2,1)} %get-tuple-element.55.qf_ref, bf16[1024,2048]{1,0:T(8,128)(2,1)} %get-tuple-element.56.kf_ref, bf16[1024,512]{1,0:T(8,128)(2,1)} %get-tuple-element.57.v_ref, f32[1024,128]{1,0:T(8,128)} %get-tuple-element.58.gcol_ref, f32[16,1024]{1,0:T(8,128)} %get-tuple-element.59.grow_ref, ...), custom_call_target="tpu_custom_call" | custom-call | tf_op jit(solution)/shard_map/inner/pallas_call | solution.py:508
  63.9 4.5 %all-gather.1 = f32[2048]{0:T(1024)} all-gather(f32[1024]{0:T(1024)S(1)} %all_gather.28), channel_id=3, replica_groups=mesh['dp'=16,'seq'=2] {'seq'}, dimensions={0}, use_global_device_ids=true | all-gather | bytes 12288 | tf_op jit(solution)/shard_map/all_gather | solution.py:569
  68.4 12.0 %all-gather.8.cloned.1.call-done = bf16[1024,1024]{1,0:T(8,128)(2,1)} async-done(((bf16[512,1024]{1,0:T(8,128)(2,1)}), bf16[1024,1024]{1,0:T(8,128)(2,1)}) %all-gather.8.cloned.1.call-update) | async-done | bytes 2097168 | tf_op jit(solution)/shard_map/all_gather | solution.py:568
  80.5 31.8 %feed.1 = (bf16[1024,512]{1,0:T(8,128)(2,1)}, f32[1024,512]{1,0:T(8,128)}, bf16[1024,512]{1,0:T(8,128)(2,1)}, bf16[1024,2048]{1,0:T(8,128)(2,1)}, bf16[1024,2048...) custom-call(bf16[1024,512]{1,0:T(8,128)(2,1)} %bitcast.61, ...), custom_call_target="tpu_custom_call" | custom-call | tf_op jit(solution)/shard_map/feed/pallas_call | solution.py:508
  112.3 1.5 collective-permute-start.1
  113.8 5.0 %convolution_convert_fusion.1 = bf16[512,2048]{1,0:T(8,128)(2,1)S(1)} fusion(bf16[1024,512]{1,0:T(8,128)(2,1)} %get-tuple-element.72, bf16[1024,2048]{1,0:T(8,128)(2,1)} %get-tuple-element.73), kind=kOutput, calls=%fused_computation.2 | convolution fusion | flops 2148532224 | bytes 7340032 | tf_op jit(solution)/shard_map/dot_general | solution.py:42
  119.0 1.0 copy-done.2
  120.0 2.4 fusion
  122.7 2.3 pad_maximum_fusion.refs_0_
  125.2 1.5 convolution_convert_fusion.2.refs_4_
  127.5 42.8 %back.1 = (f32[1024,512]{1,0:T(8,128)}, f32[512,512]{1,0:T(8,128)}, f32[512,512]{1,0:T(8,128)}, f32[512,512]{1,0:T(8,128)}, f32[512,128]{1,0:T(8,128)}, /*index=5*/f32[8,128,256]{2,1,0:T(8,128)}, f32[24,512]{1,0:T(8,128)}) custom-call(bf16[1024,512]{1,0:T(8,128)(2,1)} %bitcast.62, f32[1024,512]{1,0:T(8,128)} %get-tuple-element.63.mg_ref, ...), custom_call_target="tpu_custom_call" | custom-call | tf_op jit(solution)/shard_map/back/pallas_call | solution.py:508
  170.3 1.5 broadcast_select_fusion
  171.9 0.8 select_convert_fusion
  172.7 1.0 slice_bitcast_fusion
  174.6 0.9 convert_element_type.55.refs_1_
  175.4 0.9 convert_element_type.56.refs_2_
  176.3 0.9 convert_element_type.57.refs_3_
  177.2 92.6 %sums.1 = (bf16[1024,1024]{1,0:T(8,128)(2,1)}, bf16[512,512]{1,0:T(8,128)(2,1)}, bf16[512,512]{1,0:T(8,128)(2,1)}, bf16[512,512]{1,0:T(8,128)(2,1)}, bf16[512,51...) custom-call(bf16[2048,1024]{1,0:T(8,128)(2,1)} %pad_maximum_fusion.refs_0_, ...), custom_call_target="tpu_custom_call" | custom-call | tf_op jit(solution)/shard_map/sums/pallas_call | solution.py:996
  269.8 0.8 slice.112
  272.0 1.4 slice_bitcast_fusion.1
  273.4 1.3 select_bitcast_fusion.2
  274.7 4.1 %slice_convert_fusion = (f32[512,1024]{1,0:T(8,128)}, f32[512,1024]{1,0:T(8,128)}) fusion(bf16[1024,1024]{1,0:T(8,128)(2,1)} %get-tuple-element.91), kind=kLoop, calls=%fused_computation.6 | loop fusion | flops 1048576 | bytes 6291456 | tf_op jit(solution)/shard_map/convert_element_type | solution.py:811
  278.8 1.1 convert_element_type.60
  279.9 1.1 convert_element_type.61
  281.0 1.1 convert_element_type.62
  282.1 1.1 convert_element_type.63
  283.2 0.8 convert_bitcast_fusion
  (92 shorter events, 11.3 us)
Async XLA Ops:
  7.2 7.7 %copy-start.19 = (f32[8]{0:T(128)S(1)}, f32[8]{0:T(128)}, u32[]{:S(2)}) copy-start(f32[8]{0:T(128)} %param.27) | copy-start | bytes 100
  7.2 6.4 %copy-start.10 = (f32[8,256,64]{1,2,0:T(8,128)S(1)}, f32[8,256,64]{1,2,0:T(8,128)}, u32[]{:S(2)}) copy-start(f32[8,256,64]{1,2,0:T(8,128)} %param.30) | copy-start | bytes 1572868
  7.2 6.4 %copy-start.17 = (f32[8,256]{1,0:T(8,128)S(1)}, f32[8,256]{1,0:T(8,128)}, u32[]{:S(2)}) copy-start(f32[8,256]{1,0:T(8,128)} %param.31) | copy-start | bytes 24580
  7.2 61.2 %all-gather.6.cloned.1.call-start = ((), (), s32[]{:S(2)}) async-start(), calls=%async_computation | async-start | bytes 3145728 | tf_op jit(solution)/shard_map/all_gather | solution.py:567
  8.0 72.5 %all-gather.8.cloned.1.call-start = ((), (), s32[]{:S(2)}) async-start(), calls=%async_computation.1 | async-start | bytes 3145728 | tf_op jit(solution)/shard_map/all_gather | solution.py:568
  13.6 1.9 copy-start
  13.6 37.1 %copy-start.18 = (bf16[1024]{0:T(1024)(128)(2,1)S(1)}, bf16[1024]{0:T(1024)(128)(2,1)}, u32[]{:S(2)}) copy-start(bf16[1024]{0:T(1024)(128)(2,1)} %param.35) | copy-start | bytes 6148
  13.7 37.1 %copy-start.13 = (bf16[512,8]{0,1:T(8,128)(2,1)S(1)}, bf16[512,8]{0,1:T(8,128)(2,1)}, u32[]{:S(2)}) copy-start(bf16[512,8]{0,1:T(8,128)(2,1)} %param.26) | copy-start | bytes 24580
  45.6 22.8 %collective-permute-start = (bf16[8,80,256]{2,1,0:T(8,128)(2,1)}, bf16[8,80,256]{2,1,0:T(8,128)(2,1)S(1)}, u32[]{:S(2)}, u32[]{:S(2)}) collective-permute-start(bf16[8,80,256]{2,1,0:T(8,128)(2,1)} %get-tuple-element.61), channel_id=1, source_target_pairs={{0,1},{2,3},{4,5},{6,7},{8,9},{10,11},{12,13},{14,15},{16,17},{18,... | collective-permute-start | bytes 983048 | tf_op jit(solution)/shard_map/ppermute | solution.py:525
  68.4 12.1 %copy-start.1 = (bf16[8,80,256]{2,1,0:T(8,128)(2,1)}, bf16[8,80,256]{2,1,0:T(8,128)(2,1)S(1)}, u32[]{:S(2)}) copy-start(bf16[8,80,256]{2,1,0:T(8,128)(2,1)S(1)} %collective-permute-done.entry_ref) | copy-start | bytes 983044
  112.3 14.4 %collective-permute-start.1 = (bf16[8,80,256]{2,1,0:T(8,128)(2,1)}, bf16[8,80,256]{2,1,0:T(8,128)(2,1)S(1)}, u32[]{:S(2)}, u32[]{:S(2)}) collective-permute-start(bf16[8,80,256]{2,1,0:T(8,128)(2,1)} %get-tuple-element.70), channel_id=1, source_target_pairs={{1,0},{3,2},{5,4},{7,6},{9,8},{11,10},{13,12},{15,14},{17,16},{19,... | collective-permute-start | bytes 983048 | tf_op jit(solution)/shard_map/ppermute | solution.py:525
  113.8 5.2 %copy-start.20 = (bf16[1024,2048]{1,0:T(8,128)(2,1)S(1)}, bf16[1024,2048]{1,0:T(8,128)(2,1)}, u32[]{:S(2)}) copy-start(bf16[1024,2048]{1,0:T(8,128)(2,1)} %get-tuple-element.74) | copy-start | bytes 12582916
  118.8 1.2 copy-start.2
  122.7 2.3 copy-start.16
  122.7 2.4 copy-start.14
  122.7 2.4 copy-start.21
  122.7 2.5 copy-start.22
  126.7 0.7 copy-start.11
  170.2 3.6 %copy-start.15 = (f32[24,512]{1,0:T(8,128)S(1)}, f32[24,512]{1,0:T(8,128)}, u32[]{:S(2)}) copy-start(f32[24,512]{1,0:T(8,128)} %get-tuple-element.83) | copy-start | bytes 147460
  170.2 4.3 %copy-start.5 = (f32[512,512]{1,0:T(8,128)S(1)}, f32[512,512]{1,0:T(8,128)}, u32[]{:S(2)}) copy-start(f32[512,512]{1,0:T(8,128)} %get-tuple-element.75) | copy-start | bytes 3145732
  170.3 5.2 %copy-start.4 = (f32[512,512]{1,0:T(8,128)S(1)}, f32[512,512]{1,0:T(8,128)}, u32[]{:S(2)}) copy-start(f32[512,512]{1,0:T(8,128)} %get-tuple-element.76) | copy-start | bytes 3145732
  170.3 6.0 %copy-start.3 = (f32[512,512]{1,0:T(8,128)S(1)}, f32[512,512]{1,0:T(8,128)}, u32[]{:S(2)}) copy-start(f32[512,512]{1,0:T(8,128)} %get-tuple-element.77) | copy-start | bytes 3145732
  269.8 9.0 %copy-start.9 = (bf16[512,512]{1,0:T(8,128)(2,1)S(1)}, bf16[512,512]{1,0:T(8,128)(2,1)}, u32[]{:S(2)}) copy-start(bf16[512,512]{1,0:T(8,128)(2,1)} %get-tuple-element.86) | copy-start | bytes 1572868
  269.8 10.1 %copy-start.8 = (bf16[512,512]{1,0:T(8,128)(2,1)S(1)}, bf16[512,512]{1,0:T(8,128)(2,1)}, u32[]{:S(2)}) copy-start(bf16[512,512]{1,0:T(8,128)(2,1)} %get-tuple-element.87) | copy-start | bytes 1572868
  274.7 6.3 %copy-start.7 = (bf16[512,512]{1,0:T(8,128)(2,1)S(1)}, bf16[512,512]{1,0:T(8,128)(2,1)}, u32[]{:S(2)}) copy-start(bf16[512,512]{1,0:T(8,128)(2,1)} %get-tuple-element.88) | copy-start | bytes 1572868
  274.7 7.4 %copy-start.6 = (bf16[512,512]{1,0:T(8,128)(2,1)S(1)}, bf16[512,512]{1,0:T(8,128)(2,1)}, u32[]{:S(2)}) copy-start(bf16[512,512]{1,0:T(8,128)(2,1)} %get-tuple-element.89) | copy-start | bytes 1572868
  278.8 4.4 %copy-start.12 = (bf16[512,256]{1,0:T(8,128)(2,1)S(1)}, bf16[512,256]{1,0:T(8,128)(2,1)}, u32[]{:S(2)}) copy-start(bf16[512,256]{1,0:T(8,128)(2,1)} %get-tuple-element.90) | copy-start | bytes 786436
Sparse Core Ops, SparseCore 0:
  9.6 35.7 all-gather.5
  47.0 33.4 all-gather.7

commit v3 on v2

--- a/solution.py
+++ b/solution.py
@@ -20,6 +20,7 @@
 C = 128
 T = 256
 HB = 512
+GROUP_HEADS = 4
 LANES = 128
 PAY = 80
 
@@ -187,7 +188,15 @@
     keep_row = log_sigmoid(logit_row)
     upper = jnp.where(iota((C, C), 0) <= iota((C, C), 1), 1.0, 0.0)
     decay_row = exact(keep_row, upper)
-    grow_ref[...] = jnp.concatenate([keep_row - logit_row - decay_row, decay_row], axis=0)
+    grow_ref[...] = jnp.concatenate(
+        [
+            keep_row - logit_row - decay_row,
+            decay_row,
+            jax.nn.sigmoid(logit_row),
+            jax.nn.sigmoid(-logit_row),
+        ],
+        axis=0,
+    )
 
     lower = lower_half((C, LANES))
     ftr_scale = 1.0 / math.sqrt(LANES)
@@ -356,67 +365,143 @@
             final_ref[h] = shrink_state(adj[h], h)
 
 
-def back_kernel(
-    heads,
-    x_ref,
-    mg_ref,
-    ml_ref,
-    uq_ref,
-    uk_ref,
-    rq_ref,
-    rk_ref,
-    qf_ref,
-    kf_ref,
-    v_ref,
-    a_ref,
-    gcol_ref,
-    grow_ref,
-    before_ref,
-    entry_ref,
-    after_ref,
-    gain_ref,
-    wq_ref,
-    wk_ref,
-    wv_ref,
-    wgt_ref,
-    pcat_ref,
-    dx_ref,
-    dwq_ref,
-    dwk_ref,
-    dwv_ref,
-    dwg_ref,
-    adj_ref,
-    sums_ref,
-):
-    step = pl.program_id(0)
-
-    @pl.when(step == 0)
+def back_kernel(heads, hg, chunks, comm, *refs):
+    refs = list(refs)
+
+    def take(n):
+        taken = refs[:n]
+        del refs[:n]
+        return taken
+
+    (qf_ref, kf_ref, v_ref, uq_ref, uk_ref, rq_ref, rk_ref, a_ref, gcol_ref, grow_ref) = take(10)
+    before_ref, entry_ref, after_ref, proj_ref = take(4)
+    x_hbm, mg_hbm, ml_hbm, wq_hbm, wk_hbm, wv_hbm, wgt_ref, gain_ref = take(8)
+    u_hbm, o_hbm, s_hbm, f_hbm = take(4) if comm else (None,) * 4
+    dx_ref, w_ref, small_ref = take(3)
+    usum_hbm, osum_hbm, ssum_hbm, fsum_hbm = take(4) if comm else (None,) * 4
+    adj_ref, dqkv, dlogit, x_ref, mg_ref, ml_ref, wq_ref, wk_ref, wv_ref, load_sems = take(10)
+    g, i = pl.program_id(0), pl.program_id(1)
+    tick = g * chunks + i
+    last = heads // hg * chunks - 1
+    chunk = chunks - 1 - i
+    here = pl.ds(pl.multiple_of(chunk * C, C), C)
+    groups = heads // hg
+    loads = [
+        (x_hbm, x_ref),
+        (mg_hbm, mg_ref),
+        (ml_hbm, ml_ref),
+        (wq_hbm, wq_ref),
+        (wk_hbm, wk_ref),
+        (wv_hbm, wv_ref),
+    ]
+    if comm:
+        u_ref, o_ref, s_ref, f_ref, w_src, small_src = take(6)
+        usum_ref, osum_ref, ssum_ref, fsum_ref, wsum_ref, smallsum_ref = take(6)
+        store_sems = refs.pop(0)
+        loads = [(u_hbm, u_ref), (o_hbm, o_ref), (s_hbm, s_ref), (f_hbm, f_ref)] + loads
+        links = Links()
+        streams, starts, stores = [], [], []
+
+        def add(plan, source, out, final, start):
+            streams.append(Stream(plan, links, source, out, take(len(plan.scratch()))))
+            starts.append(start)
+            stores.append((out, final))
+
+        def store(k):
+            return pltpu.make_async_copy(*stores[k], store_sems.at[k])
+
+        plans = back_plans(u_hbm.shape, o_hbm.shape, s_hbm.shape, f_hbm.shape, w_src.shape, small_src.shape)
+        n_u = u_hbm.shape[1] // plans["u"].lanes
+        for k in range(n_u):
+            lanes = pl.ds(k * plans["u"].lanes, plans["u"].lanes)
+            add(plans["u"], u_ref.at[:, lanes], usum_ref.at[:, lanes], usum_hbm.at[:, lanes], k + 1)
+        add(plans["f"], f_ref, fsum_ref, fsum_hbm, 3)
+        add(plans["s"], s_ref, ssum_ref, ssum_hbm, 5)
+        add(plans["o"], o_ref, osum_ref, osum_hbm, 7)
+        for k in range(groups):
+            for j in range(3):
+                lanes = pl.ds(j * plans["w"].lanes, plans["w"].lanes)
+                add(
+                    plans["w"],
+                    w_src.at[k, :, lanes],
+                    wsum_ref.at[k, :, lanes],
+                    w_ref.at[k, :, lanes],
+                    (k + 1) * chunks,
+                )
+
+        def advance(now):
+            for k, (stream, start) in enumerate(zip(streams, starts)):
+                stage = now - start
+                if 0 < stage <= stream.plan.stages:
+                    stream.finish(stage - 1)
+                    if stage == stream.plan.stages:
+                        store(k).start()
+                if 0 <= stage < stream.plan.stages:
+                    stream.start(stage)
+
+    def load(k):
+        return pltpu.make_async_copy(loads[k][0], loads[k][1], load_sems.at[k])
+
+    @pl.when(tick == 0)
     def _():
-        for h in range(heads):
+        for k in range(len(loads)):
+            load(k).start()
+        dlogit[...] = jnp.zeros_like(dlogit)
+        if comm:
+            links.greet(("core", "plane", "z"))
+
+    if comm:
+        @pl.when(tick == 1)
+        def _():
+            for k in range(4):
+                load(k).wait()
+
+        for now in range(1, last + 1):
+            pl.when(tick == now)(partial(advance, now))
+
+    @pl.when(i == 0)
+    def _():
+        for h in range(hg):
             adj_ref[h] = grow_state(after_ref, h)
-        for ref in (dwq_ref, dwk_ref, dwv_ref, dwg_ref, sums_ref):
-            ref[...] = jnp.zeros_like(ref)
 
     row = iota((C, C), 0)
     col = iota((C, C), 1)
     causal = row >= col
-    strict = row > col
-    from_here = jnp.where(row <= col, 1.0, 0.0).astype(BF16)
-    until_here = jnp.where(strict, 1.0, 0.0).astype(BF16)
-    both_sums = jnp.concatenate([from_here, until_here], axis=1)
+    one = jnp.ones((C, C), BF16)
+    zero = jnp.zeros((C, C), BF16)
+    later = jnp.where(row < col, 1.0, 0.0).astype(BF16)
+    pair_sums = jnp.concatenate([later, one], axis=0)
+    two_sums = jnp.concatenate(
+        [jnp.concatenate([one, zero], axis=1), jnp.concatenate([zero, one], axis=1)], axis=0
+    )
     lower = lower_half((C, LANES))
     gcol = gcol_ref[...]
-    grads = {"q": [], "k": [], "v": []}
-    logit_parts = []
-    for p in range(heads // 2):
+    if groups > 1:
+        gcol = jnp.where(g == 0, gcol, pltpu.roll(gcol, LANES - hg, 1))
+
+    def grow_row(kind, h):
+        return grow_ref[pl.ds(kind * heads + g * hg + h, 1), :]
+
+    for p in range(hg // 2):
         lanes = slice(LANES * p, LANES * (p + 1))
-        angle_q, angle_k, dvs = [], [], []
+        angle_q, angle_k, dvs, x_parts, y_parts, throughs = [], [], [], [], [], []
         v_pair = v_ref[:, lanes].astype(F32)
-        for h in (2 * p, 2 * p + 1):
+        values = [jnp.where(mine(h, lower), v_pair, 1.0) for h in range(2)]
+        values_low = [part.astype(BF16) for part in values]
+        dweights = nt(
+            a_ref[:, 2 * LANES * p : 2 * LANES * (p + 1)],
+            jnp.concatenate(
+                [
+                    jnp.concatenate([values_low[0], zero], axis=1),
+                    jnp.concatenate([zero, values_low[1]], axis=1),
+                ],
+                axis=0,
+            ),
+        )
+        for j in range(2):
+            h = 2 * p + j
             qf = qf_ref[:, 256 * h : 256 * (h + 1)]
             kf = kf_ref[:, 256 * h : 256 * (h + 1)]
-            values = jnp.where(mine(h, lower), v_pair, 1.0)
-            values_low = values.astype(BF16)
             a_low = a_ref[:, LANES * h : LANES * (h + 1)]
             a = a_low.astype(F32)
             decay = column(gcol, h, C, LANES)
@@ -424,96 +509,164 @@
             coef = jnp.exp(column(gcol, 8 + h, C, LANES))
             carried = jnp.exp(gcol[0:1, 48 + h : 49 + h])
             total = jnp.exp(gcol[0:1, 56 + h : 57 + h])
-            entry = grow_state(entry_ref, h)
-            before = before_ref[0, h].astype(F32) + carried * entry
+            before = before_ref[0, h].astype(F32) + carried * grow_state(entry_ref, h)
             before_low = before.astype(BF16)
             adj = adj_ref[h]
             adj_low = adj.astype(BF16)
-            pairs = jnp.where(causal, jnp.exp(decay + grow_ref[h : h + 1, :]), 0.0)
-            raw = nt(qf, kf)
+            kept = total * adj
+            through = jnp.sum(kept * before, axis=0, keepdims=True)
+            throughs.append(jnp.sum(through, axis=1, keepdims=True))
+            pairs = jnp.where(causal, jnp.exp(decay + grow_row(0, h)), 0.0)
+            keys_and_state = jnp.concatenate([kf, before_low], axis=0)
+            raw_and_far = nt(qf, keys_and_state)
+            raw = raw_and_far[:, :C]
             weights = (raw * pairs).astype(BF16)
-            dweights = nt(a_low, values_low).astype(BF16).astype(F32)
-            draw = dweights * pairs
+            draw = dweights[:, C * j : C * (j + 1)].astype(BF16).astype(F32) * pairs
             draw_low = draw.astype(BF16)
             both = (raw * draw).astype(BF16)
             a_lift = (a * lift).astype(BF16)
-            v_coef = (values * coef).astype(BF16)
-            dq = nn(
-                jnp.concatenate([draw_low, a_lift], axis=1),
-                jnp.concatenate([kf, before_low], axis=0),
+            v_coef = (values[j] * coef).astype(BF16)
+            dq = nn(jnp.concatenate([draw_low, a_lift], axis=1), keys_and_state)
+            dk = nn(
+                jnp.concatenate([draw_low.T, v_coef], axis=1),
+                jnp.concatenate([qf, adj_low], axis=0),
             )
-            dk = tn(draw_low, qf) + nn(v_coef, adj_low)
             dv_far = coef * nt(kf, adj_low)
             dv = tn(weights, a_low) + dv_far
-            n_far = lift * nt(qf, before_low)
-            near = jnp.concatenate([a * n_far, values * dv_far], axis=0).astype(BF16)
-            through = jnp.sum(total * adj * before, axis=0, keepdims=True)
-            through = through[:, :LANES] + through[:, LANES:]
-            flow = nn(both_sums, near) + jnp.where(strict, nn(from_here, both), 0.0) + through
-            stay = column(gcol, 24 + h, C, LANES)
-            leave = column(gcol, 40 + h, C, LANES)
-            logit_parts.append((leave * flow - stay * (values * dv)).astype(BF16))
-            adj_ref[h] = total * adj + tn(a_lift, qf)
+            x_far = (a * lift * raw_and_far[:, C:]).astype(BF16)
+            x_parts.append(jnp.concatenate([both, x_far], axis=1))
+            y_parts.append(
+                jnp.concatenate(
+                    [(values[j] * dv_far).astype(BF16), (values[j] * dv).astype(BF16)], axis=1
+                )
+            )
+            adj_ref[h] = kept + tn(a_lift, qf)
             for feats, grad, angle in ((qf, dq, angle_q), (kf, dk, angle_k)):
                 f = feats.astype(F32)
                 angle.append(grad[:, :LANES] * f[:, LANES:] - grad[:, LANES:] * f[:, :LANES])
             dvs.append(dv)
-        proj = pcat_ref[p, 0:LANES, :]
-        for name, angle, u_ref, r_ref in (
-            ("q", angle_q, uq_ref, rq_ref),
-            ("k", angle_k, uk_ref, rk_ref),
-        ):
-            du = nt(jnp.concatenate(angle, axis=1).astype(BF16), proj)
-            u = u_ref[:, lanes].astype(F32)
-            along = nn((u * du).astype(BF16), block_ones())
-            grads[name].append((2.0 * math.pi) * r_ref[:, lanes] * (du - u * along))
-        grads["v"].append(jnp.where(lower, dvs[0], dvs[1]))
-    dq, dk, dv = (jnp.concatenate(grads[name], axis=1).astype(BF16) for name in "qkv")
-    select = jnp.where(
-        iota((LANES * heads, LANES), 0) // LANES == iota((LANES * heads, LANES), 1), 1.0, 0.0
-    ).astype(BF16)
-    dlogit = nn(jnp.concatenate(logit_parts, axis=1), select).astype(BF16)
-    ml = ml_ref[...]
-    dwq_ref[...] += tn(ml, dq)
-    dwk_ref[...] += tn(ml, dk)
-    dwv_ref[...] += tn(ml, dv)
-    dwg_ref[...] += tn(ml, dlogit)
-    mixer_grad = (
-        nt(dq, wq_ref[...])
-        + nt(dk, wk_ref[...])
-        + nt(dv, wv_ref[...])
-        + nn(dlogit, wgt_ref[...])
-    )
-    xhat, scale = normalize(x_ref[...].astype(F32))
-    sums_ref[0:8, :] += fold_rows(mixer_grad * xhat)
-    sums_ref[8:16, :] += fold_rows(mixer_grad)
-    sums_ref[16:24, 0:LANES] += fold_rows(dlogit.astype(F32))
-    dx_ref[...] = mg_ref[...] + normalize_back(mixer_grad, gain_ref[...], xhat, scale)
+        upto = nn(jnp.concatenate(x_parts, axis=0), pair_sums)
+        ends = nn(jnp.concatenate(y_parts, axis=0), two_sums)
+        for j in range(2):
+            h = 2 * p + j
+            rows = slice(C * j, C * (j + 1))
+            flow = jnp.where(causal, upto[rows], ends[rows, :C])
+            flow = jnp.sum(flow, axis=0, keepdims=True) + throughs[j]
+            own = jnp.sum(jnp.where(row == col, ends[rows, C:], 0.0), axis=0, keepdims=True)
+            dlogit[g, h : h + 1, here] = grow_row(3, h) * flow - grow_row(2, h) * own
+        angles = jnp.concatenate(
+            [jnp.concatenate(angle_q, axis=1), jnp.concatenate(angle_k, axis=1)], axis=0
+        )
+        du = nt(angles.astype(BF16), proj_ref[p])
+        u = jnp.concatenate([uq_ref[:, lanes], uk_ref[:, lanes]], axis=0).astype(F32)
+        scale = jnp.concatenate([rq_ref[:, lanes], rk_ref[:, lanes]], axis=0)
+        along = nn((u * du).astype(BF16), block_ones())
+        dqk = ((2.0 * math.pi) * scale * (du - u * along)).astype(BF16)
+        width = hg * 64
+        dqkv[g, here, LANES * p : LANES * (p + 1)] = dqk[:C]
+        dqkv[g, here, width + LANES * p : width + LANES * (p + 1)] = dqk[C:]
+        dqkv[g, here, 2 * width + LANES * p : 2 * width + LANES * (p + 1)] = jnp.where(
+            lower, dvs[0], dvs[1]
+        ).astype(BF16)
+
+    @pl.when(i == chunks - 1)
+    def _():
+        @pl.when(g == 0)
+        def _():
+            load(len(loads) - 4).wait()
+
+        grads = tn(ml_ref[...], dqkv[g]).astype(BF16)
+        if comm:
+            w_src[g] = grads
+        else:
+            w_ref[g] = grads
+
+    @pl.when(tick == last)
+    def _():
+        if comm:
+            advance(last + 1)
+        for k in range(len(loads) - 6, len(loads)):
+            if k != len(loads) - 4:
+                load(k).wait()
+        tokens = chunks * C
+        block = min(T, tokens)
+        small = small_src if comm else small_ref
+        rows8 = jnp.concatenate(
+            [dlogit[k, 0:hg, :] for k in range(groups)]
+            + [jnp.zeros((16 - heads, dlogit.shape[2]), F32)],
+            axis=0,
+        ).astype(BF16)
+        small[...] = jnp.zeros_like(small)
+        small[0:heads, :] = nn(rows8, ml_ref[...])[0:heads]
+        bias_sum = jnp.sum(rows8.astype(F32), axis=1, keepdims=True)[0:heads]
+        small[heads : 2 * heads, :] = jnp.broadcast_to(bias_sum, (heads, small.shape[1]))
+        gain = gain_ref[...]
+        now = last + 2
+        for b in range(tokens // block):
+            rows = slice(block * b, block * (b + 1))
+            mixer_grad = tn(rows8[:, rows], wgt_ref[...])
+            for k in range(groups):
+                for j, ref in enumerate((wq_ref, wk_ref, wv_ref)):
+                    mixer_grad = mixer_grad + nt(
+                        dqkv[k, rows, hg * 64 * j : hg * 64 * (j + 1)],
+                        ref[:, hg * 64 * k : hg * 64 * (k + 1)],
+                    )
+            xhat, scale = normalize(x_ref[rows, :].astype(F32))
+            small[2 * heads : 2 * heads + 1, :] += jnp.sum(
+                mixer_grad * xhat, axis=0, keepdims=True
+            )
+            small[2 * heads + 1 : 2 * heads + 2, :] += jnp.sum(mixer_grad, axis=0, keepdims=True)
+            dx_ref[rows, :] = mg_ref[rows, :] + normalize_back(mixer_grad, gain, xhat, scale)
+            if comm:
+                advance(now)
+                now += 1
+        if comm:
+            add(plans["small"], small_src, smallsum_ref, small_ref, now)
+            finish = max(start + stream.plan.stages for stream, start in zip(streams, starts))
+            for later_tick in range(now, finish + 1):
+                advance(later_tick)
+            for k, stream in enumerate(streams):
+                stream.drain()
+                store(k).wait()
+
+
+def back_plans(u, o, s, f, w, small):
+    return {
+        "u": Plan(u[0], 128, BF16, *UP_PLAN),
+        "o": Plan(o[0], o[1], BF16, *ALL_PLAN),
+        "s": Plan(s[0], s[1], BF16, *ALL_PLAN),
+        "f": Plan(f[0], f[1], F32, *SHARE_PLAN),
+        "w": Plan(w[1], w[2] // 3, BF16, *ALL_PLAN),
+        "small": Plan(small[0], small[1], F32, *SHARE_PLAN),
+    }
 
 
 def whole(shape):
     zeros = (0,) * len(shape)
-    return pl.BlockSpec(shape, lambda i: zeros)
-
-
-def call(kernel, steps, ins, outs, scratch, name):
-    in_specs = [
-        whole(array.shape) if block is None else pl.BlockSpec(block, index)
-        for array, block, index in ins
-    ]
-    out_specs = [
-        whole(shape) if block is None else pl.BlockSpec(block, index)
-        for shape, dtype, block, index in outs
-    ]
+    return pl.BlockSpec(shape, lambda *at: zeros, pipeline_mode=pl.Buffered(1))
+
+
+ANY = pl.BlockSpec(memory_space=pl.ANY)
+
+
+def call(kernel, grid, ins, outs, scratch, name, collective_id=None):
+    def spec(shape, block, index):
+        if block is None:
+            return whole(shape)
+        return block if isinstance(block, pl.BlockSpec) else pl.BlockSpec(block, index)
+
+    params = {} if collective_id is None else {
+        "collective_id": collective_id, "has_side_effects": True
+    }
     return pl.pallas_call(
         kernel,
-        grid=(steps,),
-        in_specs=in_specs,
-        out_specs=out_specs,
+        grid=grid,
+        in_specs=[spec(array.shape, block, index) for array, block, index in ins],
+        out_specs=[spec(shape, block, index) for shape, _, block, index in outs],
         out_shape=[jax.ShapeDtypeStruct(shape, dtype) for shape, dtype, _, _ in outs],
         scratch_shapes=scratch,
         compiler_params=pltpu.CompilerParams(
-            dimension_semantics=("arbitrary",), vmem_limit_bytes=VMEM
+            dimension_semantics=("arbitrary",) * len(grid), vmem_limit_bytes=VMEM, **params
         ),
         name=name,
     )(*[array for array, _, _ in ins])
@@ -610,7 +763,7 @@
     wider = heads * 2 * feats
     ml, uq, uk, rq, rk, qf, kf, v, gcol, grow, before, final, total = call(
         partial(features_kernel, heads),
-        chunks,
+        (chunks,),
         [
             (x,) + rows(width),
             const(mixer_gain),
@@ -635,7 +788,7 @@
             out_rows(wider, BF16),
             out_rows(width, BF16),
             out_rows(LANES, F32),
-            ((2 * heads, tokens), F32, (2 * heads, C), lambda i: (0, i)),
+            ((4 * heads, tokens), F32, (4 * heads, C), lambda i: (0, i)),
             (
                 (chunks, heads, LANES, 2 * feats),
                 BF16,
@@ -653,13 +806,13 @@
     state_block = (1, heads, LANES, 2 * feats)
     (num,) = call(
         partial(inner_kernel, heads),
-        chunks,
+        (chunks,),
         [
             (qf,) + rows(wider),
             (kf,) + rows(wider),
             (v,) + rows(width),
             (gcol,) + rows(LANES),
-            (grow, (2 * heads, C), lambda i: (0, i)),
+            (grow, (4 * heads, C), lambda i: (0, i)),
             (before, state_block, lambda i: (i, 0, 0, 0)),
         ],
         [out_rows(wide, F32)],
@@ -668,7 +821,7 @@
     )
     out, mg, fl, hl, pre, mix, br, a, adj_final, feed_sums, upbg = call(
         partial(feed_kernel, heads, shards),
-        tiles,
+        (tiles,),
         [
             (x,) + rows(width, tile),
             (dout,) + rows(width, tile),
@@ -708,101 +861,148 @@
     up_grad = tn(fl, pre).astype(BF16)
     output_grad = tn(mix, br).astype(BF16)
 
-    def back_rows(n):
-        return (C, n), lambda i: (chunks - 1 - i, 0)
-
-    dx, dwq, dwk, dwv, dwg, adj, mixer_sums = call(
-        partial(back_kernel, heads),
-        chunks,
-        [
-            (x,) + back_rows(width),
-            (mg,) + back_rows(width),
-            (ml,) + back_rows(width),
-            (uq,) + back_rows(width),
-            (uk,) + back_rows(width),
-            (rq,) + back_rows(width),
-            (rk,) + back_rows(width),
-            (qf,) + back_rows(wider),
-            (kf,) + back_rows(wider),
-            (v,) + back_rows(width),
-            (a,) + back_rows(wide),
-            (gcol,) + back_rows(LANES),
-            (grow, (2 * heads, C), lambda i: (0, chunks - 1 - i)),
-            (before, state_block, lambda i: (chunks - 1 - i, 0, 0, 0)),
-            const(entry),
-            const(after),
-            const(mixer_gain),
-            const(query_weight),
-            const(key_weight),
-            const(value_weight),
-            const(jnp.pad(wgt, ((0, LANES - heads), (0, 0)))),
-            const(pcat),
-        ],
-        [
-            ((tokens, width), F32) + back_rows(width),
-            keep((width, width), F32),
-            keep((width, width), F32),
-            keep((width, width), F32),
-            keep((width, LANES), F32),
-            keep((heads, LANES, 2 * feats), F32),
-            keep((24, width), F32),
-        ],
-        [],
+    feed_three = jnp.sum(feed_sums.reshape(3, 8, width), axis=1)
+    upb_grad = jnp.sum(upbg, axis=0)
+    begin = adj_final.astype(F32) + jnp.exp(logs)[:, None, None] * after.astype(F32)
+    begin = jnp.where(first, begin, 0.0)
+    state_grad = begin[:, :64].astype(BF16).reshape(heads * 64, 2 * feats)
+    norm_grad = 64.0 * begin[:, 64]
+
+    hg = GROUP_HEADS
+    groups = heads // hg
+    comm = (lax.axis_size("dp"), lax.axis_size("seq")) == (16, 2)
+
+    def back_rows(n, per_group=True):
+        return (C, n), lambda g, i: (chunks - 1 - i, g if per_group else 0)
+
+    def per_group(array, *shape):
+        zeros = (0,) * (len(shape) - 1)
+        return (array, shape, lambda g, i: (g,) + zeros)
+
+    def hbm(array):
+        return (array, ANY, None)
+
+    ins = [
+        (qf,) + back_rows(hg * 2 * feats),
+        (kf,) + back_rows(hg * 2 * feats),
+        (v,) + back_rows(hg * size),
+        (uq,) + back_rows(hg * size),
+        (uk,) + back_rows(hg * size),
+        (rq,) + back_rows(hg * size),
+        (rk,) + back_rows(hg * size),
+        (a,) + back_rows(hg * LANES),
+        (gcol,) + back_rows(LANES, False),
+        (grow, (4 * heads, C), lambda g, i: (0, chunks - 1 - i)),
+        (before, (1, hg, LANES, 2 * feats), lambda g, i: (chunks - 1 - i, g, 0, 0)),
+        per_group(entry, hg, PAY, 2 * feats),
+        per_group(after, hg, PAY, 2 * feats),
+        per_group(pcat, hg // 2, LANES, 2 * feats),
+        hbm(x),
+        hbm(mg),
+        hbm(ml),
+        hbm(query_weight),
+        hbm(key_weight),
+        hbm(value_weight),
+        const(jnp.pad(wgt, ((0, 16 - heads), (0, 0)))),
+        const(mixer_gain),
+    ]
+    w_shape, small_shape = (groups, width, 3 * hg * size), (32, width)
+
+    def result(shape, dtype):
+        return (shape, dtype, ANY if comm else None, None)
+
+    outs = [keep((tokens, width), F32), result(w_shape, BF16), result(small_shape, F32)]
+    scratch = [
+        pltpu.VMEM((hg, LANES, 2 * feats), F32),
+        pltpu.VMEM((groups, tokens, 3 * hg * size), BF16),
+        pltpu.VMEM((groups, 8, tokens), F32),
+        pltpu.VMEM((tokens, width), BF16),
+        pltpu.VMEM((tokens, width), F32),
+        pltpu.VMEM((tokens, width), BF16),
+        pltpu.VMEM((width, width), BF16),
+        pltpu.VMEM((width, width), BF16),
+        pltpu.VMEM((width, width), BF16),
+        pltpu.SemaphoreType.DMA((10,)),
+    ]
+    if comm:
+        half = hidden // 2
+        up_halves = (up_grad[:, :half], up_grad[:, half:])
+        down_halves = (down_grad[:, :half], down_grad[:, half:])
+        up_down = jnp.concatenate(up_halves + down_halves)
+        flat = jnp.concatenate(
+            [feed_three, upb_grad.reshape(-1, width), norm_grad.reshape(-1, width)]
+        )
+        flat = jnp.pad(flat, ((0, 16 - flat.shape[0]), (0, 0)))
+        ins += [hbm(up_down), hbm(output_grad), hbm(state_grad), hbm(flat)]
+        outs += [
+            result((up_down.shape[0] // 2, half), BF16),
+            result(output_grad.shape, BF16),
+            result(state_grad.shape, BF16),
+            result(flat.shape, F32),
+        ]
+        plans = back_plans(
+            up_down.shape, output_grad.shape, state_grad.shape, flat.shape, w_shape, small_shape
+        )
+        scratch += [
+            pltpu.VMEM(up_down.shape, BF16),
+            pltpu.VMEM(output_grad.shape, BF16),
+            pltpu.VMEM(state_grad.shape, BF16),
+            pltpu.VMEM(flat.shape, F32),
+            pltpu.VMEM(w_shape, BF16),
+            pltpu.VMEM(small_shape, F32),
+            pltpu.VMEM((up_down.shape[0] // 2, half), BF16),
+            pltpu.VMEM(output_grad.shape, BF16),
+            pltpu.VMEM(state_grad.shape, BF16),
+            pltpu.VMEM(flat.shape, F32),
+            pltpu.VMEM(w_shape, BF16),
+            pltpu.VMEM(small_shape, F32),
+            pltpu.SemaphoreType.DMA((32,)),
+        ]
+        for _ in range(half // plans["u"].lanes):
+            scratch += plans["u"].scratch()
+        for name in ("f", "s", "o") + ("w",) * (3 * groups) + ("small",):
+            scratch += plans[name].scratch()
+    results = call(
+        partial(back_kernel, heads, hg, chunks, comm),
+        (groups, chunks),
+        ins,
+        outs,
+        scratch,
         "back",
+        1 if comm else None,
     )
-    adj = jnp.where(first, adj, 0.0)
-    state_grad = jnp.where(even, adj[:, :64], adj[:, 64:])
-    norm_grad = jnp.sum(jnp.where(even, adj[:, 64:], adj[:, :64]), axis=1)
-
-    feed_three = jnp.sum(feed_sums.reshape(3, 8, width), axis=1)
-    mixer_three = jnp.sum(mixer_sums.reshape(3, 8, width), axis=1)
-    upb_grad = jnp.sum(upbg, axis=0)
-    weight_grads = (dwq.astype(BF16), dwk.astype(BF16), dwv.astype(BF16), output_grad)
-    small = (dwg[:, :heads].T, norm_grad, feed_three, mixer_three)
-    if (lax.axis_size("dp"), lax.axis_size("seq")) == (16, 2):
-        half = hidden // 2
-        up_down = jnp.concatenate(
-            [up_grad[:, :half], up_grad[:, half:], down_grad[:, :half], down_grad[:, half:]]
-        )
-        flat = jnp.concatenate([part.reshape(-1) for part in small + (upb_grad,)])
-        flat = jnp.pad(flat, (0, 256 * LANES - flat.shape[0])).reshape(256, LANES)
-        state_rows = state_grad.astype(BF16).reshape(heads * 64, 2 * feats)
-        sum_up_down, sum_q, sum_k, sum_v, sum_o, sum_state, flat = sum_devices(
-            (up_down,) + weight_grads + (state_rows, flat),
-            ("half", "all", "all", "all", "all", "all", "all"),
-            (4, 1, 1, 1, 1, 1, 1),
-        )
+    dx, sum_w, small = results[:3]
+    if comm:
+        sum_up_down, sum_o, sum_state, flat = results[3:]
         sum_up, sum_down = sum_up_down[:width], sum_up_down[width:]
-        flat = flat.reshape(-1)
-        sums, at = [], 0
-        for part in small + (upb_grad,):
-            sums.append(flat[at : at + part.size].reshape(part.shape))
-            at += part.size
-        sum_g, sum_norm, sum_feed, sum_mixer, sum_upb = sums
+        sum_feed = flat[0:3]
+        sum_upb = flat[3 : 3 + hidden // width].reshape(-1)
         sum_upb = jnp.where(first, sum_upb[:half], sum_upb[half:])
-        sum_state = sum_state.reshape(heads, 64, 2 * feats)
+        sum_norm = flat[3 + hidden // width :][:4].reshape(heads, 2 * feats)
     else:
         halves = lax.psum_scatter(
             jnp.stack([up_grad, down_grad]), "seq", scatter_dimension=2, tiled=True
         )
         upb_half = lax.psum_scatter(upb_grad, "seq", scatter_dimension=0, tiled=True)
         (sum_up, sum_down), sum_upb = lax.psum((halves, upb_half), "dp")
-        sum_q, sum_k, sum_v, sum_o, sum_state = lax.psum(
-            weight_grads + (state_grad.astype(BF16),), ("dp", "seq")
+        sum_w, sum_o, sum_state, small, sum_norm, sum_feed = lax.psum(
+            (sum_w, output_grad, state_grad, small, norm_grad, feed_three), ("dp", "seq")
         )
-        sum_g, sum_norm, sum_feed, sum_mixer = lax.psum(small, ("dp", "seq"))
+    sum_w = sum_w.reshape(groups, width, 3, hg * size).transpose(2, 1, 0, 3)
+    sum_q, sum_k, sum_v = sum_w.reshape(3, width, width).astype(F32)
+    sum_state = sum_state.reshape(heads, size, 2 * feats).astype(F32).transpose(0, 2, 1)
     return (
         out.reshape(inputs.shape),
         dx.reshape(inputs.shape),
-        sum_mixer[0],
-        sum_mixer[1],
-        sum_q.astype(F32),
-        sum_k.astype(F32),
-        sum_v.astype(F32),
-        sum_g.T,
-        sum_mixer[2, :heads],
+        small[2 * heads],
+        small[2 * heads + 1],
+        sum_q,
+        sum_k,
+        sum_v,
+        small[:heads].T,
+        small[heads : 2 * heads, 0],
         sum_o.astype(F32),
-        sum_state.astype(F32).transpose(0, 2, 1),
+        sum_state,
         sum_norm,
         sum_feed[0],
         sum_feed[1],
@@ -848,10 +1048,11 @@
 
 
 class Plan:
-    def __init__(self, rows, lanes, dtype, scatter, gather):
-        self.scatter, self.gather, self.lanes, self.dtype = scatter, gather, lanes, dtype
-        self.rows = rows
-        self.stages = len(scatter) + len(gather)
+    def __init__(self, rows, lanes, dtype, scatter, gather, share=()):
+        self.scatter, self.gather, self.share = scatter, gather, share
+        self.rows, self.lanes, self.dtype = rows, lanes, dtype
+        self.groups = scatter + gather + share
+        self.stages = len(self.groups)
 
     def scratch(self):
         shapes = []
@@ -862,7 +1063,11 @@
             shapes.append(pltpu.VMEM((n - 1, rows, self.lanes), self.dtype))
             if i < len(self.scatter) - 1:
                 shapes.append(pltpu.VMEM((rows, self.lanes), self.dtype))
-        for group in self.scatter + self.gather:
+        for i, group in enumerate(self.share):
+            shapes.append(pltpu.VMEM((Links.size[group], rows, self.lanes), self.dtype))
+            if i < len(self.share) - 1:
+                shapes.append(pltpu.VMEM((rows, self.lanes), self.dtype))
+        for group in self.groups:
             n = Links.size[group]
             shapes.append(pltpu.SemaphoreType.DMA((n - 1,)))
             shapes.append(pltpu.SemaphoreType.DMA((n - 1,)))
@@ -874,9 +1079,10 @@
         self.plan, self.links, self.source, self.out = plan, links, source, out
         scratch = list(scratch)
         self.landing, self.parts = [], [source]
-        for i in range(len(plan.scatter)):
+        summed = plan.scatter + plan.share
+        for i in range(len(summed)):
             self.landing.append(scratch.pop(0))
-            if i < len(plan.scatter) - 1:
+            if i < len(summed) - 1:
                 self.parts.append(scratch.pop(0))
         self.sems = [(scratch.pop(0), scratch.pop(0)) for _ in range(plan.stages)]
         self.places = {}
@@ -890,37 +1096,37 @@
 
     def copies(self, stage, sending):
         plan, links = self.plan, self.links
-        scattering = stage < len(plan.scatter)
-        group = (plan.scatter + plan.gather)[stage]
+        group = plan.groups[stage]
         n, me = Links.size[group], links.at[group]
         sends, recvs = self.sems[stage]
         made = []
         for step in range(1, n):
-            if scattering:
+            target, origin = (me + step) % n, (me + n - step) % n
+            if plan.share:
+                source = self.parts[stage]
+                lands = self.landing[stage].at[me]
+                arrives = self.landing[stage].at[origin]
+            elif stage < len(plan.scatter):
                 landing = self.landing[stage]
                 rows = landing.shape[1]
-                target = (me + step) % n
                 source = self.parts[stage].at[pl.ds(pl.multiple_of(target * rows, 8), rows)]
                 arrives = lands = landing.at[step - 1]
             else:
                 start, rows = self.places[group]
                 mine_at = pl.multiple_of(start + me * rows, 8)
-                theirs_at = pl.multiple_of(start + ((me + n - step) % n) * rows, 8)
+                theirs_at = pl.multiple_of(start + origin * rows, 8)
                 source = lands = self.out.at[pl.ds(mine_at, rows)]
                 arrives = self.out.at[pl.ds(theirs_at, rows)]
-            device = links.partner(group, step)
-
-            def copy(src, dst):
-                return pltpu.make_async_remote_copy(
-                    src_ref=src,
-                    dst_ref=dst,
+            made.append(
+                pltpu.make_async_remote_copy(
+                    src_ref=source if sending else arrives,
+                    dst_ref=lands if sending else arrives,
                     send_sem=sends.at[step - 1],
                     recv_sem=recvs.at[step - 1],
-                    device_id=device,
+                    device_id=links.partner(group, step),
                     device_id_type=MESH,
                 )
-
-            made.append(copy(source, lands) if sending else copy(arrives, arrives))
+            )
         return made
 
     def start(self, stage):
@@ -928,19 +1134,30 @@
             copy.start()
 
     def finish(self, stage):
+        plan = self.plan
         for copy in self.copies(stage, False):
             copy.wait_recv()
-        if stage >= len(self.plan.scatter):
+        if plan.share:
+            landing, me = self.landing[stage], self.links.at[plan.groups[stage]]
+            landing[me] = self.parts[stage][...]
+            total = landing[0]
+            for k in range(1, landing.shape[0]):
+                total = total + landing[k]
+            if stage + 1 < plan.stages:
+                self.parts[stage + 1][...] = total
+            else:
+                self.out[...] = total
             return
-        group = self.plan.scatter[stage]
+        if stage >= len(plan.scatter):
+            return
         landing = self.landing[stage]
         arrivals, rows, _ = landing.shape
-        own = pl.multiple_of(self.links.at[group] * rows, 8)
+        own = pl.multiple_of(self.links.at[plan.groups[stage]] * rows, 8)
         total = self.parts[stage][pl.ds(own, rows), :].astype(F32)
         for step in range(arrivals):
             total = total + landing[step].astype(F32)
         total = total.astype(landing.dtype)
-        if stage + 1 < len(self.plan.scatter):
+        if stage + 1 < len(plan.scatter):
             self.parts[stage + 1][...] = total
         else:
             start, rows = self.final
@@ -952,58 +1169,9 @@
                 copy.wait_send()
 
 
-def run_streams(streams):
-    stages = max(stream.plan.stages for stream in streams)
-    for tick in range(stages + len(streams)):
-        for i, stream in enumerate(streams):
-            stage = tick - i
-            if 0 < stage <= stream.plan.stages:
-                stream.finish(stage - 1)
-            if 0 <= stage < stream.plan.stages:
-                stream.start(stage)
-    for stream in streams:
-        stream.drain()
-
-
 UP_PLAN = (("core", "x", "y", "z"), ("z", "y", "core"))
 ALL_PLAN = (("core", "plane", "z"), ("z", "plane", "core"))
-
-
-def sum_kernel(plans, splits, n_in, *refs):
-    sources, outs, scratch = refs[:n_in], refs[n_in : 2 * n_in], list(refs[2 * n_in :])
-    links = Links()
-    links.greet(("core", "plane", "z"))
-    streams = []
-    for source, out, plan, split in zip(sources, outs, plans, splits):
-        for part in range(split):
-            own = [scratch.pop(0) for _ in plan.scratch()]
-            lanes = pl.ds(part * plan.lanes, plan.lanes)
-            streams.append(Stream(plan, links, source.at[:, lanes], out.at[:, lanes], own))
-    run_streams(streams)
-
-
-def sum_devices(arrays, kinds, splits):
-    plans, shapes, scratch = [], [], []
-    for array, kind, split in zip(arrays, kinds, splits):
-        rows, lanes = array.shape
-        scatter, gather = UP_PLAN if kind == "half" else ALL_PLAN
-        plan = Plan(rows, lanes // split, array.dtype, scatter, gather)
-        plans.append(plan)
-        for _ in range(split):
-            scratch.extend(plan.scratch())
-        out_rows = rows // 2 if kind == "half" else rows
-        shapes.append(jax.ShapeDtypeStruct((out_rows, lanes), array.dtype))
-    return pl.pallas_call(
-        partial(sum_kernel, plans, splits, len(arrays)),
-        in_specs=[pl.BlockSpec(memory_space=pltpu.VMEM)] * len(arrays),
-        out_specs=[pl.BlockSpec(memory_space=pltpu.VMEM)] * len(arrays),
-        out_shape=shapes,
-        scratch_shapes=scratch,
-        compiler_params=pltpu.CompilerParams(
-            collective_id=1, has_side_effects=True, vmem_limit_bytes=VMEM
-        ),
-        name="sums",
-    )(*arrays)
+SHARE_PLAN = ((), (), ("core", "plane", "z"))
 
 
 def solution(mesh):

time: 293 us -> 271 us (0.925)
  Pallas kernels: 210 us -> 185 us
  local copies, waits for them, and re-layouts: 13.6 us -> 26.2 us
  other arithmetic: 21.2 us -> 11.6 us
    pallas_call x5 -> x4, Pallas kernels: 210 us -> 185 us  [call(): pl.pallas_call(kernel, grid=grid, in_specs=[spec(array.shape, block, inde...]
    unnamed x57 -> x48, local copies, waits for them, and re-layouts: 2.05 us -> 11.5 us
    convert_element_type x7 -> x0, other arithmetic: 6.72 us -> none  [the longest x1 1.1 us: local(): sum_q.astype(F32)]
  transfers between devices with their start and end apart: 4 -> 4, of which waited for: 1 -> 1; matrix products, arithmetic and copies ran while one was open for 7% -> 7% of each run, Pallas kernels for 15% -> 16%
where the time goes in v3:
time: 271 us; the launch traced here: 270 us
  Pallas kernels  185 us (68%)
  local copies, waits for them, and re-layouts  26.2 us (10%)
  between operations  14.4 us (5%)
  waiting for transfers between devices  12.8 us (5%)
  other arithmetic  11.6 us (4%)
  matrix products  8.98 us (3%)
  starting transfers between devices  6.64 us (2%)
  blocking collectives  4.48 us (2%)
    pallas_call x4, Pallas kernels, call(): pl.pallas_call(kernel, grid=grid, in_specs=[spec(array.shape, block, inde...  185 us
    unnamed x48, local copies, waits for them, and re-layouts  11.5 us
    all_gather x1, waiting for transfers between devices, local(): every_down = lax.all_gather(down_weight, 'seq')  11.4 us
    dot_general x3, matrix products, tn(): lax.dot_general(a, b, (((0,), (0,)), ((), ())), preferred_element_type=F32)  8.98 us
    ppermute x2, starting transfers between devices, carry_over(): return lax.ppermute(payload, 'seq', [(0, 1)] if forward else [(1, 0)])  6.57 us
  transfers between devices with their start and end apart: 4, of which 1 were waited for; matrix products, arithmetic and copies ran while one was open for 7% of the time, Pallas kernels for 16%

profile of v3, /device:TPU:0, one launch (start us, length us, event | category | flops | bytes accessed | tf_op | source)
XLA Modules:
  0.0 270.0 jit_solution(1962544950883259996)
XLA Ops:
  8.7 1.0 multiply_reduce-precision_fusion
  10.4 0.8 copy.46.wg_ref
  12.5 1.0 subtract_convert_fusion
  13.8 1.1 maximum_select_fusion.start_ref
  15.6 30.1 %features.1 = (bf16[1024,512]{1,0:T(8,128)(2,1)}, bf16[1024,512]{1,0:T(8,128)(2,1)}, bf16[1024,512]{1,0:T(8,128)(2,1)}, f32[1024,512]{1,0:T(8,128)}, f32[1024,51...) custom-call(bf16[1024,512]{1,0:T(8,128)(2,1)} %bitcast.54, ...), custom_call_target="tpu_custom_call" | custom-call | tf_op jit(solution)/shard_map/features/pallas_call | solution.py:661
  45.6 5.1 %collective-permute-start = (bf16[8,80,256]{2,1,0:T(8,128)(2,1)}, bf16[8,80,256]{2,1,0:T(8,128)(2,1)S(1)}, u32[]{:S(2)}, u32[]{:S(2)}) collective-permute-start(bf16[8,80,256]{2,1,0:T(8,128)(2,1)} %get-tuple-element.55), channel_id=1, source_target_pairs={{0,1},{2,3},{4,5},{6,7},{8,9},{10,11},{12,13},{14,15},{16,17},{18,... | collective-permute-start | bytes 983048 | tf_op jit(solution)/shard_map/ppermute | solution.py:678
  51.4 12.4 %inner.1.n_ref = f32[1024,1024]{1,0:T(8,128)} custom-call(bf16[1024,2048]{1,0:T(8,128)(2,1)} %get-tuple-element.49.qf_ref.refs_0_, bf16[1024,2048]{1,0:T(8,128)(2,1)} %get-tuple-element.50.kf_ref.refs_1_, bf16[1024,512]{1,0:T(8,128)(2,1)} %get-tuple-element.51.v_ref.refs_2_, f32[1024,128]{1,0:T(8,128)} %get-tuple-element.52.gcol_ref.refs_8_, ...), custom_call_target="tpu_custom_call" | custom-call | tf_op jit(solution)/shard_map/inner/pallas_call | solution.py:661
  63.8 4.5 %all-gather.1 = f32[2048]{0:T(1024)} all-gather(f32[1024]{0:T(1024)S(1)} %all_gather.28), channel_id=3, replica_groups=mesh['dp'=16,'seq'=2] {'seq'}, dimensions={0}, use_global_device_ids=true | all-gather | bytes 12288 | tf_op jit(solution)/shard_map/all_gather | solution.py:722
  69.0 11.4 %all-gather.8.cloned.1.call-done = bf16[1024,1024]{1,0:T(8,128)(2,1)} async-done(((bf16[512,1024]{1,0:T(8,128)(2,1)}), bf16[1024,1024]{1,0:T(8,128)(2,1)}) %all-gather.8.cloned.1.call-update) | async-done | bytes 2097168 | tf_op jit(solution)/shard_map/all_gather | solution.py:721
  80.5 31.8 %feed.1 = (bf16[1024,512]{1,0:T(8,128)(2,1)}, f32[1024,512]{1,0:T(8,128)}, bf16[1024,512]{1,0:T(8,128)(2,1)}, bf16[1024,2048]{1,0:T(8,128)(2,1)}, bf16[1024,2048...) custom-call(bf16[1024,512]{1,0:T(8,128)(2,1)} %bitcast.55, ...), custom_call_target="tpu_custom_call" | custom-call | tf_op jit(solution)/shard_map/feed/pallas_call | solution.py:661
  112.3 1.5 collective-permute-start.1
  113.8 5.0 %convolution_convert_fusion.1 = bf16[512,2048]{1,0:T(8,128)(2,1)S(1)} fusion(bf16[1024,512]{1,0:T(8,128)(2,1)} %get-tuple-element.65, bf16[1024,2048]{1,0:T(8,128)(2,1)} %get-tuple-element.66), kind=kOutput, calls=%fused_computation.2 | convolution fusion | flops 2148532224 | bytes 7340032 | tf_op jit(solution)/shard_map/dot_general | solution.py:43
  119.0 1.0 copy-done.5
  120.0 2.4 fusion
  122.7 2.3 pad_maximum_fusion.refs_22_
  125.2 1.5 convolution_convert_fusion.2.refs_23_
  126.9 0.7 slice.128
  128.3 110.5 %back.1 = (f32[1024,512]{1,0:T(8,128)}, bf16[2,512,768]{2,1,0:T(8,128)(2,1)}, f32[32,512]{1,0:T(8,128)}, bf16[1024,1024]{1,0:T(8,128)(2,1)}, bf16[512,512]{1,0:T...) custom-call(bf16[1024,2048]{1,0:T(8,128)(2,1)} %get-tuple-element.49.qf_ref.refs_0_, ...), custom_call_target="tpu_custom_call" | custom-call | tf_op jit(solution)/shard_map/back/pallas_call | solution.py:661
  238.8 0.8 slice.103
  239.6 1.4 fusion.13
  241.0 1.3 slice_bitcast_fusion
  242.4 0.8 select_bitcast_fusion.2
  243.2 1.3 slice_reduce_fusion
  244.5 1.7 copy.47
  246.2 1.7 fusion.8
  247.9 2.7 copy.48
  250.6 2.5 copy.49
  253.1 1.3 copy.50
  254.4 2.5 slice_convert_fusion
  256.9 1.1 convert_element_type.57
  258.0 0.8 convert_bitcast_fusion
  260.1 3.1 %copy.58 = f32[1,1024,512]{2,1,0:T(8,128)} copy(f32[1,1024,512]{2,1,0:T(8,128)} %bitcast.62) | data formatting | bytes 4194304
  (72 shorter events, 8.4 us)
Async XLA Ops:
  7.2 7.7 %copy-start.15 = (f32[8]{0:T(128)S(1)}, f32[8]{0:T(128)}, u32[]{:S(2)}) copy-start(f32[8]{0:T(128)} %param.27) | copy-start | bytes 100
  7.2 6.4 %copy-start.7 = (f32[8,256,64]{1,2,0:T(8,128)S(1)}, f32[8,256,64]{1,2,0:T(8,128)}, u32[]{:S(2)}) copy-start(f32[8,256,64]{1,2,0:T(8,128)} %param.30) | copy-start | bytes 1572868
  7.2 6.4 %copy-start.13 = (f32[8,256]{1,0:T(8,128)S(1)}, f32[8,256]{1,0:T(8,128)}, u32[]{:S(2)}) copy-start(f32[8,256]{1,0:T(8,128)} %param.31) | copy-start | bytes 24580
  7.2 61.8 %all-gather.6.cloned.1.call-start = ((), (), s32[]{:S(2)}) async-start(), calls=%async_computation | async-start | bytes 3145728 | tf_op jit(solution)/shard_map/all_gather | solution.py:720
  8.0 72.5 %all-gather.8.cloned.1.call-start = ((), (), s32[]{:S(2)}) async-start(), calls=%async_computation.1 | async-start | bytes 3145728 | tf_op jit(solution)/shard_map/all_gather | solution.py:721
  13.6 1.9 copy-start.1
  13.6 37.1 %copy-start.14 = (bf16[1024]{0:T(1024)(128)(2,1)S(1)}, bf16[1024]{0:T(1024)(128)(2,1)}, u32[]{:S(2)}) copy-start(bf16[1024]{0:T(1024)(128)(2,1)} %param.35) | copy-start | bytes 6148
  13.7 37.1 %copy-start.10 = (bf16[512,8]{0,1:T(8,128)(2,1)S(1)}, bf16[512,8]{0,1:T(8,128)(2,1)}, u32[]{:S(2)}) copy-start(bf16[512,8]{0,1:T(8,128)(2,1)} %param.26) | copy-start | bytes 24580
  45.6 23.4 %collective-permute-start = (bf16[8,80,256]{2,1,0:T(8,128)(2,1)}, bf16[8,80,256]{2,1,0:T(8,128)(2,1)S(1)}, u32[]{:S(2)}, u32[]{:S(2)}) collective-permute-start(bf16[8,80,256]{2,1,0:T(8,128)(2,1)} %get-tuple-element.55), channel_id=1, source_target_pairs={{0,1},{2,3},{4,5},{6,7},{8,9},{10,11},{12,13},{14,15},{16,17},{18,... | collective-permute-start | bytes 983048 | tf_op jit(solution)/shard_map/ppermute | solution.py:678
  69.0 11.5 %copy-start.4 = (bf16[8,80,256]{2,1,0:T(8,128)(2,1)}, bf16[8,80,256]{2,1,0:T(8,128)(2,1)S(1)}, u32[]{:S(2)}) copy-start(bf16[8,80,256]{2,1,0:T(8,128)(2,1)S(1)} %collective-permute-done.entry_ref.refs_11_) | copy-start | bytes 983044
  112.3 14.4 %collective-permute-start.1 = (bf16[8,80,256]{2,1,0:T(8,128)(2,1)}, bf16[8,80,256]{2,1,0:T(8,128)(2,1)S(1)}, u32[]{:S(2)}, u32[]{:S(2)}) collective-permute-start(bf16[8,80,256]{2,1,0:T(8,128)(2,1)} %get-tuple-element.62), channel_id=1, source_target_pairs={{1,0},{3,2},{5,4},{7,6},{9,8},{11,10},{13,12},{15,14},{17,16},{19,... | collective-permute-start | bytes 983048 | tf_op jit(solution)/shard_map/ppermute | solution.py:678
  113.8 5.3 %copy-start.16 = (bf16[1024,2048]{1,0:T(8,128)(2,1)S(1)}, bf16[1024,2048]{1,0:T(8,128)(2,1)}, u32[]{:S(2)}) copy-start(bf16[1024,2048]{1,0:T(8,128)(2,1)} %get-tuple-element.67) | copy-start | bytes 12582916
  118.8 1.2 copy-start.5
  122.7 2.3 copy-start.12
  122.7 2.3 copy-start.11
  122.7 2.4 copy-start.17
  122.7 2.5 copy-start.18
  125.0 1.8 copy-start.8
  126.7 1.6 copy-start.3
  247.9 5.2 %copy-start = (f32[1,512,2,256]{1,3,0,2:T(8,128)S(1)}, f32[1,512,2,256]{1,3,0,2:T(8,128)}, u32[]{:S(2)}) copy-start(f32[1,512,2,256]{1,3,0,2:T(8,128)} %get-tuple-element.116) | copy-start | bytes 3145732
  247.9 6.5 %copy-start.2 = (bf16[1024,1024]{1,0:T(8,128)(2,1)S(1)}, bf16[1024,1024]{1,0:T(8,128)(2,1)}, u32[]{:S(2)}) copy-start(bf16[1024,1024]{1,0:T(8,128)(2,1)} %get-tuple-element.79) | copy-start | bytes 6291460
  254.4 2.5 copy-start.6
  254.4 3.6 %copy-start.9 = (bf16[512,256]{1,0:T(8,128)(2,1)S(1)}, bf16[512,256]{1,0:T(8,128)(2,1)}, u32[]{:S(2)}) copy-start(bf16[512,256]{1,0:T(8,128)(2,1)} %get-tuple-element.77) | copy-start | bytes 786436
Sparse Core Ops, SparseCore 0:
  9.6 35.7 all-gather.5
  47.0 33.4 all-gather.7

commit v4 on v3

v4 whole, which is shorter than its diff:
```python
from functools import partial
import math

import jax
import jax.numpy as jnp
from jax import lax
from jax.experimental import pallas as pl
from jax.experimental.pallas import tpu as pltpu
from jax.sharding import PartitionSpec as P

F32 = jnp.float32
BF16 = jnp.bfloat16
EPS_NORM = 1e-05
EPS_UNIT = 1e-06
GUARD = 0.0625
MESH = pl.DeviceIdType.MESH
VMEM = 56 * 1024 * 1024

C = 128
T = 256
HB = 256
GROUP_HEADS = 4
LANES = 128

SIN = (3.14158202, -5.16714278, 2.54189892, -0.55463591)
COS = (0.99999995, -4.93479286, 4.05841191, -1.33188012, 0.21969671)
ERF = (0.319381530, -0.356563782, 1.781477937, -1.821255978, 1.330274429)
ERF_P = 0.2316419
INV_SQRT_2PI = 0.3989422804014327


def nn(a, b):
    return lax.dot_general(a, b, (((1,), (0,)), ((), ())), preferred_element_type=F32)


def nt(a, b):
    return lax.dot_general(a, b, (((1,), (1,)), ((), ())), preferred_element_type=F32)


def tn(a, b):
    return lax.dot_general(a, b, (((0,), (0,)), ((), ())), preferred_element_type=F32)


def thirds(x):
    high = x.astype(BF16)
    rest = x - high.astype(F32)
    middle = rest.astype(BF16)
    return high, middle, (rest - middle.astype(F32)).astype(BF16)


def rows_up_to(x):
    n = x.shape[0]
    tri = jnp.where(iota((n, n), 0) >= iota((n, n), 1), 1.0, 0.0).astype(BF16)
    return nn(jnp.concatenate([tri] * 3, axis=1), jnp.concatenate(thirds(x), axis=0))


def lanes_up_to(x):
    n = x.shape[1]
    tri = jnp.where(iota((n, n), 0) <= iota((n, n), 1), 1.0, 0.0).astype(BF16)
    return nn(jnp.concatenate(thirds(x), axis=1), jnp.concatenate([tri] * 3, axis=0))


def iota(shape, dim):
    return lax.broadcasted_iota(jnp.int32, shape, dim)


def log_sigmoid(x):
    return jnp.minimum(x, 0.0) - jnp.log(1.0 + jnp.exp(-jnp.abs(x)))


def normalize(x):
    centred = x - jnp.mean(x, axis=-1, keepdims=True)
    scale = lax.rsqrt(jnp.mean(centred * centred, axis=-1, keepdims=True) + EPS_NORM)
    return centred * scale, scale


def normalize_back(grad, gain, xhat, scale):
    inner = grad * gain
    mean_inner = jnp.mean(inner, axis=-1, keepdims=True)
    mean_both = jnp.mean(inner * xhat, axis=-1, keepdims=True)
    return scale * (inner - mean_inner - xhat * mean_both)


def fold_rows(x):
    return jnp.sum(x.reshape(x.shape[0] // 8, 8, x.shape[1]), axis=0)


def block_ones():
    return jnp.where(
        iota((LANES, LANES), 0) // 64 == iota((LANES, LANES), 1) // 64, 1.0, 0.0
    ).astype(BF16)


def head_sums(x):
    high = x.astype(BF16)
    rest = (x - high.astype(F32)).astype(BF16)
    ones = block_ones()
    return nn(jnp.concatenate([high, rest], axis=1), jnp.concatenate([ones, ones], axis=0))


def lower_half(shape):
    return iota(shape, 1) < 64


def mine(h, lower):
    return lower if h % 2 == 0 else jnp.logical_not(lower)


def column(block, index, rows, width):
    return jnp.broadcast_to(block[:, index : index + 1], (rows, width))


def sin_cos(turns, scale):
    r = turns - jnp.floor(turns + 0.5)
    r2 = r * r
    s = (((SIN[3] * r2 + SIN[2]) * r2 + SIN[1]) * r2 + SIN[0]) * r
    k = 2.0 * scale
    c = (((k * COS[4] * r2 + k * COS[3]) * r2 + k * COS[2]) * r2 + k * COS[1]) * r2 + k * COS[0]
    return s * c, scale - (k * s) * s


class Links:
    def __init__(self):
        self.dp, self.seq = lax.axis_index("dp"), lax.axis_index("seq")
        core, y, z = self.dp % 2, (self.dp // 2) % 2, self.dp // 4
        self.y = y
        self.at = {"core": core, "y": y, "z": z, "plane": self.seq * 2 + y}
        self.at["xr"] = 0

    size = {"core": 2, "xr": 2, "y": 2, "z": 4, "plane": 4}

    def partner(self, group, step):
        dp, seq = self.dp, self.seq
        if group == "core":
            return (dp + 1 - 2 * self.at["core"], seq)
        if group == "xr":
            return (dp, 1 - seq)
        if group == "y":
            return (dp + 2 - 4 * self.y, seq)
        target = (self.at[group] + step) % 4
        if group == "z":
            return (dp % 4 + 4 * target, seq)
        return (dp + 2 * (target % 2 - self.y), target // 2)

    def greet(self, groups):
        barrier = pltpu.get_barrier_semaphore()
        count = 0
        for group in groups:
            for step in range(1, self.size[group]):
                pl.semaphore_signal(
                    barrier, inc=1, device_id=self.partner(group, step), device_id_type=MESH
                )
                count += 1
        pl.semaphore_wait(barrier, count)


class Plan:
    def __init__(self, rows, lanes, dtype, scatter, gather, share=(), pre=()):
        self.pre = pre
        self.scatter, self.gather, self.share = scatter, gather, share
        self.rows, self.lanes, self.dtype = rows, lanes, dtype
        self.groups = scatter + gather + share
        self.left = rows
        for group in scatter:
            self.left //= Links.size[group]
        self.stages = len(self.groups)

    def scratch(self):
        shapes = []
        rows = self.rows
        for i, group in enumerate(self.scatter):
            n = Links.size[group]
            rows //= n
            shapes.append(pltpu.VMEM((n - 1, rows, self.lanes), self.dtype))
            if i < len(self.scatter) - 1:
                shapes.append(pltpu.VMEM((rows, self.lanes), self.dtype))
        for i, group in enumerate(self.share):
            shapes.append(pltpu.VMEM((Links.size[group], rows, self.lanes), self.dtype))
            if i < len(self.share) - 1:
                shapes.append(pltpu.VMEM((rows, self.lanes), self.dtype))
        for group in self.groups:
            n = Links.size[group]
            shapes.append(pltpu.SemaphoreType.DMA((n - 1,)))
            shapes.append(pltpu.SemaphoreType.DMA((n - 1,)))
        return shapes


class Stream:
    def __init__(self, plan, links, source, out, scratch):
        self.plan, self.links, self.source, self.out = plan, links, source, out
        scratch = list(scratch)
        self.landing, self.parts = [], [source]
        summed = plan.scatter + plan.share
        for i in range(len(summed)):
            self.landing.append(scratch.pop(0))
            if i < len(summed) - 1:
                self.parts.append(scratch.pop(0))
        self.sems = [(scratch.pop(0), scratch.pop(0)) for _ in range(plan.stages)]
        self.places = {}
        rows, start = out.shape[0], 0
        for group in plan.pre + plan.scatter:
            if group in plan.gather:
                rows //= Links.size[group]
                self.places[group] = (start, rows)
                start = start + links.at[group] * rows
        self.final = (start, rows)

    def copies(self, stage, sending):
        plan, links = self.plan, self.links
        group = plan.groups[stage]
        n, me = Links.size[group], links.at[group]
        sends, recvs = self.sems[stage]
        made = []
        for step in range(1, n):
            target, origin = (me + step) % n, (me + n - step) % n
            if plan.share:
                source = self.parts[stage]
                lands = self.landing[stage].at[me]
                arrives = self.landing[stage].at[origin]
            elif stage < len(plan.scatter):
                landing = self.landing[stage]
                rows = landing.shape[1]
                source = self.parts[stage].at[pl.ds(pl.multiple_of(target * rows, 8), rows)]
                arrives = lands = landing.at[step - 1]
            else:
                start, rows = self.places[group]
                mine_at = pl.multiple_of(start + me * rows, 8)
                theirs_at = pl.multiple_of(start + origin * rows, 8)
                source = lands = self.out.at[pl.ds(mine_at, rows)]
                arrives = self.out.at[pl.ds(theirs_at, rows)]
            made.append(
                pltpu.make_async_remote_copy(
                    src_ref=source if sending else arrives,
                    dst_ref=lands if sending else arrives,
                    send_sem=sends.at[step - 1],
                    recv_sem=recvs.at[step - 1],
                    device_id=links.partner(group, step),
                    device_id_type=MESH,
                )
            )
        return made

    def start(self, stage):
        if stage == 0 and not (self.plan.scatter or self.plan.share):
            start, rows = self.final
            self.out[pl.ds(pl.multiple_of(start, 8), rows), :] = self.source[...]
        for copy in self.copies(stage, True):
            copy.start()

    def finish(self, stage):
        plan = self.plan
        for copy in self.copies(stage, False):
            copy.wait_recv()
        if plan.share:
            landing, me = self.landing[stage], self.links.at[plan.groups[stage]]
            landing[me] = self.parts[stage][...]
            total = landing[0]
            for k in range(1, landing.shape[0]):
                total = total + landing[k]
            if stage + 1 < plan.stages:
                self.parts[stage + 1][...] = total
            else:
                self.out[...] = total
            return
        if stage >= len(plan.scatter):
            return
        landing = self.landing[stage]
        arrivals, rows, _ = landing.shape
        own = pl.multiple_of(self.links.at[plan.groups[stage]] * rows, 8)
        total = self.parts[stage][pl.ds(own, rows), :].astype(F32)
        for step in range(arrivals):
            total = total + landing[step].astype(F32)
        total = total.astype(landing.dtype)
        if stage + 1 < len(plan.scatter):
            self.parts[stage + 1][...] = total
        else:
            start, rows = self.final
            self.out[pl.ds(pl.multiple_of(start, 8), rows), :] = total

    def drain(self):
        for stage in range(self.plan.stages):
            for copy in self.copies(stage, True):
                copy.wait_send()


ALL_PLAN = (("core", "plane", "z"), ("z", "plane", "core"))
SHARE_PLAN = ((), (), ("core", "plane", "z"))


def pick_row(block, index):
    return jnp.sum(jnp.where(iota(block.shape, 0) == index, block, 0.0), axis=0, keepdims=True)


def grow_state(rows, norm, h):
    rows = rows.astype(F32)
    norm = jnp.broadcast_to(norm, rows.shape)
    return jnp.concatenate([rows, norm] if h % 2 == 0 else [norm, rows], axis=0)


def state_part(state, h):
    return state[0:64] if h % 2 == 0 else state[64:128]


def norm_part(state, h):
    return state[64:65] if h % 2 == 0 else state[0:1]


def pack_states(states, out_ref):
    heads = len(states)
    for h, state in enumerate(states):
        out_ref[64 * h : 64 * (h + 1), :] = state_part(state, h).astype(BF16)
    norms = [norm_part(state, h) for h, state in enumerate(states)]
    pad = jnp.zeros((16 - heads, states[0].shape[1]), F32)
    out_ref[64 * heads : 64 * heads + 16, :] = jnp.concatenate(norms + [pad], axis=0).astype(BF16)


def projection_blocks(proj_ref, p, scale):
    parts = [proj_ref[2 * p + j] * scale for j in range(2)]
    highs = [part.astype(BF16) for part in parts]
    rests = [(part - high.astype(F32)).astype(BF16) for part, high in zip(parts, highs)]
    zero = jnp.zeros(highs[0].shape, BF16)

    def diagonal(pair):
        return jnp.concatenate(
            [
                jnp.concatenate([pair[0], zero], axis=1),
                jnp.concatenate([zero, pair[1]], axis=1),
            ],
            axis=0,
        )

    return diagonal(highs), diagonal(rests)


def gate_rows(wg):
    eye = jnp.where(iota((16, wg.shape[1]), 0) == iota((16, wg.shape[1]), 1), 1.0, 0.0)
    return nt(eye.astype(BF16), wg).astype(BF16)


class Taker:
    def __init__(self, refs):
        self.refs = list(refs)

    def __call__(self, n):
        taken = self.refs[:n]
        del self.refs[:n]
        return taken


class Board:
    def __init__(self, links, take, store_sems):
        self.links, self.take, self.store_sems = links, take, store_sems
        self.entries = []

    def add(self, plan, source, out, final, ticks):
        stream = Stream(plan, self.links, source, out, self.take(len(plan.scratch())))
        self.entries.append((stream, ticks, out, final))

    def store(self, k):
        _, _, out, final = self.entries[k]
        return pltpu.make_async_copy(out, final, self.store_sems.at[k])

    def advance(self, now):
        for k, (stream, ticks, _, final) in enumerate(self.entries):
            for stage, tick in enumerate(ticks):
                if tick == now:
                    if stage > 0:
                        stream.finish(stage - 1)
                    if stage < stream.plan.stages:
                        stream.start(stage)
                    elif final is not None:
                        self.store(k).start()

    def last(self):
        return max(ticks[-1] for _, ticks, _, _ in self.entries)

    def drain(self):
        for k, (stream, _, _, final) in enumerate(self.entries):
            stream.drain()
            if final is not None:
                self.store(k).wait()


def features_kernel(heads, chunks, comm, *refs):
    take = Taker(refs)
    x_ref, gain_ref, bias_ref, wq_ref, wk_ref, wv_ref = take(6)
    gate_ref, gb_smem, proj_ref, start_ref, start_norm_ref = take(5)
    up_hbm, down_hbm, upb_ref = take(3) if comm else (None,) * 3
    ml_ref, uq_ref, uk_ref, rq_ref, rk_ref, qf_ref, kf_ref, v_ref = take(8)
    gcol_ref, grow_ref, before_ref, n_ref = take(4)
    if comm:
        entry_ref, upo_hbm, downo_hbm, upbs_ref = take(4)
    else:
        final_ref, total_ref = take(2)
    state, carry, qf_s, kf_s, v_s, gcol_s, grow_s, before_s = take(8)
    wg_ref, wgt_ref, gb_ref, gbt_ref, pcat_ref = take(5)
    step = pl.program_id(0)
    chunk = lax.rem(step, chunks)

    if comm:
        sent, landed, upb_landed, sends, recvs = take(5)
        links = Links()
        core = links.at["core"]
        half = up_hbm.shape[0] // 2
        own_rows = pl.ds(pl.multiple_of(core * half, 16), half)
        other_rows = pl.ds(pl.multiple_of((1 - core) * half, 16), half)

        def remote(k, sending):
            group = "core" if k >= 4 else "xr"
            if k == 2:
                source, lands = upb_ref, upb_landed
            elif k == 3:
                source, lands = sent, landed
            else:
                into = (upo_hbm, downo_hbm)[k % 2].at[own_rows]
                source, lands = (up_hbm, down_hbm)[k % 2].at[own_rows], into
                if k >= 4:
                    source = into
                    if not sending:
                        lands = (upo_hbm, downo_hbm)[k % 2].at[other_rows]
            return pltpu.make_async_remote_copy(
                src_ref=source if sending else lands,
                dst_ref=lands,
                send_sem=sends.at[k],
                recv_sem=recvs.at[k],
                device_id=links.partner(group, 1),
                device_id_type=MESH,
            )

        @pl.when(step == 0)
        def _():
            links.greet(("core", "xr"))
            for k in (0, 1, 2):
                remote(k, True).start()

        @pl.when(step == chunks)
        def _():
            remote(3, True).start()

        @pl.when(step == chunks + chunks // 2)
        def _():
            for k in (0, 1):
                remote(k, False).wait_recv()
                remote(k + 4, True).start()

    @pl.when(step == 0)
    def _():
        carry[...] = jnp.zeros_like(carry)
        is_first = lax.axis_index("seq") == 0
        wg = gate_ref[...]
        spread = jnp.where(iota((heads, LANES), 0) == iota((heads, LANES), 1) % heads, 1.0, 0.0)
        wg_ref[...] = nn(wg, spread.astype(BF16)).astype(BF16)
        wgt_ref[...] = gate_rows(wg)[0:heads]
        lane_head = iota((1, LANES), 1) % heads
        row_head = iota((heads, LANES), 0)
        gb = jnp.zeros((1, LANES), F32)
        gbt = jnp.zeros((heads, LANES), F32)
        for h in range(heads):
            gb = jnp.where(lane_head == h, gb_smem[h], gb)
            gbt = jnp.where(row_head == h, gb_smem[h], gbt)
            begin = start_ref[h].T
            norm = jnp.broadcast_to(start_norm_ref[h : h + 1, :], begin.shape)
            both = [begin, norm] if h % 2 == 0 else [norm, begin]
            state[h] = jnp.where(is_first, jnp.concatenate(both, axis=0), 0.0)
        gb_ref[...] = gb
        gbt_ref[...] = gbt
        for p in range(heads // 2):
            high, rest = projection_blocks(proj_ref, p, 1.0 / (2.0 * math.pi))
            pcat_ref[p, 0:LANES, :] = high
            pcat_ref[p, LANES : 2 * LANES, :] = high
            pcat_ref[p, 2 * LANES : 3 * LANES, :] = rest

    lower = lower_half((C, LANES))

    @pl.when(step < chunks)
    def _():
        xhat, _ = normalize(x_ref[...].astype(F32))
        ml = (xhat * gain_ref[...] + bias_ref[...]).astype(BF16)
        ml_ref[...] = ml
        q = nn(ml, wq_ref[...])
        k = nn(ml, wk_ref[...])
        v = nn(ml, wv_ref[...])
        v_low = v.astype(BF16)
        v_ref[...] = v_low
        v_s[chunk] = v_low
        logit = nn(ml, wg_ref[...]) + gb_ref[...]
        keep = log_sigmoid(logit)
        gain_in = keep - logit
        decay = rows_up_to(keep)
        total = decay[C - 1 : C, :]
        group = iota((C, LANES), 1) // 8
        coef = total - decay + gain_in
        packed = jnp.where(group == 0, decay, coef)
        packed = jnp.where(group == 2, carry[...] + decay, packed)
        packed = jnp.where(group == 6, jnp.broadcast_to(carry[...], (C, LANES)), packed)
        packed = jnp.where(group == 7, jnp.broadcast_to(total, (C, LANES)), packed)
        gcol_ref[...] = packed
        gcol_s[chunk] = packed
        carry[...] = carry[...] + total
        if not comm:
            total_ref[...] = jnp.broadcast_to(carry[...], total_ref.shape)
        logit_row = nt(wgt_ref[...], ml) + gbt_ref[...][:, 0:1]
        keep_row = log_sigmoid(logit_row)
        decay_row = lanes_up_to(keep_row)
        rows = jnp.concatenate(
            [
                keep_row - logit_row - decay_row,
                decay_row,
                jax.nn.sigmoid(logit_row),
                jax.nn.sigmoid(-logit_row),
            ],
            axis=0,
        )
        grow_ref[...] = rows
        grow_s[chunk] = rows

        ftr_scale = 1.0 / math.sqrt(LANES)
        for p in range(heads // 2):
            lanes = slice(LANES * p, LANES * (p + 1))
            both = jnp.concatenate([q[:, lanes], k[:, lanes]], axis=0)
            scale = lax.rsqrt(head_sums(both * both) + EPS_UNIT)
            unit = both * scale
            high = unit.astype(BF16)
            rest = (unit - high.astype(F32)).astype(BF16)
            uq_ref[:, lanes] = high[:C]
            uk_ref[:, lanes] = high[C:]
            rq_ref[:, lanes] = scale[:C]
            rk_ref[:, lanes] = scale[C:]
            turns = nn(jnp.concatenate([high, rest, high], axis=1), pcat_ref[p])
            s, c = sin_cos(turns, ftr_scale)
            s = s.astype(BF16)
            c = c.astype(BF16)
            for j in range(2):
                h = 2 * p + j
                half_lanes = slice(LANES * j, LANES * (j + 1))
                feats = jnp.concatenate([s[:, half_lanes], c[:, half_lanes]], axis=1)
                place = slice(256 * h, 256 * (h + 1))
                qf_ref[:, place] = feats[:C]
                qf_s[chunk, :, place] = feats[:C]
                kf = feats[C:]
                kf_ref[:, place] = kf
                kf_s[chunk, :, place] = kf
                values = jnp.where(mine(h, lower), v[:, lanes], 1.0)
                weighted = (values * jnp.exp(column(coef, h, C, LANES))).astype(BF16)
                now = state[h]
                now_low = now.astype(BF16)
                before_ref[0, h] = now_low
                before_s[chunk, h] = now_low
                state[h] = jnp.exp(total[:, h : h + 1]) * now + tn(weighted, kf)

    @pl.when(step == chunks - 1)
    def _():
        pack_states([state[h] for h in range(heads)], sent if comm else final_ref)

    @pl.when(step >= chunks)
    def _():
        causal = iota((C, C), 0) >= iota((C, C), 1)
        gcol = gcol_s[chunk]
        for h in range(heads):
            qf = qf_s[chunk, :, 256 * h : 256 * (h + 1)]
            kf = kf_s[chunk, :, 256 * h : 256 * (h + 1)]
            p = h // 2
            v = v_s[chunk, :, LANES * p : LANES * (p + 1)].astype(F32)
            values = jnp.where(mine(h, lower), v, 1.0).astype(BF16)
            decay = column(gcol, h, C, LANES)
            pairs = jnp.where(causal, jnp.exp(decay + grow_s[chunk, h : h + 1, :]), 0.0)
            both = nt(qf, jnp.concatenate([kf, before_s[chunk, h]], axis=0))
            weights = (both[:, :C] * pairs).astype(BF16)
            n_ref[:, LANES * h : LANES * (h + 1)] = (
                nn(weights, values) + jnp.exp(decay) * both[:, C:]
            )

    if comm:
        @pl.when(step == 2 * chunks - 1)
        def _():
            for k in (2, 3, 4, 5):
                remote(k, False).wait_recv()
            later = links.seq == 1
            entry_ref[...] = jnp.where(later, landed[...].astype(F32), 0.0).astype(BF16)
            upbs_ref[0:1, :] = upb_ref[...]
            upbs_ref[1:2, :] = upb_landed[...]
            for k in range(6):
                remote(k, True).wait_send()


def feed_kernel(heads, tiles, pairs, comm, *refs):
    take = Taker(refs)
    x_ref, qf_hbm, n_ref, gcol_ref, entry_ref, wo_ref = take(6)
    gain_ref, bias_ref, downb_ref, upb_ref, dout_hbm = take(5)
    weights_hbm = take(4 if comm else 2)
    out_ref, mg_ref, a_ref = take(3)
    if comm:
        usum_hbm, *late_refs = take(1 + len(FEED_STAGES) - 1)
        os_ref, flat_ref, after_ref = take(3)
    else:
        upg_ref, downg_ref, upbg_ref, o_ref, final_ref, sums_out = take(6)
    entry, adj, middle_s, num_s, den_s, fl_s, mix_s, br_s = take(8)
    acc_s, fg_s, dout_s, up_s, down_s, hid_s, pre_s, sums_s, load_sems = take(9)
    step = pl.program_id(0)
    tokens, width = middle_s.shape
    rows = x_ref.shape[0]
    shards, _, shard_width = up_s.shape
    hb = hid_s.shape[1] // 2
    (qf_s,) = take(1)
    loads = [
        (qf_hbm.at[pl.ds(rows * t, rows)], qf_s.at[pl.ds(rows * t, rows)]) for t in range(tiles)
    ]
    loads += [(dout_hbm, dout_s)]
    if comm:
        up_own, up_other, down_own, down_other = weights_hbm
        loads += [(up_own, up_s.at[0]), (up_other, up_s.at[1])]
        loads += [(down_own, down_s.at[0]), (down_other, down_s.at[1])]
        u_src, usum_s, upbg_s, sent, landed, sends, recvs, store_sems = take(8)
        links = Links()
        board = Board(links, take, store_sems)
        for j, (plan, ticks) in enumerate(zip(feed_plans(hb), FEED_TICKS)):
            if j == 0:
                board.add(plan, u_src.at[j], usum_s, usum_hbm, ticks)
            else:
                board.add(plan, u_src.at[j], late_refs[j - 1], None, ticks)

        def exchange():
            return pltpu.make_async_remote_copy(
                src_ref=sent,
                dst_ref=landed,
                send_sem=sends,
                recv_sem=recvs,
                device_id=links.partner("xr", 1),
                device_id_type=MESH,
            )
    else:
        upbg_s = upbg_ref
        loads += [(weights_hbm[0], up_s), (weights_hbm[1], down_s)]

    def load(k):
        return pltpu.make_async_copy(loads[k][0], loads[k][1], load_sems.at[k])

    @pl.when(step == 0)
    def _():
        for k in range(len(loads)):
            load(k).start()
        adj[...] = jnp.zeros_like(adj)
        sums_s[...] = jnp.zeros_like(sums_s)
        norms = entry_ref[64 * heads : 64 * heads + 16, :].astype(F32)
        for h in range(heads):
            grown = grow_state(entry_ref[64 * h : 64 * (h + 1), :], norms[h : h + 1], h)
            entry[h] = grown.astype(BF16)
        if comm:
            links.greet(("core", "xr", "y", "z"))

    lower = lower_half((rows, LANES))

    @pl.when(step < tiles)
    def _():
        for t in range(tiles):
            pl.when(step == t)(load(t).wait)
        here = pl.ds(pl.multiple_of(step * rows, rows), rows)
        gcol = gcol_ref[...]
        mixed = []
        for p in range(heads // 2):
            lanes = slice(LANES * p, LANES * (p + 1))
            both = []
            for h in (2 * p, 2 * p + 1):
                far = nt(qf_s[here, 256 * h : 256 * (h + 1)], entry[h])
                far = far * jnp.exp(column(gcol, 16 + h, rows, LANES))
                both.append(n_ref[:, LANES * h : LANES * (h + 1)] + far)
            num = jnp.where(lower, both[0], both[1])
            den = pltpu.roll(jnp.where(lower, both[1], both[0]), 64, 1)
            num_s[here, lanes] = num
            den_s[here, lanes] = den
            mixed.append(num * lax.rsqrt(den * den + GUARD))
        mixed = jnp.concatenate(mixed, axis=1).astype(BF16)
        mix_s[here, :] = mixed
        middle = x_ref[...].astype(F32) + nn(mixed, wo_ref[...])
        middle_s[here, :] = middle
        acc_s[here, :] = middle + downb_ref[...]
        fg_s[here, :] = jnp.zeros_like(middle)
        xhat, _ = normalize(middle)
        fl_s[here, :] = (xhat * gain_ref[...] + bias_ref[...]).astype(BF16)

    @pl.when(step == tiles)
    def _():
        for k in range(tiles, len(loads)):
            load(k).wait()

    @pl.when(jnp.logical_and(step >= tiles, step < tiles + pairs))
    def _():
        j = step - tiles
        blocks = []
        for s in range(2):
            if comm:
                shard, off = s, pl.multiple_of(j * hb, hb)
            else:
                at = (2 * j + s) * hb
                shard, off = at // shard_width, pl.multiple_of(at % shard_width, hb)
            blocks.append((shard, pl.ds(off, hb)))
        ups = [up_s[shard, :, cols] for shard, cols in blocks]
        downs = [down_s[shard, :, cols] for shard, cols in blocks]
        up = jnp.concatenate(ups, axis=1)
        down = jnp.concatenate(downs, axis=1)
        if comm:
            upb = jnp.concatenate(
                [upb_ref[s : s + 1, cols] for s, (_, cols) in enumerate(blocks)], axis=1
            )
        else:
            upb = jnp.concatenate([upb_ref[shard, :, cols] for shard, cols in blocks], axis=1)
        for r in range(tokens // rows):
            if comm and r % 2 == 0:
                for k in range(pairs):
                    pl.when(j == k)(partial(board.advance, 2 * k + r // 2))
            here = slice(rows * r, rows * (r + 1))
            feed_low = fl_s[here, :]
            pre = nn(feed_low, up) + upb
            pre_grad = nn(dout_s[here, :], down)
            t = 1.0 / (1.0 + ERF_P * jnp.abs(pre))
            bell = INV_SQRT_2PI * jnp.exp(-0.5 * pre * pre)
            tail = ((((ERF[4] * t + ERF[3]) * t + ERF[2]) * t + ERF[1]) * t + ERF[0]) * t * bell
            phi = jnp.where(pre >= 0.0, 1.0 - tail, tail)
            hidden = (pre * phi).astype(BF16)
            pre_low = (pre_grad * (phi + pre * bell)).astype(BF16)
            hid_s[here, :] = hidden
            pre_s[here, :] = pre_low
            acc_s[here, :] += nt(hidden, down)
            fg_s[here, :] += nt(pre_low, up)
        up_grad = tn(fl_s[...], pre_s[...]).astype(BF16)
        down_grad = tn(dout_s[...], hid_s[...]).astype(BF16)
        bias_grad = nn(jnp.ones((16, tokens), BF16), pre_s[...])[0:1]
        for s, (shard, cols) in enumerate(blocks):
            part = slice(hb * s, hb * (s + 1))
            upbg_s[shard, :, cols] = bias_grad[:, part]
            if comm:
                u_src[j, width * s : width * (s + 1), :] = up_grad[:, part]
                u_src[j, width * (2 + s) : width * (3 + s), :] = down_grad[:, part]
            else:
                upg_ref[shard, :, cols] = up_grad[:, part]
                downg_ref[shard, :, cols] = down_grad[:, part]

    @pl.when(step >= tiles + pairs)
    def _():
        tile = step - tiles - pairs

        if comm:
            for t in range(tiles):
                pl.when(tile == t)(partial(board.advance, 2 * pairs + t))
        here = pl.ds(pl.multiple_of(tile * rows, rows), rows)
        gcol = gcol_ref[...]
        dout = dout_s[here, :].astype(F32)
        out_ref[...] = acc_s[here, :].astype(BF16)
        feed_grad = fg_s[here, :]
        xhat, scale = normalize(middle_s[here, :])
        sums_s[0:8, :] += fold_rows(feed_grad * xhat)
        sums_s[8:16, :] += fold_rows(feed_grad)
        sums_s[16:24, :] += fold_rows(dout)
        middle_grad = dout + normalize_back(feed_grad, gain_ref[...], xhat, scale)
        mg_ref[...] = middle_grad
        branch = middle_grad.astype(BF16)
        br_s[here, :] = branch
        mixed_grad = nt(branch, wo_ref[...])
        for p in range(heads // 2):
            lanes = slice(LANES * p, LANES * (p + 1))
            num, den = num_s[here, lanes], den_s[here, lanes]
            inv = lax.rsqrt(den * den + GUARD)
            mg = mixed_grad[:, lanes]
            b = head_sums(mg * num) * den * (inv * inv * inv) * (-1.0 / 64)
            b = pltpu.roll(b, 64, 1)
            for h in (2 * p, 2 * p + 1):
                a = jnp.where(mine(h, lower), mg * inv, b)
                a_ref[:, LANES * h : LANES * (h + 1)] = a.astype(BF16)
                lifted = (a * jnp.exp(column(gcol, 16 + h, rows, LANES))).astype(BF16)
                adj[h] += tn(lifted, qf_s[here, 256 * h : 256 * (h + 1)])

    @pl.when(step == 2 * tiles + pairs - 1)
    def _():
        pack_states([adj[h] for h in range(heads)], sent if comm else final_ref)
        if comm:
            exchange().start()
        output_grad = tn(mix_s[...], br_s[...]).astype(BF16)
        if not comm:
            o_ref[...] = output_grad
            sums_out[...] = sums_s[...]
            return
        os_ref[:, 0:width] = output_grad
        for later in range(2 * pairs + tiles, board.last() + 1):
            board.advance(later)
        exchange().wait_recv()
        is_first = links.seq == 0
        after_ref[...] = jnp.where(is_first, landed[...].astype(F32), 0.0).astype(BF16)
        logs = gcol_ref[rows - 1 : rows, :]
        norms = landed[64 * heads : 64 * heads + 16, :].astype(F32)
        flat_ref[...] = jnp.zeros_like(flat_ref)
        for k in range(3):
            flat_ref[k : k + 1, :] = jnp.sum(sums_s[8 * k : 8 * (k + 1), :], axis=0, keepdims=True)
        for k in range(2 * shard_width // width):
            cols = slice(width * k % shard_width, width * k % shard_width + width)
            in_first = k < shard_width // width
            own, other = upbg_s[0, :, cols], upbg_s[1, :, cols]
            flat_ref[3 + k : 4 + k, :] = jnp.where(is_first, own, other) if in_first else jnp.where(
                is_first, other, own
            )
        for h in range(heads):
            grown = grow_state(landed[64 * h : 64 * (h + 1), :], norms[h : h + 1], h)
            begin = adj[h] + jnp.exp(logs[:, 16 + h : 17 + h]) * grown
            begin = jnp.where(is_first, begin, 0.0)
            os_ref[64 * h : 64 * (h + 1), width : width + 256] = state_part(begin, h).astype(BF16)
            flat_ref[8 + h : 9 + h, 0:256] = 64.0 * norm_part(begin, h)
        exchange().wait_send()
        board.drain()


U_SCATTER, U_GATHER = ("core", "xr", "y", "z"), ("z", "y", "core")
FEED_STAGES = (7, 4, 3, 2)
FEED_TICKS = ((2, 3, 5, 7, 8, 9, 11, 12), (4, 5, 8, 10, 12), (6, 7, 10, 12), (8, 9, 13))
BACK_TICKS = ((2, 4, 6, 8), (1, 3, 5, 7, 9), (1, 3, 5, 7, 9, 11))


def feed_plans(hb):
    return [
        Plan(2048, hb, BF16, U_SCATTER[:n], U_GATHER if n > 4 else ()) for n in FEED_STAGES
    ]


def late_plans(hb):
    plans = []
    for plan, n in zip(feed_plans(hb)[1:], FEED_STAGES[1:]):
        done = [group for group in U_SCATTER[:n] if group != "xr"]
        plans.append(Plan(plan.left, hb, BF16, U_SCATTER[n:], U_GATHER, pre=tuple(done)))
    return plans


def back_kernel(heads, hg, chunks, comm, *refs):
    take = Taker(refs)
    (qf_ref, kf_ref, v_ref, uq_ref, uk_ref, rq_ref, rk_ref, a_ref, gcol_ref, grow_ref) = take(10)
    before_ref, entry_ref, entry_norm, after_ref, after_norm, proj_in = take(6)
    x_hbm, mg_hbm, ml_hbm, wq_hbm, wk_hbm, wv_hbm, gate_ref, gain_ref = take(8)
    u_hbms = take(3) if comm else ()
    os_hbm, f_hbm = take(2) if comm else (None,) * 2
    dx_ref, w_ref, small_ref = take(3)
    usum_hbm, ossum_hbm, fsum_hbm = take(3) if comm else (None,) * 3
    adj_ref, dqkv, dlogit, x_ref, mg_ref, ml_ref, wq_ref, wk_ref, wv_ref, load_sems = take(10)
    (proj_ref,) = take(1)
    g, i = pl.program_id(0), pl.program_id(1)
    tick = g * chunks + i
    last = heads // hg * chunks - 1
    chunk = chunks - 1 - i
    here = pl.ds(pl.multiple_of(chunk * C, C), C)
    groups = heads // hg
    loads = [
        (x_hbm, x_ref),
        (mg_hbm, mg_ref),
        (ml_hbm, ml_ref),
        (wq_hbm, wq_ref),
        (wk_hbm, wk_ref),
        (wv_hbm, wv_ref),
    ]
    if comm:
        u_refs = take(3)
        os_ref, f_ref, w_src, small_src = take(4)
        usum_ref, ossum_ref, fsum_ref, wsum_ref, smallsum_ref = take(5)
        (store_sems,) = take(1)
        loads = list(zip(u_hbms, u_refs)) + [(os_hbm, os_ref), (f_hbm, f_ref)] + loads
        early_loads = len(loads) - 6
        links = Links()
        board = Board(links, take, store_sems)
        plans = back_plans(os_hbm.shape, f_hbm.shape, w_src.shape, small_src.shape)

        def stages(start, gaps):
            ticks = [start]
            for gap in gaps:
                ticks.append(ticks[-1] + gap)
            return ticks

        for j, (plan, ticks) in enumerate(zip(late_plans(usum_ref.shape[2]), BACK_TICKS)):
            board.add(plan, u_refs[j], usum_ref.at[j], usum_hbm.at[j], ticks)
        board.add(plans["os"], os_ref, ossum_ref, ossum_hbm, OS_TICKS)
        board.add(plans["f"], f_ref, fsum_ref, fsum_hbm, F_TICKS)
        for k in range(groups):
            final = k + 1 == groups
            pieces = W_PIECES if final else 1
            lanes_each = w_src.shape[2] // pieces
            for j in range(pieces):
                lanes = pl.ds(j * lanes_each, lanes_each)
                board.add(
                    plans["w_last" if final else "w"],
                    w_src.at[k, :, lanes],
                    wsum_ref.at[k, :, lanes],
                    w_ref.at[k, :, lanes],
                    [last + 1 + i + (j if i else 0) for i in range(7)] if final else W_TICKS,
                )
        advance = board.advance

    def load(k):
        return pltpu.make_async_copy(loads[k][0], loads[k][1], load_sems.at[k])

    @pl.when(tick == 0)
    def _():
        for k in range(len(loads)):
            load(k).start()
        dlogit[...] = jnp.zeros_like(dlogit)
        if comm:
            links.greet(("core", "plane", "z"))

    if comm:
        @pl.when(tick == 1)
        def _():
            for k in range(early_loads):
                load(k).wait()

        for now in range(1, last + 1):
            pl.when(tick == now)(partial(advance, now))

    @pl.when(i == 0)
    def _():
        for p in range(hg // 2):
            proj_ref[p] = projection_blocks(proj_in, p, 1.0 / (2.0 * math.pi))[0]
        norms = after_norm[...].astype(F32)
        for h in range(hg):
            norm = pick_row(norms, g * hg + h)
            adj_ref[h] = grow_state(after_ref[64 * h : 64 * (h + 1), :], norm, h)

    row = iota((C, C), 0)
    col = iota((C, C), 1)
    causal = row >= col
    one = jnp.ones((C, C), BF16)
    zero = jnp.zeros((C, C), BF16)
    later = jnp.where(row < col, 1.0, 0.0).astype(BF16)
    pair_sums = jnp.concatenate([later, one], axis=0)
    two_sums = jnp.concatenate(
        [jnp.concatenate([one, zero], axis=1), jnp.concatenate([zero, one], axis=1)], axis=0
    )
    lower = lower_half((C, LANES))
    entry_norms = entry_norm[...].astype(F32)
    gcol = gcol_ref[...]
    if groups > 1:
        gcol = jnp.where(g == 0, gcol, pltpu.roll(gcol, LANES - hg, 1))

    def grow_row(kind, h):
        return grow_ref[pl.ds(kind * heads + g * hg + h, 1), :]

    for p in range(hg // 2):
        lanes = slice(LANES * p, LANES * (p + 1))
        angle_q, angle_k, dvs, x_parts, y_parts, throughs = [], [], [], [], [], []
        v_pair = v_ref[:, lanes].astype(F32)
        values = [jnp.where(mine(h, lower), v_pair, 1.0) for h in range(2)]
        values_low = [part.astype(BF16) for part in values]
        dweights = nt(
            a_ref[:, 2 * LANES * p : 2 * LANES * (p + 1)],
            jnp.concatenate(
                [
                    jnp.concatenate([values_low[0], zero], axis=1),
                    jnp.concatenate([zero, values_low[1]], axis=1),
                ],
                axis=0,
            ),
        )
        for j in range(2):
            h = 2 * p + j
            qf = qf_ref[:, 256 * h : 256 * (h + 1)]
            kf = kf_ref[:, 256 * h : 256 * (h + 1)]
            a_low = a_ref[:, LANES * h : LANES * (h + 1)]
            a = a_low.astype(F32)
            decay = column(gcol, h, C, LANES)
            lift = jnp.exp(decay)
            coef = jnp.exp(column(gcol, 8 + h, C, LANES))
            carried = jnp.exp(gcol[0:1, 48 + h : 49 + h])
            total = jnp.exp(gcol[0:1, 56 + h : 57 + h])
            entry = grow_state(
                entry_ref[64 * h : 64 * (h + 1), :], pick_row(entry_norms, g * hg + h), h
            )
            before = before_ref[0, h].astype(F32) + carried * entry
            before_low = before.astype(BF16)
            adj = adj_ref[h]
            adj_low = adj.astype(BF16)
            kept = total * adj
            through = jnp.sum(kept * before, axis=0, keepdims=True)
            throughs.append(jnp.sum(through, axis=1, keepdims=True))
            pairs = jnp.where(causal, jnp.exp(decay + grow_row(0, h)), 0.0)
            keys_and_state = jnp.concatenate([kf, before_low], axis=0)
            raw_and_far = nt(qf, keys_and_state)
            raw = raw_and_far[:, :C]
            weights = (raw * pairs).astype(BF16)
            draw = dweights[:, C * j : C * (j + 1)].astype(BF16).astype(F32) * pairs
            draw_low = draw.astype(BF16)
            both = (raw * draw).astype(BF16)
            a_lift = (a * lift).astype(BF16)
            v_coef = (values[j] * coef).astype(BF16)
            dq = nn(jnp.concatenate([draw_low, a_lift], axis=1), keys_and_state)
            dk = nn(
                jnp.concatenate([draw_low.T, v_coef], axis=1),
                jnp.concatenate([qf, adj_low], axis=0),
            )
            dv_far = coef * nt(kf, adj_low)
            dv = tn(weights, a_low) + dv_far
            x_far = (a * lift * raw_and_far[:, C:]).astype(BF16)
            x_parts.append(jnp.concatenate([both, x_far], axis=1))
            y_parts.append(
                jnp.concatenate(
                    [(values[j] * dv_far).astype(BF16), (values[j] * dv).astype(BF16)], axis=1
                )
            )
            adj_ref[h] = kept + tn(a_lift, qf)
            for feats, grad, angle in ((qf, dq, angle_q), (kf, dk, angle_k)):
                f = feats.astype(F32)
                angle.append(grad[:, :LANES] * f[:, LANES:] - grad[:, LANES:] * f[:, :LANES])
            dvs.append(dv)
        upto = nn(jnp.concatenate(x_parts, axis=0), pair_sums)
        ends = nn(jnp.concatenate(y_parts, axis=0), two_sums)
        for j in range(2):
            h = 2 * p + j
            rows = slice(C * j, C * (j + 1))
            flow = jnp.where(causal, upto[rows], ends[rows, :C])
            flow = jnp.sum(flow, axis=0, keepdims=True) + throughs[j]
            own = jnp.sum(jnp.where(row == col, ends[rows, C:], 0.0), axis=0, keepdims=True)
            dlogit[g, h : h + 1, here] = grow_row(3, h) * flow - grow_row(2, h) * own
        angles = jnp.concatenate(
            [jnp.concatenate(angle_q, axis=1), jnp.concatenate(angle_k, axis=1)], axis=0
        )
        du = nt(angles.astype(BF16), proj_ref[p])
        u = jnp.concatenate([uq_ref[:, lanes], uk_ref[:, lanes]], axis=0).astype(F32)
        scale = jnp.concatenate([rq_ref[:, lanes], rk_ref[:, lanes]], axis=0)
        along = nn((u * du).astype(BF16), block_ones())
        dqk = ((2.0 * math.pi) * scale * (du - u * along)).astype(BF16)
        width = hg * 64
        dqkv[g, here, LANES * p : LANES * (p + 1)] = dqk[:C]
        dqkv[g, here, width + LANES * p : width + LANES * (p + 1)] = dqk[C:]
        dqkv[g, here, 2 * width + LANES * p : 2 * width + LANES * (p + 1)] = jnp.where(
            lower, dvs[0], dvs[1]
        ).astype(BF16)

    @pl.when(i == chunks - 1)
    def _():
        @pl.when(g == 0)
        def _():
            load(len(loads) - 4).wait()

        grads = tn(ml_ref[...], dqkv[g]).astype(BF16)
        if comm:
            w_src[g] = grads
        else:
            w_ref[g] = grads

    @pl.when(tick == last)
    def _():
        if comm:
            advance(last + 1)
        for k in range(len(loads) - 6, len(loads)):
            if k != len(loads) - 4:
                load(k).wait()
        tokens = chunks * C
        block = min(T, tokens)
        small = small_src if comm else small_ref
        rows8 = jnp.concatenate(
            [dlogit[k, 0:hg, :] for k in range(groups)]
            + [jnp.zeros((16 - heads, dlogit.shape[2]), F32)],
            axis=0,
        ).astype(BF16)
        small[...] = jnp.zeros_like(small)
        small[0:heads, :] = nn(rows8, ml_ref[...])[0:heads]
        bias_sum = nt(jnp.ones(rows8.shape, BF16), rows8)[0:1]
        small[heads : heads + 1, 0:16] = bias_sum
        gate_low = gate_rows(gate_ref[...])
        gain = gain_ref[...]
        now = last + 2
        for b in range(tokens // block):
            rows = slice(block * b, block * (b + 1))
            mixer_grad = tn(rows8[:, rows], gate_low)
            for k in range(groups):
                for j, ref in enumerate((wq_ref, wk_ref, wv_ref)):
                    mixer_grad = mixer_grad + nt(
                        dqkv[k, rows, hg * 64 * j : hg * 64 * (j + 1)],
                        ref[:, hg * 64 * k : hg * 64 * (k + 1)],
                    )
            xhat, scale = normalize(x_ref[rows, :].astype(F32))
            small[2 * heads : 2 * heads + 1, :] += jnp.sum(
                mixer_grad * xhat, axis=0, keepdims=True
            )
            small[2 * heads + 1 : 2 * heads + 2, :] += jnp.sum(mixer_grad, axis=0, keepdims=True)
            dx_ref[rows, :] = mg_ref[rows, :] + normalize_back(mixer_grad, gain, xhat, scale)
            if comm:
                advance(now)
                now += 1
        if comm:
            board.add(
                plans["small"], small_src, smallsum_ref, small_ref, [now, now + 1, now + 2, now + 3]
            )
            for later_tick in range(now, board.last() + 1):
                advance(later_tick)
            board.drain()


OS_TICKS = (2, 4, 7, 9, 11, 14, 16)
F_TICKS = (6, 8, 10, 12)
W_TICKS = (8, 10, 12, 14, 16, 18, 20)
W_PIECES = 3


def back_plans(os, f, w, small):
    return {
        "os": Plan(os[0], os[1], BF16, *ALL_PLAN),
        "f": Plan(f[0], f[1], F32, *SHARE_PLAN),
        "w": Plan(w[1], w[2], BF16, *ALL_PLAN),
        "w_last": Plan(w[1], w[2] // W_PIECES, BF16, *ALL_PLAN),
        "small": Plan(small[0], small[1], F32, *SHARE_PLAN),
    }


def whole(shape):
    zeros = (0,) * len(shape)
    return pl.BlockSpec(shape, lambda *at: zeros, pipeline_mode=pl.Buffered(1))


ANY = pl.BlockSpec(memory_space=pl.ANY)


def call(kernel, grid, ins, outs, scratch, name, collective_id=None):
    def spec(shape, block, index):
        if block is None:
            return whole(shape)
        return block if isinstance(block, pl.BlockSpec) else pl.BlockSpec(block, index)

    params = {} if collective_id is None else {
        "collective_id": collective_id, "has_side_effects": True
    }
    return pl.pallas_call(
        kernel,
        grid=grid,
        in_specs=[spec(array.shape, block, index) for array, block, index in ins],
        out_specs=[spec(shape, block, index) for shape, _, block, index in outs],
        out_shape=[jax.ShapeDtypeStruct(shape, dtype) for shape, dtype, _, _ in outs],
        scratch_shapes=scratch,
        compiler_params=pltpu.CompilerParams(
            dimension_semantics=("arbitrary",) * len(grid), vmem_limit_bytes=VMEM, **params
        ),
        name=name,
    )(*[array for array, _, _ in ins])


def finish_kernel(u_ref, late_ref, w_ref, os_ref, up_ref, down_ref, q_ref, k_ref, v_ref, o_ref, s_ref):
    hb = u_ref.shape[2]
    for part, ref in enumerate((up_ref, down_ref)):
        ref[:, 0:hb] = u_ref[part].astype(F32)
        for k in range(late_ref.shape[0]):
            ref[:, hb * (k + 1) : hb * (k + 2)] = late_ref[k, part].astype(F32)
    groups, _, lanes = w_ref.shape
    each = lanes // 3
    for part, ref in enumerate((q_ref, k_ref, v_ref)):
        for k in range(groups):
            ref[:, each * k : each * (k + 1)] = w_ref[k, :, each * part : each * (part + 1)].astype(F32)
    width = o_ref.shape[1]
    o_ref[...] = os_ref[:, 0:width].astype(F32)
    for k in range(s_ref.shape[0]):
        s_ref[k] = os_ref[64 * k : 64 * (k + 1), width:].astype(F32).T


def finish(heads, sum_u, sum_late, sum_w, out_state, small):
    width = sum_w.shape[1]
    steps = 4
    rows = width // steps
    late, _, hb = sum_late.shape
    feats = out_state.shape[1] - width
    square = ((width, width), F32, (rows, width), lambda i: (i, 0))
    wide = ((width, (late + 1) * hb), F32, (rows, (late + 1) * hb), lambda i: (i, 0))
    return call(
        finish_kernel,
        (steps,),
        [
            (sum_u.reshape(2, width, hb), (2, rows, hb), lambda i: (0, i, 0)),
            (sum_late.reshape(late, 2, width, hb), (late, 2, rows, hb), lambda i: (0, 0, i, 0)),
            (sum_w, (sum_w.shape[0], rows, sum_w.shape[2]), lambda i: (0, i, 0)),
            (out_state, (rows, width + feats), lambda i: (i, 0)),
        ],
        [wide, wide, square, square, square, square]
        + [((heads, feats, 64), F32, (heads // steps, feats, 64), lambda i: (i, 0, 0))],
        [],
        "finish",
    )


def carry_over(payload, logs, forward):
    n, index = lax.axis_size("seq"), lax.axis_index("seq")
    everything = lax.all_gather(payload, "seq")
    every_log = lax.all_gather(logs, "seq")
    heads = logs.shape[0]
    row = jnp.arange(payload.shape[0])
    head = jnp.where(row < 64 * heads, row // 64, jnp.minimum(row - 64 * heads, heads - 1))
    total = jnp.zeros(payload.shape, F32)
    for k in range(n) if forward else reversed(range(n)):
        ahead = (k < index) if forward else (k > index)
        new = jnp.exp(every_log[k])[head][:, None] * total + everything[k].astype(F32)
        total = jnp.where(ahead, new, total)
    return total.astype(BF16)


def local(
    inputs,
    cotangent,
    mixer_gain,
    mixer_bias,
    query_weight,
    key_weight,
    value_weight,
    gate_weight,
    gate_bias,
    output_weight,
    projections,
    start_state,
    start_norm,
    feed_gain,
    feed_bias,
    up_weight,
    up_bias,
    down_weight,
    down_bias,
):
    _, tokens, width = inputs.shape
    heads, size, feats = projections.shape
    chunks = tokens // C
    tile = min(T, tokens)
    tiles = tokens // tile
    shards = lax.axis_size("seq")
    first = lax.axis_index("seq") == 0
    comm = (lax.axis_size("dp"), shards) == (16, 2)
    x = inputs.reshape(tokens, width)
    dout = cotangent.reshape(tokens, width)
    shard_width = up_weight.shape[1]
    hidden = shard_width * shards
    hb = min(HB, shard_width)
    pairs = hidden // (2 * hb)
    wide = heads * LANES
    wider = heads * 2 * feats
    pay_shape = (heads * 64 + 16, 2 * feats)

    def const(array):
        return (array if array.ndim > 1 else array[None], None, None)

    def keep(shape, dtype):
        return (shape, dtype, None, None)

    def hbm(array):
        return (array, ANY, None)

    def result(shape, dtype):
        return (shape, dtype, ANY, None)

    def vmem(*shape, dtype=BF16):
        return pltpu.VMEM(shape, dtype)

    def early(n):
        return (C, n), lambda i: (jnp.minimum(i, chunks - 1), 0)

    def out_early(n, dtype):
        return ((tokens, n), dtype) + early(n)

    ins = [(x,) + early(width)]
    ins += [const(part) for part in (mixer_gain, mixer_bias, query_weight, key_weight)]
    ins += [
        const(value_weight),
        const(gate_weight),
        (gate_bias, pl.BlockSpec(memory_space=pltpu.SMEM), None),
        const(projections),
        const(start_state),
        const(start_norm),
    ]
    outs = [out_early(width, BF16)] * 3 + [out_early(width, F32)] * 2
    outs += [out_early(wider, BF16)] * 2 + [out_early(width, BF16), out_early(LANES, F32)]
    outs += [
        (
            (4 * heads, tokens),
            F32,
            (4 * heads, C),
            lambda i: (0, jnp.minimum(i, chunks - 1)),
        ),
        (
            (chunks, heads, LANES, 2 * feats),
            BF16,
            (1, heads, LANES, 2 * feats),
            lambda i: (jnp.minimum(i, chunks - 1), 0, 0, 0),
        ),
        ((tokens, wide), F32, (C, wide), lambda i: (jnp.maximum(i - chunks, 0), 0)),
    ]
    scratch = [
        vmem(heads, LANES, 2 * feats, dtype=F32),
        vmem(1, LANES, dtype=F32),
        vmem(chunks, C, wider),
        vmem(chunks, C, wider),
        vmem(chunks, C, width),
        vmem(chunks, C, LANES, dtype=F32),
        vmem(chunks, 4 * heads, C, dtype=F32),
        vmem(chunks, heads, LANES, 2 * feats),
        vmem(width, LANES),
        vmem(heads, width),
        vmem(1, LANES, dtype=F32),
        vmem(heads, LANES, dtype=F32),
        vmem(heads // 2, 3 * LANES, 2 * feats),
    ]
    upb = up_bias.astype(F32)[None]
    if comm:
        ins += [hbm(up_weight), hbm(down_weight), const(upb)]
        outs += [
            keep(pay_shape, BF16),
            result(up_weight.shape, BF16),
            result(down_weight.shape, BF16),
            keep((2, shard_width), F32),
        ]
        scratch += [
            vmem(*pay_shape),
            vmem(*pay_shape),
            vmem(1, shard_width, dtype=F32),
            pltpu.SemaphoreType.DMA((6,)),
            pltpu.SemaphoreType.DMA((6,)),
        ]
    else:
        outs += [keep(pay_shape, BF16), keep((8, LANES), F32)]
    found = call(
        partial(features_kernel, heads, chunks, comm),
        (2 * chunks,),
        ins,
        outs,
        scratch,
        "features",
        1 if comm else None,
    )
    ml, uq, uk, rq, rk, qf, kf, v, gcol, grow, before, num = found[:12]
    if comm:
        entry, up_other, down_other, upb = found[12:]
        weights = (up_weight, up_other, down_weight, down_other)
    else:
        final, total = found[12:]
        logs = total[0, :heads]
        entry = carry_over(final, logs, True)
        weights = (lax.all_gather(up_weight, "seq"), lax.all_gather(down_weight, "seq"))
        upb = lax.all_gather(upb, "seq")

    steps = 2 * tiles + pairs

    def first_last(n):
        def index(i):
            late = jnp.maximum(i - tiles - pairs, 0)
            return (jnp.where(i < tiles + pairs, jnp.minimum(i, tiles - 1), late), 0)

        return (tile, n), index

    def only_first(n):
        return (tile, n), lambda i: (jnp.minimum(i, tiles - 1), 0)

    def only_last(n, dtype):
        return (
            (tokens, n),
            dtype,
            (tile, n),
            lambda i: (jnp.maximum(i - tiles - pairs, 0), 0),
        )

    ins = [
        (x,) + only_first(width),
        hbm(qf),
        (num,) + only_first(wide),
        (gcol,) + first_last(LANES),
        const(entry),
        const(output_weight),
        const(feed_gain),
        const(feed_bias),
        const(down_bias),
        const(upb),
        hbm(dout),
    ] + [hbm(part) for part in weights]
    outs = [only_last(width, BF16), only_last(width, F32), only_last(wide, BF16)]
    scratch = [
        vmem(heads, LANES, 2 * feats),
        vmem(heads, LANES, 2 * feats, dtype=F32),
        vmem(tokens, width, dtype=F32),
        vmem(tokens, width, dtype=F32),
        vmem(tokens, width, dtype=F32),
        vmem(tokens, width),
        vmem(tokens, width),
        vmem(tokens, width),
        vmem(tokens, width, dtype=F32),
        vmem(tokens, width, dtype=F32),
        vmem(tokens, width),
        vmem(shards, width, shard_width),
        vmem(shards, width, shard_width),
        vmem(tokens, 2 * hb),
        vmem(tokens, 2 * hb),
        vmem(24, width, dtype=F32),
        pltpu.SemaphoreType.DMA((5 + tiles,)),
        vmem(tokens, wider),
    ]
    if comm:
        plans = feed_plans(hb)
        outs += [
            result((2 * width, hb), BF16),
            *[keep((plan.left, hb), BF16) for plan in plans[1:]],
            keep((width, width + 2 * feats), BF16),
            keep((16, width), F32),
            keep(pay_shape, BF16),
        ]
        scratch += [
            vmem(pairs, 4 * width, hb),
            vmem(2 * width, hb),
            vmem(shards, 1, shard_width, dtype=F32),
            vmem(*pay_shape),
            vmem(*pay_shape),
            pltpu.SemaphoreType.DMA,
            pltpu.SemaphoreType.DMA,
            pltpu.SemaphoreType.DMA((pairs,)),
        ]
        for plan in plans:
            scratch += plan.scratch()
    else:
        outs += [
            keep((shards, width, shard_width), BF16),
            keep((shards, width, shard_width), BF16),
            keep((shards, 1, shard_width), F32),
            keep((width, width), BF16),
            keep(pay_shape, BF16),
            keep((24, width), F32),
        ]
    found = call(
        partial(feed_kernel, heads, tiles, pairs, comm),
        (steps,),
        ins,
        outs,
        scratch,
        "feed",
        2 if comm else None,
    )
    out, mg, a = found[:3]
    if comm:
        sum_u, *u_late = found[3:7]
        out_state, flat, after = found[7:]
    else:
        up_grad, down_grad, upb_grad, output_grad, adj_final, feed_sums = found[3:]
        after = carry_over(adj_final, logs, False)
        feed_three = jnp.sum(feed_sums.reshape(3, 8, width), axis=1)
        begin = adj_final.astype(F32)
        row = jnp.arange(pay_shape[0])
        head = jnp.where(row < 64 * heads, row // 64, jnp.minimum(row - 64 * heads, heads - 1))
        begin = begin + jnp.exp(logs)[head][:, None] * after.astype(F32)
        begin = jnp.where(first, begin, 0.0)
        state_grad = begin[: heads * 64].astype(BF16)
        norm_grad = 64.0 * begin[heads * 64 : heads * 65]

    hg = GROUP_HEADS
    groups = heads // hg

    def back_rows(n, per_group=True):
        return (C, n), lambda g, i: (chunks - 1 - i, g if per_group else 0)

    def per_group(array, *shape):
        zeros = (0,) * (len(shape) - 1)
        return (array, shape, lambda g, i: (g,) + zeros)

    def states(array):
        return [
            (array, (hg * 64, 2 * feats), lambda g, i: (g, 0)),
            (array, (16, 2 * feats), lambda g, i: (heads * 4, 0)),
        ]

    ins = [
        (qf,) + back_rows(hg * 2 * feats),
        (kf,) + back_rows(hg * 2 * feats),
        (v,) + back_rows(hg * size),
        (uq,) + back_rows(hg * size),
        (uk,) + back_rows(hg * size),
        (rq,) + back_rows(hg * size),
        (rk,) + back_rows(hg * size),
        (a,) + back_rows(hg * LANES),
        (gcol,) + back_rows(LANES, False),
        (grow, (4 * heads, C), lambda g, i: (0, chunks - 1 - i)),
        (before, (1, hg, LANES, 2 * feats), lambda g, i: (chunks - 1 - i, g, 0, 0)),
    ]
    ins += states(entry) + states(after)
    ins += [
        per_group(projections, hg, size, feats),
        hbm(x),
        hbm(mg),
        hbm(ml),
        hbm(query_weight),
        hbm(key_weight),
        hbm(value_weight),
        const(gate_weight),
        const(mixer_gain),
    ]
    w_shape, small_shape = (groups, width, 3 * hg * size), (32, width)

    def sums(shape, dtype):
        return result(shape, dtype) if comm else keep(shape, dtype)

    outs = [keep((tokens, width), F32), sums(w_shape, BF16), sums(small_shape, F32)]
    scratch = [
        vmem(hg, LANES, 2 * feats, dtype=F32),
        vmem(groups, tokens, 3 * hg * size),
        vmem(groups, 8, tokens, dtype=F32),
        vmem(tokens, width),
        vmem(tokens, width, dtype=F32),
        vmem(tokens, width),
        vmem(width, width),
        vmem(width, width),
        vmem(width, width),
        pltpu.SemaphoreType.DMA((11,)),
        vmem(hg // 2, LANES, 2 * feats),
    ]
    if comm:
        ins += [hbm(part) for part in (*u_late, out_state, flat)]
        summed = [
            ((len(u_late), 2 * width, hb), BF16),
            (out_state.shape, BF16),
            (flat.shape, F32),
        ]
        outs += [result(*part) for part in summed]
        scratch += [vmem(*part.shape) for part in u_late]
        scratch += [
            vmem(*out_state.shape),
            vmem(*flat.shape, dtype=F32),
            vmem(*w_shape),
            vmem(*small_shape, dtype=F32),
        ]
        scratch += [vmem(*shape, dtype=dtype) for shape, dtype in summed]
        scratch += [vmem(*w_shape), vmem(*small_shape, dtype=F32)]
        plans = back_plans(out_state.shape, flat.shape, w_shape, small_shape)
        plans = late_plans(hb) + [
            plans[name]
            for name in ("os", "f") + ("w",) * (groups - 1) + ("w_last",) * W_PIECES + ("small",)
        ]
        scratch += [pltpu.SemaphoreType.DMA((len(plans),))]
        for plan in plans:
            scratch += plan.scratch()
    found = call(
        partial(back_kernel, heads, hg, chunks, comm),
        (groups, chunks),
        ins,
        outs,
        scratch,
        "back",
        3 if comm else None,
    )
    dx, sum_w, small = found[:3]
    if comm:
        sum_late, out_state, flat = found[3:]
        results = finish(heads, sum_u, sum_late, sum_w, out_state, small)
        sum_up, sum_down, sum_q, sum_k, sum_v, sum_o, sum_state = results
        sum_feed = flat[0:3]
        sum_upb = flat[3 : 3 + hidden // width].reshape(-1)
        sum_upb = jnp.where(first, sum_upb[:shard_width], sum_upb[shard_width:])
        sum_norm = flat[8 : 8 + heads, : 2 * feats]
    else:
        own = lax.psum_scatter(
            jnp.stack([up_grad, down_grad]), "seq", scatter_dimension=1, tiled=True
        )
        upb_own = lax.psum_scatter(upb_grad, "seq", scatter_dimension=0, tiled=True)
        (sum_up, sum_down), sum_upb = lax.psum((own[:, 0], upb_own.reshape(-1)), "dp")
        sum_w, sum_o, sum_state, small, sum_norm, sum_feed = lax.psum(
            (sum_w, output_grad, state_grad, small, norm_grad, feed_three), ("dp", "seq")
        )
        sum_w = sum_w.reshape(groups, width, 3, hg * size).transpose(2, 1, 0, 3)
        sum_q, sum_k, sum_v = sum_w.reshape(3, width, width).astype(F32)
        sum_state = sum_state.reshape(heads, size, 2 * feats).astype(F32).transpose(0, 2, 1)
    return (
        out.reshape(inputs.shape),
        dx.reshape(inputs.shape),
        small[2 * heads],
        small[2 * heads + 1],
        sum_q,
        sum_k,
        sum_v,
        small[:heads].T,
        small[heads, :heads],
        sum_o.astype(F32),
        sum_state,
        sum_norm,
        sum_feed[0],
        sum_feed[1],
        sum_up.astype(F32),
        sum_upb,
        sum_down.astype(F32),
        sum_feed[2],
    )


def solution(mesh):
    tokens = P("dp", "seq", None)
    columns = P(None, "seq")
    return jax.shard_map(
        local,
        mesh=mesh,
        in_specs=(tokens, tokens) + (P(),) * 13 + (columns, P("seq"), columns, P()),
        out_specs=(tokens, tokens) + (P(),) * 12 + (columns, P("seq"), columns, P()),
        check_vma=False,
    )
```

time: 271 us -> 205 us (0.76)
  between operations: 14.4 us -> 0.71 us
  waiting for transfers between devices: 12.8 us -> 0 us
  local copies, waits for them, and re-layouts: 26.2 us -> 13.7 us
  other arithmetic: 11.6 us -> 1.28 us
  matrix products: 8.98 us -> 0 us
  starting transfers between devices: 6.64 us -> 0 us
  blocking collectives: 4.48 us -> 0 us
  Pallas kernels: 185 us -> 189 us
    all_gather x2 -> x0, waiting for transfers between devices: 11.5 us -> none  [the longest x1 11.4 us: local(): every_down = lax.all_gather(down_weight, 'seq')]
    dot_general x3 -> x0, matrix products: 8.98 us -> none  [tn(): lax.dot_general(a, b, (((0,), (0,)), ((), ())), preferred_element_type=F32)]
    ppermute x2 -> x0, starting transfers between devices: 6.57 us -> none  [carry_over(): return lax.ppermute(payload, 'seq', [(0, 1)] if forward else [(1, 0)])]
    all_gather x1 -> x0, blocking collectives: 4.48 us -> none  [local(): every_upb = lax.all_gather(up_bias.astype(F32), 'seq').reshape(1, -1)]
    another operation x5 -> x0, local copies, waits for them, and re-layouts: 4.46 us -> none  [the longest x1 1.73 us: local(): sum_q, sum_k, sum_v = sum_w.reshape(3, width, width).astype(F32)]
    pallas_call x4, Pallas kernels: 185 us -> 189 us  [call(): pl.pallas_call(kernel, grid=grid, in_specs=[spec(array.shape, block, inde...]
    convert_element_type x2 -> x0, other arithmetic: 3.58 us -> none  [the longest x1 2.47 us: local(): sum_down.astype(F32)]
    concatenate x2 -> x0, other arithmetic: 2.88 us -> none  [the longest x1 2.26 us: local(): up_down = jnp.concatenate(up_halves + down_halves)]
  transfers between devices with their start and end apart: 4 -> 0, of which waited for: 1 -> 0; matrix products, arithmetic and copies ran while one was open for 7% -> 0% of each run, Pallas kernels for 16% -> 0%
where the time goes in v4:
time: 205 us; the launch traced here: 204 us
  Pallas kernels  189 us (92%)
  local copies, waits for them, and re-layouts  13.7 us (7%)
    pallas_call x4, Pallas kernels, call(): pl.pallas_call(kernel, grid=grid, in_specs=[spec(array.shape, block, inde...  189 us
    unnamed x12, local copies, waits for them, and re-layouts  9.22 us

profile of v4, /device:TPU:0, one launch (start us, length us, event | category | flops | bytes accessed | tf_op | source)
XLA Modules:
  0.0 204.4 jit_solution(3670859594102134351)
XLA Ops:
  0.7 1.5 copy.37.refs_6_.refs_22_
  2.1 2.4 %copy.38.refs_9_ = f32[8,256,64]{2,1,0:T(8,128)} copy(f32[8,256,64]{1,2,0:T(8,128)} %param.30) | data formatting | bytes 1048576 | tf_op args[11]
  4.5 1.3 broadcast_in_dim.28
  5.8 47.4 %features.1 = (bf16[1024,512]{1,0:T(8,128)(2,1)}, bf16[1024,512]{1,0:T(8,128)(2,1)}, bf16[1024,512]{1,0:T(8,128)(2,1)}, f32[1024,512]{1,0:T(8,128)}, f32[1024,51...) custom-call(bf16[1024,512]{1,0:T(8,128)(2,1)} %bitcast.24, ...), custom_call_target="tpu_custom_call" | custom-call | tf_op jit(solution)/shard_map/features/pallas_call | solution.py:1123
  53.2 53.5 %feed.1 = (bf16[1024,512]{1,0:T(8,128)(2,1)}, f32[1024,512]{1,0:T(8,128)}, bf16[1024,1024]{1,0:T(8,128)(2,1)}, bf16[1024,256]{1,0:T(8,128)(2,1)}, bf16[64,256]{1...) custom-call(bf16[1024,512]{1,0:T(8,128)(2,1)} %bitcast.25, ...), custom_call_target="tpu_custom_call" | custom-call | tf_op jit(solution)/shard_map/feed/pallas_call | solution.py:1123
  106.7 81.5 %back.1 = (f32[1024,512]{1,0:T(8,128)}, bf16[2,512,768]{2,1,0:T(8,128)(2,1)}, f32[32,512]{1,0:T(8,128)}, bf16[3,1024,256]{2,1,0:T(8,128)(2,1)}, bf16[512,768]{1,0:T(8,128)(2,1)}, /*index=5*/f32[16,512]{1,0:T(8,128)}) custom-call(bf16[1024,2048]{1,0:T(8,128)(2,1)} %get-tuple-element.57.refs_1_.refs_0_, bf16[1024,2048]{1,0:T(8,128)(2,1)} %get-tuple-element.65.refs_1_, ...), custom_call_target="tpu_custom_call" | custom-call | tf_op jit(solution)/shard_map/back/pallas_call | solution.py:1123
  188.3 0.0 copy-start.2
  188.3 0.0 copy-start.1
  188.3 6.2 %finish.1 = (f32[512,1024]{1,0:T(8,128)}, f32[512,1024]{1,0:T(8,128)}, f32[512,512]{1,0:T(8,128)}, f32[512,512]{1,0:T(8,128)}, f32[512,512]{1,0:T(8,128)}, /*index=5*/f32[512,512]{1,0:T(8,128)}, f32[8,256,64]{2,1,0:T(8,128)}) custom-call(bf16[2,512,256]{2,1,0:T(8,128)(2,1)} %bitcast.31, bf16[3,2,512,256]{3,2,1,0:T(8,128)(2,1)} %bitcast.28, ...), custom_call_target="tpu_custom_call" | custom-call | tf_op jit(solution)/shard_map/finish/pallas_call | solution.py:1123
  194.5 0.0 copy-start
  194.5 2.5 %copy.40 = f32[8,256,64]{1,2,0:T(8,128)} copy(f32[8,256,64]{2,1,0:T(8,128)} %get-tuple-element.106) | data formatting | bytes 1048576
  197.0 0.0 copy-done.2
  197.0 1.4 fusion
  198.4 1.3 slice_bitcast_fusion
  199.7 0.6 copy.41
  200.3 0.6 slice.43
  200.9 1.2 slice_bitcast_fusion.1
  202.1 0.0 copy-done.1
  202.1 1.0 copy.44
  203.1 0.0 copy-done
  203.1 1.3 copy.45
  (1 shorter events, 0.0 us)
Async XLA Ops:
  188.3 8.8 %copy-start.2 = (f32[16,512]{1,0:T(8,128)S(1)}, f32[16,512]{1,0:T(8,128)}, u32[]{:S(2)}) copy-start(f32[16,512]{1,0:T(8,128)} %get-tuple-element.93) | copy-start | bytes 98308
  188.3 13.9 %copy-start.1 = (bf16[1024,512]{1,0:T(8,128)(2,1)S(1)}, bf16[1024,512]{1,0:T(8,128)(2,1)}, u32[]{:S(2)}) copy-start(bf16[1024,512]{1,0:T(8,128)(2,1)} %get-tuple-element.64) | copy-start | bytes 3145732
  194.5 8.6 %copy-start = (f32[1024,512]{1,0:T(8,128)S(1)}, f32[1024,512]{1,0:T(8,128)}, u32[]{:S(2)}) copy-start(f32[1024,512]{1,0:T(8,128)} %get-tuple-element.82) | copy-start | bytes 6291460

commit v5 on v4

--- a/solution.py
+++ b/solution.py
@@ -19,6 +19,9 @@
 C = 128
 T = 256
 HB = 256
+INNER_HEADS = 8
+WEIGHT_STEPS = (4, 6, 8, 11)
+SPAN = 2
 GROUP_HEADS = 4
 LANES = 128
 
@@ -266,16 +269,21 @@
             return
         landing = self.landing[stage]
         arrivals, rows, _ = landing.shape
-        own = pl.multiple_of(self.links.at[plan.groups[stage]] * rows, 8)
-        total = self.parts[stage][pl.ds(own, rows), :].astype(F32)
-        for step in range(arrivals):
-            total = total + landing[step].astype(F32)
-        total = total.astype(landing.dtype)
+        own = self.links.at[plan.groups[stage]] * rows
+        into, start = self.out, self.final[0]
         if stage + 1 < len(plan.scatter):
-            self.parts[stage + 1][...] = total
-        else:
-            start, rows = self.final
-            self.out[pl.ds(pl.multiple_of(start, 8), rows), :] = total
+            into, start = self.parts[stage + 1], 0
+        block = min(rows, SUM_ROWS)
+
+        def add_block(k, carry):
+            at = k * block
+            total = self.parts[stage][pl.ds(pl.multiple_of(own + at, 16), block), :].astype(F32)
+            for step in range(arrivals):
+                total = total + landing[step, pl.ds(pl.multiple_of(at, 16), block), :].astype(F32)
+            into[pl.ds(pl.multiple_of(start + at, 16), block), :] = total.astype(landing.dtype)
+            return carry
+
+        lax.fori_loop(0, rows // block, add_block, 0)
 
     def drain(self):
         for stage in range(self.plan.stages):
@@ -400,24 +408,29 @@
     if comm:
         sent, landed, upb_landed, sends, recvs = take(5)
         links = Links()
-        core = links.at["core"]
-        half = up_hbm.shape[0] // 2
-        own_rows = pl.ds(pl.multiple_of(core * half, 16), half)
-        other_rows = pl.ds(pl.multiple_of((1 - core) * half, 16), half)
+        core, y = links.at["core"], links.at["y"]
+        part = up_hbm.shape[0] // 4
+        here = pl.ds(pl.multiple_of((2 * core + y) * part, 16), part)
+        there = pl.ds(pl.multiple_of((2 * core + 1 - y) * part, 16), part)
+        own_half = pl.ds(pl.multiple_of(2 * core * part, 16), 2 * part)
+        other_half = pl.ds(pl.multiple_of(2 * (1 - core) * part, 16), 2 * part)
 
         def remote(k, sending):
-            group = "core" if k >= 4 else "xr"
-            if k == 2:
+            group = ("xr", "y", "core")[k // 2] if k < 6 else "xr"
+            if k == 6:
                 source, lands = upb_ref, upb_landed
-            elif k == 3:
+            elif k == 7:
                 source, lands = sent, landed
             else:
-                into = (upo_hbm, downo_hbm)[k % 2].at[own_rows]
-                source, lands = (up_hbm, down_hbm)[k % 2].at[own_rows], into
-                if k >= 4:
-                    source = into
-                    if not sending:
-                        lands = (upo_hbm, downo_hbm)[k % 2].at[other_rows]
+                mine_ref, theirs_ref = ((up_hbm, upo_hbm), (down_hbm, downo_hbm))[k % 2]
+                if k < 2:
+                    source, lands = mine_ref.at[here], theirs_ref.at[here]
+                elif k < 4:
+                    source = theirs_ref.at[here]
+                    lands = source if sending else theirs_ref.at[there]
+                else:
+                    source = theirs_ref.at[own_half]
+                    lands = source if sending else theirs_ref.at[other_half]
             return pltpu.make_async_remote_copy(
                 src_ref=source if sending else lands,
                 dst_ref=lands,
@@ -429,19 +442,19 @@
 
         @pl.when(step == 0)
         def _():
-            links.greet(("core", "xr"))
-            for k in (0, 1, 2):
+            links.greet(("core", "xr", "y"))
+            for k in (6, 0, 1):
                 remote(k, True).start()
 
         @pl.when(step == chunks)
         def _():
-            remote(3, True).start()
-
-        @pl.when(step == chunks + chunks // 2)
-        def _():
-            for k in (0, 1):
+            remote(7, True).start()
+
+        for k, ready in zip(range(4), WEIGHT_STEPS):
+            @pl.when(step == ready * chunks // 8)
+            def _(k=k):
                 remote(k, False).wait_recv()
-                remote(k + 4, True).start()
+                remote(k + 2, True).start()
 
     @pl.when(step == 0)
     def _():
@@ -515,19 +528,22 @@
         grow_s[chunk] = rows
 
         ftr_scale = 1.0 / math.sqrt(LANES)
-        for p in range(heads // 2):
-            lanes = slice(LANES * p, LANES * (p + 1))
-            both = jnp.concatenate([q[:, lanes], k[:, lanes]], axis=0)
-            scale = lax.rsqrt(head_sums(both * both) + EPS_UNIT)
-            unit = both * scale
+        pairs = range(heads // 2)
+        lanes_of = [slice(LANES * p, LANES * (p + 1)) for p in pairs]
+        boths = [jnp.concatenate([q[:, at], k[:, at]], axis=0) for at in lanes_of]
+        scales = [lax.rsqrt(head_sums(both * both) + EPS_UNIT) for both in boths]
+        all_turns = []
+        for p in pairs:
+            unit = boths[p] * scales[p]
             high = unit.astype(BF16)
             rest = (unit - high.astype(F32)).astype(BF16)
-            uq_ref[:, lanes] = high[:C]
-            uk_ref[:, lanes] = high[C:]
-            rq_ref[:, lanes] = scale[:C]
-            rk_ref[:, lanes] = scale[C:]
-            turns = nn(jnp.concatenate([high, rest, high], axis=1), pcat_ref[p])
-            s, c = sin_cos(turns, ftr_scale)
+            uq_ref[:, lanes_of[p]] = high[:C]
+            uk_ref[:, lanes_of[p]] = high[C:]
+            rq_ref[:, lanes_of[p]] = scales[p][:C]
+            rk_ref[:, lanes_of[p]] = scales[p][C:]
+            all_turns.append(nn(jnp.concatenate([high, rest, high], axis=1), pcat_ref[p]))
+        for p in pairs:
+            s, c = sin_cos(all_turns[p], ftr_scale)
             s = s.astype(BF16)
             c = c.astype(BF16)
             for j in range(2):
@@ -540,7 +556,7 @@
                 kf = feats[C:]
                 kf_ref[:, place] = kf
                 kf_s[chunk, :, place] = kf
-                values = jnp.where(mine(h, lower), v[:, lanes], 1.0)
+                values = jnp.where(mine(h, lower), v[:, lanes_of[p]], 1.0)
                 weighted = (values * jnp.exp(column(coef, h, C, LANES))).astype(BF16)
                 now = state[h]
                 now_low = now.astype(BF16)
@@ -556,30 +572,36 @@
     def _():
         causal = iota((C, C), 0) >= iota((C, C), 1)
         gcol = gcol_s[chunk]
-        for h in range(heads):
-            qf = qf_s[chunk, :, 256 * h : 256 * (h + 1)]
-            kf = kf_s[chunk, :, 256 * h : 256 * (h + 1)]
-            p = h // 2
-            v = v_s[chunk, :, LANES * p : LANES * (p + 1)].astype(F32)
-            values = jnp.where(mine(h, lower), v, 1.0).astype(BF16)
-            decay = column(gcol, h, C, LANES)
-            pairs = jnp.where(causal, jnp.exp(decay + grow_s[chunk, h : h + 1, :]), 0.0)
-            both = nt(qf, jnp.concatenate([kf, before_s[chunk, h]], axis=0))
-            weights = (both[:, :C] * pairs).astype(BF16)
-            n_ref[:, LANES * h : LANES * (h + 1)] = (
-                nn(weights, values) + jnp.exp(decay) * both[:, C:]
-            )
+        for first in range(0, heads, INNER_HEADS):
+            some = range(first, first + INNER_HEADS)
+            boths = []
+            for h in some:
+                place = slice(256 * h, 256 * (h + 1))
+                keys = jnp.concatenate([kf_s[chunk, :, place], before_s[chunk, h]], axis=0)
+                boths.append(nt(qf_s[chunk, :, place], keys))
+            decays = [column(gcol, h, C, LANES) for h in some]
+            weights = []
+            for h, both, decay in zip(some, boths, decays):
+                pairs = jnp.where(causal, jnp.exp(decay + grow_s[chunk, h : h + 1, :]), 0.0)
+                weights.append((both[:, :C] * pairs).astype(BF16))
+            for k, h in enumerate(some):
+                lanes = slice(LANES * (h // 2), LANES * (h // 2 + 1))
+                v = v_s[chunk, :, lanes].astype(F32)
+                values = jnp.where(mine(h, lower), v, 1.0).astype(BF16)
+                n_ref[:, LANES * h : LANES * (h + 1)] = (
+                    nn(weights[k], values) + jnp.exp(decays[k]) * boths[k][:, C:]
+                )
 
     if comm:
         @pl.when(step == 2 * chunks - 1)
         def _():
-            for k in (2, 3, 4, 5):
+            for k in (4, 5, 6, 7):
                 remote(k, False).wait_recv()
             later = links.seq == 1
             entry_ref[...] = jnp.where(later, landed[...].astype(F32), 0.0).astype(BF16)
             upbs_ref[0:1, :] = upb_ref[...]
             upbs_ref[1:2, :] = upb_landed[...]
-            for k in range(6):
+            for k in range(8):
                 remote(k, True).wait_send()
 
 
@@ -590,7 +612,7 @@
     weights_hbm = take(4 if comm else 2)
     out_ref, mg_ref, a_ref = take(3)
     if comm:
-        usum_hbm, *late_refs = take(1 + len(FEED_STAGES) - 1)
+        late_refs = take(len(FEED_STAGES))
         os_ref, flat_ref, after_ref = take(3)
     else:
         upg_ref, downg_ref, upbg_ref, o_ref, final_ref, sums_out = take(6)
@@ -610,14 +632,11 @@
         up_own, up_other, down_own, down_other = weights_hbm
         loads += [(up_own, up_s.at[0]), (up_other, up_s.at[1])]
         loads += [(down_own, down_s.at[0]), (down_other, down_s.at[1])]
-        u_src, usum_s, upbg_s, sent, landed, sends, recvs, store_sems = take(8)
+        u_src, upbg_s, sent, landed, sends, recvs = take(6)
         links = Links()
-        board = Board(links, take, store_sems)
+        board = Board(links, take, None)
         for j, (plan, ticks) in enumerate(zip(feed_plans(hb), FEED_TICKS)):
-            if j == 0:
-                board.add(plan, u_src.at[j], usum_s, usum_hbm, ticks)
-            else:
-                board.add(plan, u_src.at[j], late_refs[j - 1], None, ticks)
+            board.add(plan, u_src.at[j], late_refs[j], None, ticks)
 
         def exchange():
             return pltpu.make_async_remote_copy(
@@ -656,13 +675,13 @@
             pl.when(step == t)(load(t).wait)
         here = pl.ds(pl.multiple_of(step * rows, rows), rows)
         gcol = gcol_ref[...]
+        fars = [nt(qf_s[here, 256 * h : 256 * (h + 1)], entry[h]) for h in range(heads)]
         mixed = []
         for p in range(heads // 2):
             lanes = slice(LANES * p, LANES * (p + 1))
             both = []
             for h in (2 * p, 2 * p + 1):
-                far = nt(qf_s[here, 256 * h : 256 * (h + 1)], entry[h])
-                far = far * jnp.exp(column(gcol, 16 + h, rows, LANES))
+                far = fars[h] * jnp.exp(column(gcol, 16 + h, rows, LANES))
                 both.append(n_ref[:, LANES * h : LANES * (h + 1)] + far)
             num = jnp.where(lower, both[0], both[1])
             den = pltpu.roll(jnp.where(lower, both[1], both[0]), 64, 1)
@@ -756,18 +775,20 @@
         branch = middle_grad.astype(BF16)
         br_s[here, :] = branch
         mixed_grad = nt(branch, wo_ref[...])
-        for p in range(heads // 2):
-            lanes = slice(LANES * p, LANES * (p + 1))
-            num, den = num_s[here, lanes], den_s[here, lanes]
+        lanes_of = [slice(LANES * p, LANES * (p + 1)) for p in range(heads // 2)]
+        alongs = [head_sums(mixed_grad[:, lanes] * num_s[here, lanes]) for lanes in lanes_of]
+        lifts = []
+        for p, lanes in enumerate(lanes_of):
+            den = den_s[here, lanes]
             inv = lax.rsqrt(den * den + GUARD)
-            mg = mixed_grad[:, lanes]
-            b = head_sums(mg * num) * den * (inv * inv * inv) * (-1.0 / 64)
+            b = alongs[p] * den * (inv * inv * inv) * (-1.0 / 64)
             b = pltpu.roll(b, 64, 1)
             for h in (2 * p, 2 * p + 1):
-                a = jnp.where(mine(h, lower), mg * inv, b)
+                a = jnp.where(mine(h, lower), mixed_grad[:, lanes] * inv, b)
                 a_ref[:, LANES * h : LANES * (h + 1)] = a.astype(BF16)
-                lifted = (a * jnp.exp(column(gcol, 16 + h, rows, LANES))).astype(BF16)
-                adj[h] += tn(lifted, qf_s[here, 256 * h : 256 * (h + 1)])
+                lifts.append((a * jnp.exp(column(gcol, 16 + h, rows, LANES))).astype(BF16))
+        for h in range(heads):
+            adj[h] += tn(lifts[h], qf_s[here, 256 * h : 256 * (h + 1)])
 
     @pl.when(step == 2 * tiles + pairs - 1)
     def _():
@@ -808,31 +829,29 @@
 
 
 U_SCATTER, U_GATHER = ("core", "xr", "y", "z"), ("z", "y", "core")
-FEED_STAGES = (7, 4, 3, 2)
-FEED_TICKS = ((2, 3, 5, 7, 8, 9, 11, 12), (4, 5, 8, 10, 12), (6, 7, 10, 12), (8, 9, 13))
-BACK_TICKS = ((2, 4, 6, 8), (1, 3, 5, 7, 9), (1, 3, 5, 7, 9, 11))
+FEED_STAGES = (4, 3, 2, 1)
+FEED_TICKS = ((2, 3, 6, 8, 11), (4, 6, 9, 12), (6, 8, 12), (8, 10))
+BACK_TICKS = ((2, 4, 6, 7), (1, 3, 5, 7, 8), (1, 3, 5, 7, 8, 9), (1, 3, 5, 7, 8, 9, 10))
 
 
 def feed_plans(hb):
-    return [
-        Plan(2048, hb, BF16, U_SCATTER[:n], U_GATHER if n > 4 else ()) for n in FEED_STAGES
-    ]
+    return [Plan(2048, hb, BF16, U_SCATTER[:n], ()) for n in FEED_STAGES]
 
 
 def late_plans(hb):
     plans = []
-    for plan, n in zip(feed_plans(hb)[1:], FEED_STAGES[1:]):
+    for plan, n in zip(feed_plans(hb), FEED_STAGES):
         done = [group for group in U_SCATTER[:n] if group != "xr"]
         plans.append(Plan(plan.left, hb, BF16, U_SCATTER[n:], U_GATHER, pre=tuple(done)))
     return plans
 
 
-def back_kernel(heads, hg, chunks, comm, *refs):
+def back_kernel(heads, hg, span, chunks, comm, *refs):
     take = Taker(refs)
     (qf_ref, kf_ref, v_ref, uq_ref, uk_ref, rq_ref, rk_ref, a_ref, gcol_ref, grow_ref) = take(10)
     before_ref, entry_ref, entry_norm, after_ref, after_norm, proj_in = take(6)
     x_hbm, mg_hbm, ml_hbm, wq_hbm, wk_hbm, wv_hbm, gate_ref, gain_ref = take(8)
-    u_hbms = take(3) if comm else ()
+    u_hbms = take(len(FEED_STAGES)) if comm else ()
     os_hbm, f_hbm = take(2) if comm else (None,) * 2
     dx_ref, w_ref, small_ref = take(3)
     usum_hbm, ossum_hbm, fsum_hbm = take(3) if comm else (None,) * 3
@@ -841,8 +860,8 @@
     g, i = pl.program_id(0), pl.program_id(1)
     tick = g * chunks + i
     last = heads // hg * chunks - 1
-    chunk = chunks - 1 - i
-    here = pl.ds(pl.multiple_of(chunk * C, C), C)
+    first_row = (chunks - 1 - i) * (span * C)
+    here = pl.ds(pl.multiple_of(first_row, C), span * C)
     groups = heads // hg
     loads = [
         (x_hbm, x_ref),
@@ -853,7 +872,7 @@
         (wv_hbm, wv_ref),
     ]
     if comm:
-        u_refs = take(3)
+        u_refs = take(len(FEED_STAGES))
         os_ref, f_ref, w_src, small_src = take(4)
         usum_ref, ossum_ref, fsum_ref, wsum_ref, smallsum_ref = take(5)
         (store_sems,) = take(1)
@@ -884,7 +903,7 @@
                     w_src.at[k, :, lanes],
                     wsum_ref.at[k, :, lanes],
                     w_ref.at[k, :, lanes],
-                    [last + 1 + i + (j if i else 0) for i in range(7)] if final else W_TICKS,
+                    [last + 1 + i for i in range(7)] if final else W_TICKS,
                 )
         advance = board.advance
 
@@ -936,95 +955,122 @@
     def grow_row(kind, h):
         return grow_ref[pl.ds(kind * heads + g * hg + h, 1), :]
 
-    for p in range(hg // 2):
-        lanes = slice(LANES * p, LANES * (p + 1))
-        angle_q, angle_k, dvs, x_parts, y_parts, throughs = [], [], [], [], [], []
-        v_pair = v_ref[:, lanes].astype(F32)
-        values = [jnp.where(mine(h, lower), v_pair, 1.0) for h in range(2)]
-        values_low = [part.astype(BF16) for part in values]
-        dweights = nt(
-            a_ref[:, 2 * LANES * p : 2 * LANES * (p + 1)],
-            jnp.concatenate(
-                [
-                    jnp.concatenate([values_low[0], zero], axis=1),
-                    jnp.concatenate([zero, values_low[1]], axis=1),
-                ],
-                axis=0,
-            ),
+    width = hg * 64
+    pairs_of_heads = range(hg // 2)
+    lanes_of = [slice(LANES * p, LANES * (p + 1)) for p in pairs_of_heads]
+    items = [(u, h) for u in reversed(range(span)) for h in range(hg)]
+    numbers = range(len(items))
+    rows_of = [slice(C * u, C * (u + 1)) for u in range(span)]
+    qfs = [qf_ref[rows_of[u], 256 * h : 256 * (h + 1)] for u, h in items]
+    kfs = [kf_ref[rows_of[u], 256 * h : 256 * (h + 1)] for u, h in items]
+    a_lows = [a_ref[rows_of[u], LANES * h : LANES * (h + 1)] for u, h in items]
+    values = [
+        jnp.where(mine(h, lower), v_ref[rows_of[u], lanes_of[h // 2]].astype(F32), 1.0)
+        for u, h in items
+    ]
+    values_low = [part.astype(BF16) for part in values]
+    lifts = [jnp.exp(column(gcol[rows_of[u]], h, C, LANES)) for u, h in items]
+    a_lifts = [(a_lows[k].astype(F32) * lifts[k]).astype(BF16) for k in numbers]
+    dweights = []
+    for k in numbers[::2]:
+        u, h = items[k]
+        top = jnp.concatenate([values_low[k], zero], axis=1)
+        bottom = jnp.concatenate([zero, values_low[k + 1]], axis=1)
+        both = nt(
+            a_ref[rows_of[u], LANES * h : LANES * (h + 2)],
+            jnp.concatenate([top, bottom], axis=0),
         )
-        for j in range(2):
-            h = 2 * p + j
-            qf = qf_ref[:, 256 * h : 256 * (h + 1)]
-            kf = kf_ref[:, 256 * h : 256 * (h + 1)]
-            a_low = a_ref[:, LANES * h : LANES * (h + 1)]
-            a = a_low.astype(F32)
-            decay = column(gcol, h, C, LANES)
-            lift = jnp.exp(decay)
-            coef = jnp.exp(column(gcol, 8 + h, C, LANES))
-            carried = jnp.exp(gcol[0:1, 48 + h : 49 + h])
-            total = jnp.exp(gcol[0:1, 56 + h : 57 + h])
-            entry = grow_state(
-                entry_ref[64 * h : 64 * (h + 1), :], pick_row(entry_norms, g * hg + h), h
+        dweights += [both[:, :C], both[:, C:]]
+    adj_lows, throughs, keys_and_states = [], [], []
+    raws, fars, dv_fars = [], [], []
+    for k, (u, h) in enumerate(items):
+        carried = jnp.exp(gcol[C * u : C * u + 1, 48 + h : 49 + h])
+        total = jnp.exp(gcol[C * u : C * u + 1, 56 + h : 57 + h])
+        entry = grow_state(
+            entry_ref[64 * h : 64 * (h + 1), :], pick_row(entry_norms, g * hg + h), h
+        )
+        before = before_ref[u, h].astype(F32) + carried * entry
+        adj = adj_ref[h]
+        adj_lows.append(adj.astype(BF16))
+        kept = total * adj
+        through = jnp.sum(kept * before, axis=0, keepdims=True)
+        throughs.append(jnp.sum(through, axis=1, keepdims=True))
+        keys_and_states.append(jnp.concatenate([kfs[k], before.astype(BF16)], axis=0))
+        raw_and_far = nt(qfs[k], keys_and_states[k])
+        raws.append(raw_and_far[:, :C])
+        fars.append(raw_and_far[:, C:])
+        dv_fars.append(nt(kfs[k], adj_lows[k]))
+        if u > 0:
+            adj_ref[h] = kept + tn(a_lifts[k], qfs[k])
+        else:
+            adj_ref[h] = kept
+    coefs = [jnp.exp(column(gcol[rows_of[u]], 8 + h, C, LANES)) for u, h in items]
+    weights, draws, boths, v_coefs = [], [], [], []
+    for k, (u, h) in enumerate(items):
+        gap = column(gcol[rows_of[u]], h, C, LANES) + grow_row(0, h)[:, rows_of[u]]
+        pairs = jnp.where(causal, jnp.exp(gap), 0.0)
+        weights.append((raws[k] * pairs).astype(BF16))
+        draw = dweights[k].astype(BF16).astype(F32) * pairs
+        draws.append(draw.astype(BF16))
+        boths.append((raws[k] * draw).astype(BF16))
+        v_coefs.append((values[k] * coefs[k]).astype(BF16))
+    dqs, dks, dvs = [], [], []
+    for k in numbers:
+        dqs.append(nn(jnp.concatenate([draws[k], a_lifts[k]], axis=1), keys_and_states[k]))
+        dks.append(
+            nn(
+                jnp.concatenate([draws[k].T, v_coefs[k]], axis=1),
+                jnp.concatenate([qfs[k], adj_lows[k]], axis=0),
             )
-            before = before_ref[0, h].astype(F32) + carried * entry
-            before_low = before.astype(BF16)
-            adj = adj_ref[h]
-            adj_low = adj.astype(BF16)
-            kept = total * adj
-            through = jnp.sum(kept * before, axis=0, keepdims=True)
-            throughs.append(jnp.sum(through, axis=1, keepdims=True))
-            pairs = jnp.where(causal, jnp.exp(decay + grow_row(0, h)), 0.0)
-            keys_and_state = jnp.concatenate([kf, before_low], axis=0)
-            raw_and_far = nt(qf, keys_and_state)
-            raw = raw_and_far[:, :C]
-            weights = (raw * pairs).astype(BF16)
-            draw = dweights[:, C * j : C * (j + 1)].astype(BF16).astype(F32) * pairs
-            draw_low = draw.astype(BF16)
-            both = (raw * draw).astype(BF16)
-            a_lift = (a * lift).astype(BF16)
-            v_coef = (values[j] * coef).astype(BF16)
-            dq = nn(jnp.concatenate([draw_low, a_lift], axis=1), keys_and_state)
-            dk = nn(
-                jnp.concatenate([draw_low.T, v_coef], axis=1),
-                jnp.concatenate([qf, adj_low], axis=0),
-            )
-            dv_far = coef * nt(kf, adj_low)
-            dv = tn(weights, a_low) + dv_far
-            x_far = (a * lift * raw_and_far[:, C:]).astype(BF16)
-            x_parts.append(jnp.concatenate([both, x_far], axis=1))
-            y_parts.append(
-                jnp.concatenate(
-                    [(values[j] * dv_far).astype(BF16), (values[j] * dv).astype(BF16)], axis=1
-                )
-            )
-            adj_ref[h] = kept + tn(a_lift, qf)
-            for feats, grad, angle in ((qf, dq, angle_q), (kf, dk, angle_k)):
-                f = feats.astype(F32)
-                angle.append(grad[:, :LANES] * f[:, LANES:] - grad[:, LANES:] * f[:, :LANES])
-            dvs.append(dv)
-        upto = nn(jnp.concatenate(x_parts, axis=0), pair_sums)
-        ends = nn(jnp.concatenate(y_parts, axis=0), two_sums)
-        for j in range(2):
-            h = 2 * p + j
-            rows = slice(C * j, C * (j + 1))
-            flow = jnp.where(causal, upto[rows], ends[rows, :C])
-            flow = jnp.sum(flow, axis=0, keepdims=True) + throughs[j]
-            own = jnp.sum(jnp.where(row == col, ends[rows, C:], 0.0), axis=0, keepdims=True)
-            dlogit[g, h : h + 1, here] = grow_row(3, h) * flow - grow_row(2, h) * own
-        angles = jnp.concatenate(
-            [jnp.concatenate(angle_q, axis=1), jnp.concatenate(angle_k, axis=1)], axis=0
         )
-        du = nt(angles.astype(BF16), proj_ref[p])
+        dvs.append(tn(weights[k], a_lows[k]))
+        if items[k][0] == 0:
+            adj_ref[items[k][1]] += tn(a_lifts[k], qfs[k])
+    x_parts, y_parts = [], []
+    for k in numbers:
+        dv_far = coefs[k] * dv_fars[k]
+        dvs[k] = dvs[k] + dv_far
+        x_far = (a_lows[k].astype(F32) * lifts[k] * fars[k]).astype(BF16)
+        x_parts.append(jnp.concatenate([boths[k], x_far], axis=1))
+        y_far = (values[k] * dv_far).astype(BF16)
+        y_parts.append(jnp.concatenate([y_far, (values[k] * dvs[k]).astype(BF16)], axis=1))
+    upto = nn(jnp.concatenate(x_parts, axis=0), pair_sums)
+    ends = nn(jnp.concatenate(y_parts, axis=0), two_sums)
+    dus = []
+    for p in pairs_of_heads:
+        angles = []
+        for feats, grads in ((qfs, dqs), (kfs, dks)):
+            for u in range(span):
+                row_angles = []
+                for k, item in enumerate(items):
+                    if item[0] == u and item[1] // 2 == p:
+                        f, grad = feats[k].astype(F32), grads[k]
+                        row_angles.append(
+                            grad[:, :LANES] * f[:, LANES:] - grad[:, LANES:] * f[:, :LANES]
+                        )
+                angles.append(jnp.concatenate(row_angles, axis=1))
+        dus.append(nt(jnp.concatenate(angles, axis=0).astype(BF16), proj_ref[p]))
+    for k, (u, h) in enumerate(items):
+        rows = slice(C * k, C * (k + 1))
+        flow = jnp.where(causal, upto[rows], ends[rows, :C])
+        flow = jnp.sum(flow, axis=0, keepdims=True) + throughs[k]
+        own = jnp.sum(jnp.where(row == col, ends[rows, C:], 0.0), axis=0, keepdims=True)
+        stay, leave = grow_row(2, h)[:, rows_of[u]], grow_row(3, h)[:, rows_of[u]]
+        at = pl.ds(pl.multiple_of(first_row + C * u, C), C)
+        dlogit[g, h : h + 1, at] = leave * flow - stay * own
+    for p, lanes in enumerate(lanes_of):
         u = jnp.concatenate([uq_ref[:, lanes], uk_ref[:, lanes]], axis=0).astype(F32)
         scale = jnp.concatenate([rq_ref[:, lanes], rk_ref[:, lanes]], axis=0)
-        along = nn((u * du).astype(BF16), block_ones())
-        dqk = ((2.0 * math.pi) * scale * (du - u * along)).astype(BF16)
-        width = hg * 64
-        dqkv[g, here, LANES * p : LANES * (p + 1)] = dqk[:C]
-        dqkv[g, here, width + LANES * p : width + LANES * (p + 1)] = dqk[C:]
-        dqkv[g, here, 2 * width + LANES * p : 2 * width + LANES * (p + 1)] = jnp.where(
-            lower, dvs[0], dvs[1]
-        ).astype(BF16)
+        along = nn((u * dus[p]).astype(BF16), block_ones())
+        dqk = ((2.0 * math.pi) * scale * (dus[p] - u * along)).astype(BF16)
+        dqkv[g, here, LANES * p : LANES * (p + 1)] = dqk[: span * C]
+        dqkv[g, here, width + LANES * p : width + LANES * (p + 1)] = dqk[span * C :]
+        for k, (u, h) in enumerate(items):
+            if h == 2 * p:
+                at = pl.ds(pl.multiple_of(first_row + C * u, C), C)
+                dqkv[g, at, 2 * width + LANES * p : 2 * width + LANES * (p + 1)] = jnp.where(
+                    lower, dvs[k], dvs[k + 1]
+                ).astype(BF16)
 
     @pl.when(i == chunks - 1)
     def _():
@@ -1045,7 +1091,7 @@
         for k in range(len(loads) - 6, len(loads)):
             if k != len(loads) - 4:
                 load(k).wait()
-        tokens = chunks * C
+        tokens = chunks * span * C
         block = min(T, tokens)
         small = small_src if comm else small_ref
         rows8 = jnp.concatenate(
@@ -1070,12 +1116,12 @@
                         ref[:, hg * 64 * k : hg * 64 * (k + 1)],
                     )
             xhat, scale = normalize(x_ref[rows, :].astype(F32))
-            small[2 * heads : 2 * heads + 1, :] += jnp.sum(
+            small[heads + 1 : heads + 2, :] += jnp.sum(
                 mixer_grad * xhat, axis=0, keepdims=True
             )
-            small[2 * heads + 1 : 2 * heads + 2, :] += jnp.sum(mixer_grad, axis=0, keepdims=True)
+            small[heads + 2 : heads + 3, :] += jnp.sum(mixer_grad, axis=0, keepdims=True)
             dx_ref[rows, :] = mg_ref[rows, :] + normalize_back(mixer_grad, gain, xhat, scale)
-            if comm:
+            if comm and b % 2 == 1 and b + 1 < tokens // block:
                 advance(now)
                 now += 1
         if comm:
@@ -1087,10 +1133,11 @@
             board.drain()
 
 
-OS_TICKS = (2, 4, 7, 9, 11, 14, 16)
-F_TICKS = (6, 8, 10, 12)
-W_TICKS = (8, 10, 12, 14, 16, 18, 20)
+OS_TICKS = (1, 3, 6, 8, 9, 10, 11)
+F_TICKS = (2, 4, 6, 8)
+W_TICKS = (4, 6, 8, 9, 10, 11, 12)
 W_PIECES = 3
+SUM_ROWS = 16
 
 
 def back_plans(os, f, w, small):
@@ -1134,12 +1181,13 @@
     )(*[array for array, _, _ in ins])
 
 
-def finish_kernel(u_ref, late_ref, w_ref, os_ref, up_ref, down_ref, q_ref, k_ref, v_ref, o_ref, s_ref):
-    hb = u_ref.shape[2]
+def finish_kernel(
+    late_ref, w_ref, os_ref, up_ref, down_ref, q_ref, k_ref, v_ref, o_ref, s_ref
+):
+    hb = late_ref.shape[3]
     for part, ref in enumerate((up_ref, down_ref)):
-        ref[:, 0:hb] = u_ref[part].astype(F32)
         for k in range(late_ref.shape[0]):
-            ref[:, hb * (k + 1) : hb * (k + 2)] = late_ref[k, part].astype(F32)
+            ref[:, hb * k : hb * (k + 1)] = late_ref[k, part].astype(F32)
     groups, _, lanes = w_ref.shape
     each = lanes // 3
     for part, ref in enumerate((q_ref, k_ref, v_ref)):
@@ -1151,19 +1199,18 @@
         s_ref[k] = os_ref[64 * k : 64 * (k + 1), width:].astype(F32).T
 
 
-def finish(heads, sum_u, sum_late, sum_w, out_state, small):
+def finish(heads, sum_late, sum_w, out_state):
     width = sum_w.shape[1]
     steps = 4
     rows = width // steps
     late, _, hb = sum_late.shape
     feats = out_state.shape[1] - width
     square = ((width, width), F32, (rows, width), lambda i: (i, 0))
-    wide = ((width, (late + 1) * hb), F32, (rows, (late + 1) * hb), lambda i: (i, 0))
+    wide = ((width, late * hb), F32, (rows, late * hb), lambda i: (i, 0))
     return call(
         finish_kernel,
         (steps,),
         [
-            (sum_u.reshape(2, width, hb), (2, rows, hb), lambda i: (0, i, 0)),
             (sum_late.reshape(late, 2, width, hb), (late, 2, rows, hb), lambda i: (0, 0, i, 0)),
             (sum_w, (sum_w.shape[0], rows, sum_w.shape[2]), lambda i: (0, i, 0)),
             (out_state, (rows, width + feats), lambda i: (i, 0)),
@@ -1305,8 +1352,8 @@
             vmem(*pay_shape),
             vmem(*pay_shape),
             vmem(1, shard_width, dtype=F32),
-            pltpu.SemaphoreType.DMA((6,)),
-            pltpu.SemaphoreType.DMA((6,)),
+            pltpu.SemaphoreType.DMA((8,)),
+            pltpu.SemaphoreType.DMA((8,)),
         ]
     else:
         outs += [keep(pay_shape, BF16), keep((8, LANES), F32)]
@@ -1387,21 +1434,18 @@
     if comm:
         plans = feed_plans(hb)
         outs += [
-            result((2 * width, hb), BF16),
-            *[keep((plan.left, hb), BF16) for plan in plans[1:]],
+            *[keep((plan.left, hb), BF16) for plan in plans],
             keep((width, width + 2 * feats), BF16),
             keep((16, width), F32),
             keep(pay_shape, BF16),
         ]
         scratch += [
             vmem(pairs, 4 * width, hb),
-            vmem(2 * width, hb),
             vmem(shards, 1, shard_width, dtype=F32),
             vmem(*pay_shape),
             vmem(*pay_shape),
             pltpu.SemaphoreType.DMA,
             pltpu.SemaphoreType.DMA,
-            pltpu.SemaphoreType.DMA((pairs,)),
         ]
         for plan in plans:
             scratch += plan.scratch()
@@ -1425,8 +1469,8 @@
     )
     out, mg, a = found[:3]
     if comm:
-        sum_u, *u_late = found[3:7]
-        out_state, flat, after = found[7:]
+        u_late = found[3:-3]
+        out_state, flat, after = found[-3:]
     else:
         up_grad, down_grad, upb_grad, output_grad, adj_final, feed_sums = found[3:]
         after = carry_over(adj_final, logs, False)
@@ -1441,9 +1485,11 @@
 
     hg = GROUP_HEADS
     groups = heads // hg
+    span = min(SPAN, chunks)
+    blocks = chunks // span
 
     def back_rows(n, per_group=True):
-        return (C, n), lambda g, i: (chunks - 1 - i, g if per_group else 0)
+        return (span * C, n), lambda g, i: (blocks - 1 - i, g if per_group else 0)
 
     def per_group(array, *shape):
         zeros = (0,) * (len(shape) - 1)
@@ -1465,8 +1511,8 @@
         (rk,) + back_rows(hg * size),
         (a,) + back_rows(hg * LANES),
         (gcol,) + back_rows(LANES, False),
-        (grow, (4 * heads, C), lambda g, i: (0, chunks - 1 - i)),
-        (before, (1, hg, LANES, 2 * feats), lambda g, i: (chunks - 1 - i, g, 0, 0)),
+        (grow, (4 * heads, span * C), lambda g, i: (0, blocks - 1 - i)),
+        (before, (span, hg, LANES, 2 * feats), lambda g, i: (blocks - 1 - i, g, 0, 0)),
     ]
     ins += states(entry) + states(after)
     ins += [
@@ -1480,7 +1526,7 @@
         const(gate_weight),
         const(mixer_gain),
     ]
-    w_shape, small_shape = (groups, width, 3 * hg * size), (32, width)
+    w_shape, small_shape = (groups, width, 3 * hg * size), (16, width)
 
     def sums(shape, dtype):
         return result(shape, dtype) if comm else keep(shape, dtype)
@@ -1496,7 +1542,7 @@
         vmem(width, width),
         vmem(width, width),
         vmem(width, width),
-        pltpu.SemaphoreType.DMA((11,)),
+        pltpu.SemaphoreType.DMA((12,)),
         vmem(hg // 2, LANES, 2 * feats),
     ]
     if comm:
@@ -1525,8 +1571,8 @@
         for plan in plans:
             scratch += plan.scratch()
     found = call(
-        partial(back_kernel, heads, hg, chunks, comm),
-        (groups, chunks),
+        partial(back_kernel, heads, hg, span, blocks, comm),
+        (groups, blocks),
         ins,
         outs,
         scratch,
@@ -1536,7 +1582,7 @@
     dx, sum_w, small = found[:3]
     if comm:
         sum_late, out_state, flat = found[3:]
-        results = finish(heads, sum_u, sum_late, sum_w, out_state, small)
+        results = finish(heads, sum_late, sum_w, out_state)
         sum_up, sum_down, sum_q, sum_k, sum_v, sum_o, sum_state = results
         sum_feed = flat[0:3]
         sum_upb = flat[3 : 3 + hidden // width].reshape(-1)
@@ -1557,8 +1603,8 @@
     return (
         out.reshape(inputs.shape),
         dx.reshape(inputs.shape),
-        small[2 * heads],
-        small[2 * heads + 1],
+        small[heads + 1],
+        small[heads + 2],
         sum_q,
         sum_k,
         sum_v,

time: 205 us -> 172 us (0.84)
  Pallas kernels: 189 us -> 157 us
    pallas_call x4, Pallas kernels: 189 us -> 157 us  [call(): pl.pallas_call(kernel, grid=grid, in_specs=[spec(array.shape, block, inde...]
    unnamed x12 -> x14, local copies, waits for them, and re-layouts: 9.22 us -> 9.08 us
where the time goes in v5:
time: 172 us; the launch traced here: 171 us
  Pallas kernels  157 us (91%)
  local copies, waits for them, and re-layouts  12.2 us (7%)
    pallas_call x4, Pallas kernels, call(): pl.pallas_call(kernel, grid=grid, in_specs=[spec(array.shape, block, inde...  157 us
    unnamed x14, local copies, waits for them, and re-layouts  9.08 us

profile of v5, /device:TPU:0, one launch (start us, length us, event | category | flops | bytes accessed | tf_op | source)
XLA Modules:
  0.0 171.5 jit_solution(7369076817278237971)
XLA Ops:
  0.7 1.5 copy.37.refs_6_.refs_22_
  2.1 2.4 %copy.38.refs_9_ = f32[8,256,64]{2,1,0:T(8,128)} copy(f32[8,256,64]{1,2,0:T(8,128)} %param.30) | data formatting | bytes 1048576 | tf_op args[11]
  4.5 1.3 broadcast_in_dim.28
  5.8 34.6 %features.1 = (bf16[1024,512]{1,0:T(8,128)(2,1)}, bf16[1024,512]{1,0:T(8,128)(2,1)}, bf16[1024,512]{1,0:T(8,128)(2,1)}, f32[1024,512]{1,0:T(8,128)}, f32[1024,51...) custom-call(bf16[1024,512]{1,0:T(8,128)(2,1)} %bitcast.23, ...), custom_call_target="tpu_custom_call" | custom-call | tf_op jit(solution)/shard_map/features/pallas_call | solution.py:1170
  40.4 49.7 %feed.1 = (bf16[1024,512]{1,0:T(8,128)(2,1)}, f32[1024,512]{1,0:T(8,128)}, bf16[1024,1024]{1,0:T(8,128)(2,1)}, bf16[64,256]{1,0:T(8,128)(2,1)}, bf16[256,256]{1,...) custom-call(bf16[1024,512]{1,0:T(8,128)(2,1)} %bitcast.24, ...), custom_call_target="tpu_custom_call" | custom-call | tf_op jit(solution)/shard_map/feed/pallas_call | solution.py:1170
  90.1 66.7 %back.1 = (f32[1024,512]{1,0:T(8,128)}, bf16[2,512,768]{2,1,0:T(8,128)(2,1)}, f32[16,512]{1,0:T(8,128)}, bf16[4,1024,256]{2,1,0:T(8,128)(2,1)}, bf16[512,768]{1,0:T(8,128)(2,1)}, /*index=5*/f32[16,512]{1,0:T(8,128)}) custom-call(bf16[1024,2048]{1,0:T(8,128)(2,1)} %get-tuple-element.57.refs_1_.refs_0_, bf16[1024,2048]{1,0:T(8,128)(2,1)} %get-tuple-element.65.refs_1_, ...), custom_call_target="tpu_custom_call" | custom-call | tf_op jit(solution)/shard_map/back/pallas_call | solution.py:1170
  156.8 1.4 fusion
  158.3 0.0 copy-start.3
  158.3 0.0 copy-start.2
  158.3 0.0 copy-start.1
  158.3 6.2 %finish.1 = (f32[512,1024]{1,0:T(8,128)}, f32[512,1024]{1,0:T(8,128)}, f32[512,512]{1,0:T(8,128)}, f32[512,512]{1,0:T(8,128)}, f32[512,512]{1,0:T(8,128)}, /*index=5*/f32[512,512]{1,0:T(8,128)}, f32[8,256,64]{2,1,0:T(8,128)}) custom-call(bf16[4,2,512,256]{3,2,1,0:T(8,128)(2,1)} %bitcast.27, bf16[2,512,768]{2,1,0:T(8,128)(2,1)} %get-tuple-element.86.w_ref, ...), custom_call_target="tpu_custom_call" | custom-call | tf_op jit(solution)/shard_map/finish/pallas_call | solution.py:1170
  164.5 0.0 copy-start
  164.5 0.0 copy-done.3
  164.5 0.6 slice_bitcast_fusion
  165.1 0.5 slice_bitcast_fusion.1
  165.6 2.3 %copy.40 = f32[8,256,64]{1,2,0:T(8,128)} copy(f32[8,256,64]{2,1,0:T(8,128)} %get-tuple-element.106) | data formatting | bytes 1048576
  168.0 0.0 copy-done.2
  168.0 0.6 slice.43
  168.6 0.6 copy.41
  169.2 0.0 copy-done.1
  169.2 1.0 copy.44
  170.2 0.0 copy-done
  170.2 1.3 copy.45
  (1 shorter events, 0.0 us)
Async XLA Ops:
  158.3 6.3 %copy-start.3 = (f32[16,512]{1,0:T(8,128)S(1)}, f32[16,512]{1,0:T(8,128)}, u32[]{:S(2)}) copy-start(f32[16,512]{1,0:T(8,128)} %get-tuple-element.84) | copy-start | bytes 98308
  158.3 9.7 %copy-start.2 = (f32[16,512]{1,0:T(8,128)S(1)}, f32[16,512]{1,0:T(8,128)}, u32[]{:S(2)}) copy-start(f32[16,512]{1,0:T(8,128)} %get-tuple-element.93) | copy-start | bytes 98308
  158.3 10.9 %copy-start.1 = (bf16[1024,512]{1,0:T(8,128)(2,1)S(1)}, bf16[1024,512]{1,0:T(8,128)(2,1)}, u32[]{:S(2)}) copy-start(bf16[1024,512]{1,0:T(8,128)(2,1)} %get-tuple-element.64) | copy-start | bytes 3145732
  164.5 5.7 %copy-start = (f32[1024,512]{1,0:T(8,128)S(1)}, f32[1024,512]{1,0:T(8,128)}, u32[]{:S(2)}) copy-start(f32[1024,512]{1,0:T(8,128)} %get-tuple-element.83) | copy-start | bytes 6291460

commit v6 on v5

--- a/solution.py
+++ b/solution.py
@@ -18,9 +18,10 @@
 
 C = 128
 T = 256
+FEED_ROWS = 512
 HB = 256
 INNER_HEADS = 8
-WEIGHT_STEPS = (4, 6, 8, 11)
+WEIGHT_STEPS = (2, 3, 5, 8)
 SPAN = 2
 GROUP_HEADS = 4
 LANES = 128
@@ -340,11 +341,6 @@
     return diagonal(highs), diagonal(rests)
 
 
-def gate_rows(wg):
-    eye = jnp.where(iota((16, wg.shape[1]), 0) == iota((16, wg.shape[1]), 1), 1.0, 0.0)
-    return nt(eye.astype(BF16), wg).astype(BF16)
-
-
 class Taker:
     def __init__(self, refs):
         self.refs = list(refs)
@@ -389,7 +385,7 @@
                 self.store(k).wait()
 
 
-def features_kernel(heads, chunks, comm, *refs):
+def features_kernel(heads, span, blocks, comm, *refs):
     take = Taker(refs)
     x_ref, gain_ref, bias_ref, wq_ref, wk_ref, wv_ref = take(6)
     gate_ref, gb_smem, proj_ref, start_ref, start_norm_ref = take(5)
@@ -401,9 +397,10 @@
     else:
         final_ref, total_ref = take(2)
     state, carry, qf_s, kf_s, v_s, gcol_s, grow_s, before_s = take(8)
-    wg_ref, wgt_ref, gb_ref, gbt_ref, pcat_ref = take(5)
+    wg_ref, gb_ref, gbt_ref, pcat_ref = take(4)
     step = pl.program_id(0)
-    chunk = lax.rem(step, chunks)
+    chunks = span * blocks
+    full = span * C
 
     if comm:
         sent, landed, upb_landed, sends, recvs = take(5)
@@ -446,12 +443,12 @@
             for k in (6, 0, 1):
                 remote(k, True).start()
 
-        @pl.when(step == chunks)
+        @pl.when(step == blocks)
         def _():
             remote(7, True).start()
 
         for k, ready in zip(range(4), WEIGHT_STEPS):
-            @pl.when(step == ready * chunks // 8)
+            @pl.when(step == ready)
             def _(k=k):
                 remote(k, False).wait_recv()
                 remote(k + 2, True).start()
@@ -460,10 +457,8 @@
     def _():
         carry[...] = jnp.zeros_like(carry)
         is_first = lax.axis_index("seq") == 0
-        wg = gate_ref[...]
-        spread = jnp.where(iota((heads, LANES), 0) == iota((heads, LANES), 1) % heads, 1.0, 0.0)
-        wg_ref[...] = nn(wg, spread.astype(BF16)).astype(BF16)
-        wgt_ref[...] = gate_rows(wg)[0:heads]
+        spread = jnp.where(iota((LANES, heads), 0) % heads == iota((LANES, heads), 1), 1.0, 0.0)
+        wg_ref[...] = nn(spread.astype(BF16), gate_ref[...]).astype(BF16)
         lane_head = iota((1, LANES), 1) % heads
         row_head = iota((heads, LANES), 0)
         gb = jnp.zeros((1, LANES), F32)
@@ -471,7 +466,7 @@
         for h in range(heads):
             gb = jnp.where(lane_head == h, gb_smem[h], gb)
             gbt = jnp.where(row_head == h, gb_smem[h], gbt)
-            begin = start_ref[h].T
+            begin = start_ref[h]
             norm = jnp.broadcast_to(start_norm_ref[h : h + 1, :], begin.shape)
             both = [begin, norm] if h % 2 == 0 else [norm, begin]
             state[h] = jnp.where(is_first, jnp.concatenate(both, axis=0), 0.0)
@@ -485,7 +480,7 @@
 
     lower = lower_half((C, LANES))
 
-    @pl.when(step < chunks)
+    @pl.when(step < blocks)
     def _():
         xhat, _ = normalize(x_ref[...].astype(F32))
         ml = (xhat * gain_ref[...] + bias_ref[...]).astype(BF16)
@@ -495,37 +490,11 @@
         v = nn(ml, wv_ref[...])
         v_low = v.astype(BF16)
         v_ref[...] = v_low
-        v_s[chunk] = v_low
-        logit = nn(ml, wg_ref[...]) + gb_ref[...]
+        rows_of = [slice(C * u, C * (u + 1)) for u in range(span)]
+        logit = nt(ml, wg_ref[...]) + gb_ref[...]
         keep = log_sigmoid(logit)
-        gain_in = keep - logit
-        decay = rows_up_to(keep)
-        total = decay[C - 1 : C, :]
-        group = iota((C, LANES), 1) // 8
-        coef = total - decay + gain_in
-        packed = jnp.where(group == 0, decay, coef)
-        packed = jnp.where(group == 2, carry[...] + decay, packed)
-        packed = jnp.where(group == 6, jnp.broadcast_to(carry[...], (C, LANES)), packed)
-        packed = jnp.where(group == 7, jnp.broadcast_to(total, (C, LANES)), packed)
-        gcol_ref[...] = packed
-        gcol_s[chunk] = packed
-        carry[...] = carry[...] + total
-        if not comm:
-            total_ref[...] = jnp.broadcast_to(carry[...], total_ref.shape)
-        logit_row = nt(wgt_ref[...], ml) + gbt_ref[...][:, 0:1]
+        logit_row = nt(gate_ref[...], ml) + gbt_ref[...][:, 0:1]
         keep_row = log_sigmoid(logit_row)
-        decay_row = lanes_up_to(keep_row)
-        rows = jnp.concatenate(
-            [
-                keep_row - logit_row - decay_row,
-                decay_row,
-                jax.nn.sigmoid(logit_row),
-                jax.nn.sigmoid(-logit_row),
-            ],
-            axis=0,
-        )
-        grow_ref[...] = rows
-        grow_s[chunk] = rows
 
         ftr_scale = 1.0 / math.sqrt(LANES)
         pairs = range(heads // 2)
@@ -537,11 +506,38 @@
             unit = boths[p] * scales[p]
             high = unit.astype(BF16)
             rest = (unit - high.astype(F32)).astype(BF16)
-            uq_ref[:, lanes_of[p]] = high[:C]
-            uk_ref[:, lanes_of[p]] = high[C:]
-            rq_ref[:, lanes_of[p]] = scales[p][:C]
-            rk_ref[:, lanes_of[p]] = scales[p][C:]
+            uq_ref[:, lanes_of[p]] = high[:full]
+            uk_ref[:, lanes_of[p]] = high[full:]
+            rq_ref[:, lanes_of[p]] = scales[p][:full]
+            rk_ref[:, lanes_of[p]] = scales[p][full:]
             all_turns.append(nn(jnp.concatenate([high, rest, high], axis=1), pcat_ref[p]))
+        coefs, totals = [], []
+        group = iota((C, LANES), 1) // 8
+        for u, rows in enumerate(rows_of):
+            decay = rows_up_to(keep[rows])
+            total = decay[C - 1 : C, :]
+            coef = total - decay + keep[rows] - logit[rows]
+            packed = jnp.where(group == 0, decay, coef)
+            packed = jnp.where(group == 2, carry[...] + decay, packed)
+            packed = jnp.where(group == 6, jnp.broadcast_to(carry[...], (C, LANES)), packed)
+            packed = jnp.where(group == 7, jnp.broadcast_to(total, (C, LANES)), packed)
+            gcol_ref[rows, :] = packed
+            gcol_s[span * step + u] = packed
+            carry[...] = carry[...] + total
+            coefs.append(coef)
+            totals.append(total)
+            gate_rows = jnp.concatenate(
+                [
+                    keep_row[:, rows] - logit_row[:, rows] - lanes_up_to(keep_row[:, rows]),
+                    jax.nn.sigmoid(logit_row[:, rows]),
+                    jax.nn.sigmoid(-logit_row[:, rows]),
+                ],
+                axis=0,
+            )
+            grow_ref[:, rows] = gate_rows
+            grow_s[span * step + u] = gate_rows
+        if not comm:
+            total_ref[...] = jnp.broadcast_to(carry[...], total_ref.shape)
         for p in pairs:
             s, c = sin_cos(all_turns[p], ftr_scale)
             s = s.astype(BF16)
@@ -551,25 +547,29 @@
                 half_lanes = slice(LANES * j, LANES * (j + 1))
                 feats = jnp.concatenate([s[:, half_lanes], c[:, half_lanes]], axis=1)
                 place = slice(256 * h, 256 * (h + 1))
-                qf_ref[:, place] = feats[:C]
-                qf_s[chunk, :, place] = feats[:C]
-                kf = feats[C:]
-                kf_ref[:, place] = kf
-                kf_s[chunk, :, place] = kf
-                values = jnp.where(mine(h, lower), v[:, lanes_of[p]], 1.0)
-                weighted = (values * jnp.exp(column(coef, h, C, LANES))).astype(BF16)
-                now = state[h]
-                now_low = now.astype(BF16)
-                before_ref[0, h] = now_low
-                before_s[chunk, h] = now_low
-                state[h] = jnp.exp(total[:, h : h + 1]) * now + tn(weighted, kf)
-
-    @pl.when(step == chunks - 1)
+                qf_ref[:, place] = feats[:full]
+                kf_ref[:, place] = feats[full:]
+                for u, rows in enumerate(rows_of):
+                    at = span * step + u
+                    kf = feats[full + C * u : full + C * (u + 1)]
+                    qf_s[at, :, place] = feats[rows]
+                    kf_s[at, :, place] = kf
+                    v_s[at, :, lanes_of[p]] = v_low[rows, lanes_of[p]]
+                    values = jnp.where(mine(h, lower), v[rows, lanes_of[p]], 1.0)
+                    weighted = values * jnp.exp(column(coefs[u], h, C, LANES))
+                    now = state[h]
+                    now_low = now.astype(BF16)
+                    before_ref[u, h] = now_low
+                    before_s[at, h] = now_low
+                    state[h] = jnp.exp(totals[u][:, h : h + 1]) * now + tn(weighted.astype(BF16), kf)
+
+    @pl.when(step == blocks - 1)
     def _():
         pack_states([state[h] for h in range(heads)], sent if comm else final_ref)
 
-    @pl.when(step >= chunks)
+    @pl.when(step >= blocks)
     def _():
+        chunk = step - blocks
         causal = iota((C, C), 0) >= iota((C, C), 1)
         gcol = gcol_s[chunk]
         for first in range(0, heads, INNER_HEADS):
@@ -593,7 +593,7 @@
                 )
 
     if comm:
-        @pl.when(step == 2 * chunks - 1)
+        @pl.when(step == blocks + chunks - 1)
         def _():
             for k in (4, 5, 6, 7):
                 remote(k, False).wait_recv()
@@ -723,11 +723,12 @@
             )
         else:
             upb = jnp.concatenate([upb_ref[shard, :, cols] for shard, cols in blocks], axis=1)
-        for r in range(tokens // rows):
-            if comm and r % 2 == 0:
-                for k in range(pairs):
-                    pl.when(j == k)(partial(board.advance, 2 * k + r // 2))
-            here = slice(rows * r, rows * (r + 1))
+        if comm:
+            for k in range(pairs):
+                pl.when(j == k)(partial(board.advance, 2 * k))
+        many = min(FEED_ROWS, tokens)
+        for r in range(tokens // many):
+            here = slice(many * r, many * (r + 1))
             feed_low = fl_s[here, :]
             pre = nn(feed_low, up) + upb
             pre_grad = nn(dout_s[here, :], down)
@@ -830,7 +831,7 @@
 
 U_SCATTER, U_GATHER = ("core", "xr", "y", "z"), ("z", "y", "core")
 FEED_STAGES = (4, 3, 2, 1)
-FEED_TICKS = ((2, 3, 6, 8, 11), (4, 6, 9, 12), (6, 8, 12), (8, 10))
+FEED_TICKS = ((2, 4, 6, 8, 11), (4, 6, 9, 12), (6, 8, 12), (8, 10))
 BACK_TICKS = ((2, 4, 6, 7), (1, 3, 5, 7, 8), (1, 3, 5, 7, 8, 9), (1, 3, 5, 7, 8, 9, 10))
 
 
@@ -888,11 +889,7 @@
                 ticks.append(ticks[-1] + gap)
             return ticks
 
-        for j, (plan, ticks) in enumerate(zip(late_plans(usum_ref.shape[2]), BACK_TICKS)):
-            board.add(plan, u_refs[j], usum_ref.at[j], usum_hbm.at[j], ticks)
-        board.add(plans["os"], os_ref, ossum_ref, ossum_hbm, OS_TICKS)
-        board.add(plans["f"], f_ref, fsum_ref, fsum_hbm, F_TICKS)
-        for k in range(groups):
+        for k in reversed(range(groups)):
             final = k + 1 == groups
             pieces = W_PIECES if final else 1
             lanes_each = w_src.shape[2] // pieces
@@ -903,8 +900,14 @@
                     w_src.at[k, :, lanes],
                     wsum_ref.at[k, :, lanes],
                     w_ref.at[k, :, lanes],
-                    [last + 1 + i for i in range(7)] if final else W_TICKS,
+                    [last + 1 + i for i in range(7)]
+                    if final
+                    else [(k + 1) * chunks + gap for gap in W_GAPS],
                 )
+        for j, (plan, ticks) in enumerate(zip(late_plans(usum_ref.shape[2]), BACK_TICKS)):
+            board.add(plan, u_refs[j], usum_ref.at[j], usum_hbm.at[j], ticks)
+        board.add(plans["os"], os_ref, ossum_ref, ossum_hbm, OS_TICKS)
+        board.add(plans["f"], f_ref, fsum_ref, fsum_hbm, F_TICKS)
         advance = board.advance
 
     def load(k):
@@ -1055,7 +1058,7 @@
         flow = jnp.where(causal, upto[rows], ends[rows, :C])
         flow = jnp.sum(flow, axis=0, keepdims=True) + throughs[k]
         own = jnp.sum(jnp.where(row == col, ends[rows, C:], 0.0), axis=0, keepdims=True)
-        stay, leave = grow_row(2, h)[:, rows_of[u]], grow_row(3, h)[:, rows_of[u]]
+        stay, leave = grow_row(1, h)[:, rows_of[u]], grow_row(2, h)[:, rows_of[u]]
         at = pl.ds(pl.multiple_of(first_row + C * u, C), C)
         dlogit[g, h : h + 1, at] = leave * flow - stay * own
     for p, lanes in enumerate(lanes_of):
@@ -1103,12 +1106,11 @@
         small[0:heads, :] = nn(rows8, ml_ref[...])[0:heads]
         bias_sum = nt(jnp.ones(rows8.shape, BF16), rows8)[0:1]
         small[heads : heads + 1, 0:16] = bias_sum
-        gate_low = gate_rows(gate_ref[...])
         gain = gain_ref[...]
         now = last + 2
         for b in range(tokens // block):
             rows = slice(block * b, block * (b + 1))
-            mixer_grad = tn(rows8[:, rows], gate_low)
+            mixer_grad = tn(rows8[0:heads, rows], gate_ref[...])
             for k in range(groups):
                 for j, ref in enumerate((wq_ref, wk_ref, wv_ref)):
                     mixer_grad = mixer_grad + nt(
@@ -1133,9 +1135,9 @@
             board.drain()
 
 
-OS_TICKS = (1, 3, 6, 8, 9, 10, 11)
-F_TICKS = (2, 4, 6, 8)
-W_TICKS = (4, 6, 8, 9, 10, 11, 12)
+OS_TICKS = (1, 3, 5, 7, 8, 9, 10)
+F_TICKS = (5, 7, 8, 9)
+W_GAPS = (0, 2, 4, 5, 6, 7, 8)
 W_PIECES = 3
 SUM_ROWS = 16
 
@@ -1196,7 +1198,7 @@
     width = o_ref.shape[1]
     o_ref[...] = os_ref[:, 0:width].astype(F32)
     for k in range(s_ref.shape[0]):
-        s_ref[k] = os_ref[64 * k : 64 * (k + 1), width:].astype(F32).T
+        s_ref[k] = os_ref[64 * k : 64 * (k + 1), width:].astype(F32)
 
 
 def finish(heads, sum_late, sum_w, out_state):
@@ -1216,7 +1218,7 @@
             (out_state, (rows, width + feats), lambda i: (i, 0)),
         ],
         [wide, wide, square, square, square, square]
-        + [((heads, feats, 64), F32, (heads // steps, feats, 64), lambda i: (i, 0, 0))],
+        + [((heads, 64, feats), F32, (heads // steps, 64, feats), lambda i: (i, 0, 0))],
         [],
         "finish",
     )
@@ -1261,11 +1263,14 @@
     _, tokens, width = inputs.shape
     heads, size, feats = projections.shape
     chunks = tokens // C
+    span = min(SPAN, chunks)
+    blocks = chunks // span
     tile = min(T, tokens)
     tiles = tokens // tile
     shards = lax.axis_size("seq")
     first = lax.axis_index("seq") == 0
     comm = (lax.axis_size("dp"), shards) == (16, 2)
+    gate_rows = gate_weight.T
     x = inputs.reshape(tokens, width)
     dout = cotangent.reshape(tokens, width)
     shard_width = up_weight.shape[1]
@@ -1292,7 +1297,7 @@
         return pltpu.VMEM(shape, dtype)
 
     def early(n):
-        return (C, n), lambda i: (jnp.minimum(i, chunks - 1), 0)
+        return (span * C, n), lambda i: (jnp.minimum(i, blocks - 1), 0)
 
     def out_early(n, dtype):
         return ((tokens, n), dtype) + early(n)
@@ -1301,28 +1306,28 @@
     ins += [const(part) for part in (mixer_gain, mixer_bias, query_weight, key_weight)]
     ins += [
         const(value_weight),
-        const(gate_weight),
+        const(gate_rows),
         (gate_bias, pl.BlockSpec(memory_space=pltpu.SMEM), None),
         const(projections),
-        const(start_state),
+        const(start_state.transpose(0, 2, 1)),
         const(start_norm),
     ]
     outs = [out_early(width, BF16)] * 3 + [out_early(width, F32)] * 2
     outs += [out_early(wider, BF16)] * 2 + [out_early(width, BF16), out_early(LANES, F32)]
     outs += [
         (
-            (4 * heads, tokens),
+            (3 * heads, tokens),
             F32,
-            (4 * heads, C),
-            lambda i: (0, jnp.minimum(i, chunks - 1)),
+            (3 * heads, span * C),
+            lambda i: (0, jnp.minimum(i, blocks - 1)),
         ),
         (
             (chunks, heads, LANES, 2 * feats),
             BF16,
-            (1, heads, LANES, 2 * feats),
-            lambda i: (jnp.minimum(i, chunks - 1), 0, 0, 0),
+            (span, heads, LANES, 2 * feats),
+            lambda i: (jnp.minimum(i, blocks - 1), 0, 0, 0),
         ),
-        ((tokens, wide), F32, (C, wide), lambda i: (jnp.maximum(i - chunks, 0), 0)),
+        ((tokens, wide), F32, (C, wide), lambda i: (jnp.maximum(i - blocks, 0), 0)),
     ]
     scratch = [
         vmem(heads, LANES, 2 * feats, dtype=F32),
@@ -1331,10 +1336,9 @@
         vmem(chunks, C, wider),
         vmem(chunks, C, width),
         vmem(chunks, C, LANES, dtype=F32),
-        vmem(chunks, 4 * heads, C, dtype=F32),
+        vmem(chunks, 3 * heads, C, dtype=F32),
         vmem(chunks, heads, LANES, 2 * feats),
-        vmem(width, LANES),
-        vmem(heads, width),
+        vmem(LANES, width),
         vmem(1, LANES, dtype=F32),
         vmem(heads, LANES, dtype=F32),
         vmem(heads // 2, 3 * LANES, 2 * feats),
@@ -1358,8 +1362,8 @@
     else:
         outs += [keep(pay_shape, BF16), keep((8, LANES), F32)]
     found = call(
-        partial(features_kernel, heads, chunks, comm),
-        (2 * chunks,),
+        partial(features_kernel, heads, span, blocks, comm),
+        (blocks + chunks,),
         ins,
         outs,
         scratch,
@@ -1485,9 +1489,6 @@
 
     hg = GROUP_HEADS
     groups = heads // hg
-    span = min(SPAN, chunks)
-    blocks = chunks // span
-
     def back_rows(n, per_group=True):
         return (span * C, n), lambda g, i: (blocks - 1 - i, g if per_group else 0)
 
@@ -1511,7 +1512,7 @@
         (rk,) + back_rows(hg * size),
         (a,) + back_rows(hg * LANES),
         (gcol,) + back_rows(LANES, False),
-        (grow, (4 * heads, span * C), lambda g, i: (0, blocks - 1 - i)),
+        (grow, (3 * heads, span * C), lambda g, i: (0, blocks - 1 - i)),
         (before, (span, hg, LANES, 2 * feats), lambda g, i: (blocks - 1 - i, g, 0, 0)),
     ]
     ins += states(entry) + states(after)
@@ -1523,7 +1524,7 @@
         hbm(query_weight),
         hbm(key_weight),
         hbm(value_weight),
-        const(gate_weight),
+        const(gate_rows),
         const(mixer_gain),
     ]
     w_shape, small_shape = (groups, width, 3 * hg * size), (16, width)
@@ -1563,10 +1564,12 @@
         scratch += [vmem(*shape, dtype=dtype) for shape, dtype in summed]
         scratch += [vmem(*w_shape), vmem(*small_shape, dtype=F32)]
         plans = back_plans(out_state.shape, flat.shape, w_shape, small_shape)
-        plans = late_plans(hb) + [
-            plans[name]
-            for name in ("os", "f") + ("w",) * (groups - 1) + ("w_last",) * W_PIECES + ("small",)
-        ]
+        first_names = ("w_last",) * W_PIECES + ("w",) * (groups - 1)
+        plans = (
+            [plans[name] for name in first_names]
+            + late_plans(hb)
+            + [plans[name] for name in ("os", "f", "small")]
+        )
         scratch += [pltpu.SemaphoreType.DMA((len(plans),))]
         for plan in plans:
             scratch += plan.scratch()
@@ -1599,7 +1602,7 @@
         )
         sum_w = sum_w.reshape(groups, width, 3, hg * size).transpose(2, 1, 0, 3)
         sum_q, sum_k, sum_v = sum_w.reshape(3, width, width).astype(F32)
-        sum_state = sum_state.reshape(heads, size, 2 * feats).astype(F32).transpose(0, 2, 1)
+        sum_state = sum_state.reshape(heads, size, 2 * feats).astype(F32)
     return (
         out.reshape(inputs.shape),
         dx.reshape(inputs.shape),
@@ -1611,7 +1614,7 @@
         small[:heads].T,
         small[heads, :heads],
         sum_o.astype(F32),
-        sum_state,
+        sum_state.transpose(0, 2, 1),
         sum_norm,
         sum_feed[0],
         sum_feed[1],

time: 172 us -> 160 us (0.930)
  local copies, waits for them, and re-layouts: 12.2 us -> 6.05 us
  Pallas kernels: 157 us -> 152 us
    unnamed x14 -> x11, local copies, waits for them, and re-layouts: 9.08 us -> 2.9 us
    pallas_call x4, Pallas kernels: 157 us -> 152 us  [call(): pl.pallas_call(kernel, grid=grid, in_specs=[spec(array.shape, block, inde...]
where the time goes in v6:
time: 160 us
  Pallas kernels  152 us (95%)
  local copies, waits for them, and re-layouts  6.05 us (4%)
    pallas_call x4, Pallas kernels, call(): pl.pallas_call(kernel, grid=grid, in_specs=[spec(array.shape, block, inde...  152 us

profile of v6, /device:TPU:0, one launch (start us, length us, event | category | flops | bytes accessed | tf_op | source)
XLA Modules:
  0.0 159.8 jit_solution(2254574458985544964)
XLA Ops:
  0.7 1.3 broadcast_in_dim.28
  1.9 32.5 %features.1 = (bf16[1024,512]{1,0:T(8,128)(2,1)}, bf16[1024,512]{1,0:T(8,128)(2,1)}, bf16[1024,512]{1,0:T(8,128)(2,1)}, f32[1024,512]{1,0:T(8,128)}, f32[1024,51...) custom-call(bf16[1024,512]{1,0:T(8,128)(2,1)} %bitcast.26, ...), custom_call_target="tpu_custom_call" | custom-call | tf_op jit(solution)/shard_map/features/pallas_call | solution.py:1172
  34.5 48.7 %feed.1 = (bf16[1024,512]{1,0:T(8,128)(2,1)}, f32[1024,512]{1,0:T(8,128)}, bf16[1024,1024]{1,0:T(8,128)(2,1)}, bf16[64,256]{1,0:T(8,128)(2,1)}, bf16[256,256]{1,...) custom-call(bf16[1024,512]{1,0:T(8,128)(2,1)} %bitcast.27, ...), custom_call_target="tpu_custom_call" | custom-call | tf_op jit(solution)/shard_map/feed/pallas_call | solution.py:1172
  83.2 64.4 %back.1 = (f32[1024,512]{1,0:T(8,128)}, bf16[2,512,768]{2,1,0:T(8,128)(2,1)}, f32[16,512]{1,0:T(8,128)}, bf16[4,1024,256]{2,1,0:T(8,128)(2,1)}, bf16[512,768]{1,0:T(8,128)(2,1)}, /*index=5*/f32[16,512]{1,0:T(8,128)}) custom-call(bf16[1024,2048]{1,0:T(8,128)(2,1)} %get-tuple-element.57.refs_1_.refs_0_, bf16[1024,2048]{1,0:T(8,128)(2,1)} %get-tuple-element.65.refs_1_, ...), custom_call_target="tpu_custom_call" | custom-call | tf_op jit(solution)/shard_map/back/pallas_call | solution.py:1172
  147.6 1.4 fusion
  149.1 0.0 copy-start.3
  149.1 0.0 copy-start.2
  149.1 0.0 copy-start.1
  149.1 6.1 %finish.1 = (f32[512,1024]{1,0:T(8,128)}, f32[512,1024]{1,0:T(8,128)}, f32[512,512]{1,0:T(8,128)}, f32[512,512]{1,0:T(8,128)}, f32[512,512]{1,0:T(8,128)}, /*index=5*/f32[512,512]{1,0:T(8,128)}, f32[8,64,256]{2,1,0:T(8,128)}) custom-call(bf16[4,2,512,256]{3,2,1,0:T(8,128)(2,1)} %bitcast.30, bf16[2,512,768]{2,1,0:T(8,128)(2,1)} %get-tuple-element.86.w_ref, ...), custom_call_target="tpu_custom_call" | custom-call | tf_op jit(solution)/shard_map/finish/pallas_call | solution.py:1172
  155.2 0.0 copy-start
  155.2 0.0 copy-done.3
  155.2 0.6 slice_bitcast_fusion
  155.8 0.5 slice_bitcast_fusion.1
  156.3 0.0 copy-done.2
  156.3 0.6 slice.43
  156.9 0.6 copy.37
  157.5 0.0 copy-done.1
  157.5 1.0 copy.40
  158.5 0.0 copy-done
  158.5 1.3 copy.41
  (1 shorter events, 0.0 us)
Async XLA Ops:
  149.1 6.1 %copy-start.3 = (f32[16,512]{1,0:T(8,128)S(1)}, f32[16,512]{1,0:T(8,128)}, u32[]{:S(2)}) copy-start(f32[16,512]{1,0:T(8,128)} %get-tuple-element.84) | copy-start | bytes 98308
  149.1 7.2 %copy-start.2 = (f32[16,512]{1,0:T(8,128)S(1)}, f32[16,512]{1,0:T(8,128)}, u32[]{:S(2)}) copy-start(f32[16,512]{1,0:T(8,128)} %get-tuple-element.93) | copy-start | bytes 98308
  149.1 8.4 %copy-start.1 = (bf16[1024,512]{1,0:T(8,128)(2,1)S(1)}, bf16[1024,512]{1,0:T(8,128)(2,1)}, u32[]{:S(2)}) copy-start(bf16[1024,512]{1,0:T(8,128)(2,1)} %get-tuple-element.64) | copy-start | bytes 3145732
  155.2 3.3 %copy-start = (f32[1024,512]{1,0:T(8,128)S(1)}, f32[1024,512]{1,0:T(8,128)}, u32[]{:S(2)}) copy-start(f32[1024,512]{1,0:T(8,128)} %get-tuple-element.83) | copy-start | bytes 6291460

commit v7 on v6

--- a/solution.py
+++ b/solution.py
@@ -403,7 +403,7 @@
     full = span * C
 
     if comm:
-        sent, landed, upb_landed, sends, recvs = take(5)
+        sent, landed, upb_own, upb_landed, sends, recvs = take(6)
         links = Links()
         core, y = links.at["core"], links.at["y"]
         part = up_hbm.shape[0] // 4
@@ -415,7 +415,7 @@
         def remote(k, sending):
             group = ("xr", "y", "core")[k // 2] if k < 6 else "xr"
             if k == 6:
-                source, lands = upb_ref, upb_landed
+                source, lands = upb_own, upb_landed
             elif k == 7:
                 source, lands = sent, landed
             else:
@@ -440,6 +440,7 @@
         @pl.when(step == 0)
         def _():
             links.greet(("core", "xr", "y"))
+            upb_own[...] = upb_ref[...].astype(F32)
             for k in (6, 0, 1):
                 remote(k, True).start()
 
@@ -599,7 +600,7 @@
                 remote(k, False).wait_recv()
             later = links.seq == 1
             entry_ref[...] = jnp.where(later, landed[...].astype(F32), 0.0).astype(BF16)
-            upbs_ref[0:1, :] = upb_ref[...]
+            upbs_ref[0:1, :] = upb_own[...]
             upbs_ref[1:2, :] = upb_landed[...]
             for k in range(8):
                 remote(k, True).wait_send()
@@ -1183,9 +1184,32 @@
     )(*[array for array, _, _ in ins])
 
 
-def finish_kernel(
-    late_ref, w_ref, os_ref, up_ref, down_ref, q_ref, k_ref, v_ref, o_ref, s_ref
-):
+def finish_kernel(heads, *refs):
+    take = Taker(refs)
+    late_ref, w_ref, os_ref, flat_ref, small_ref = take(5)
+    up_ref, down_ref, q_ref, k_ref, v_ref, o_ref, s_ref = take(7)
+    vectors, (upb_ref, norm_ref, gate_ref, gate_bias_ref) = take(5), take(4)
+
+    @pl.when(pl.program_id(0) == 0)
+    def _():
+        def spread(row, ref, first):
+            for k in range(row.shape[1] // LANES):
+                ref[first + k : first + k + 1, :] = row[:, LANES * k : LANES * (k + 1)]
+
+        flat, small = flat_ref[...], small_ref[...]
+        rows = [small[heads + 1 : heads + 2], small[heads + 2 : heads + 3]]
+        rows += [flat[k : k + 1] for k in range(3)]
+        for row, ref in zip(rows, vectors):
+            spread(row, ref, 0)
+        is_first = lax.axis_index("seq") == 0
+        half = upb_ref.shape[0] * LANES // flat.shape[1]
+        for k in range(half):
+            row = jnp.where(is_first, flat[3 + k : 4 + k], flat[3 + half + k : 4 + half + k])
+            spread(row, upb_ref, k * (flat.shape[1] // LANES))
+        norm_ref[...] = flat[8 : 8 + heads, 0 : norm_ref.shape[1]]
+        gate_ref[...] = small[0:heads]
+        gate_bias_ref[...] = small[heads : heads + 1, 0:heads]
+
     hb = late_ref.shape[3]
     for part, ref in enumerate((up_ref, down_ref)):
         for k in range(late_ref.shape[0]):
@@ -1201,7 +1225,7 @@
         s_ref[k] = os_ref[64 * k : 64 * (k + 1), width:].astype(F32)
 
 
-def finish(heads, sum_late, sum_w, out_state):
+def finish(heads, sum_late, sum_w, out_state, flat, small):
     width = sum_w.shape[1]
     steps = 4
     rows = width // steps
@@ -1210,15 +1234,24 @@
     square = ((width, width), F32, (rows, width), lambda i: (i, 0))
     wide = ((width, late * hb), F32, (rows, late * hb), lambda i: (i, 0))
     return call(
-        finish_kernel,
+        partial(finish_kernel, heads),
         (steps,),
         [
             (sum_late.reshape(late, 2, width, hb), (late, 2, rows, hb), lambda i: (0, 0, i, 0)),
             (sum_w, (sum_w.shape[0], rows, sum_w.shape[2]), lambda i: (0, i, 0)),
             (out_state, (rows, width + feats), lambda i: (i, 0)),
+            (flat, None, None),
+            (small, None, None),
         ],
         [wide, wide, square, square, square, square]
-        + [((heads, 64, feats), F32, (heads // steps, 64, feats), lambda i: (i, 0, 0))],
+        + [((heads, 64, feats), F32, (heads // steps, 64, feats), lambda i: (i, 0, 0))]
+        + [((width // LANES, LANES), F32, None, None)] * 5
+        + [
+            ((late * hb // LANES, LANES), F32, None, None),
+            ((heads, feats), F32, None, None),
+            ((heads, width), F32, None, None),
+            ((1, heads), F32, None, None),
+        ],
         [],
         "finish",
     )
@@ -1343,9 +1376,8 @@
         vmem(heads, LANES, dtype=F32),
         vmem(heads // 2, 3 * LANES, 2 * feats),
     ]
-    upb = up_bias.astype(F32)[None]
     if comm:
-        ins += [hbm(up_weight), hbm(down_weight), const(upb)]
+        ins += [hbm(up_weight), hbm(down_weight), const(up_bias)]
         outs += [
             keep(pay_shape, BF16),
             result(up_weight.shape, BF16),
@@ -1355,6 +1387,7 @@
         scratch += [
             vmem(*pay_shape),
             vmem(*pay_shape),
+            vmem(1, shard_width, dtype=F32),
             vmem(1, shard_width, dtype=F32),
             pltpu.SemaphoreType.DMA((8,)),
             pltpu.SemaphoreType.DMA((8,)),
@@ -1379,7 +1412,7 @@
         logs = total[0, :heads]
         entry = carry_over(final, logs, True)
         weights = (lax.all_gather(up_weight, "seq"), lax.all_gather(down_weight, "seq"))
-        upb = lax.all_gather(upb, "seq")
+        upb = lax.all_gather(up_bias.astype(F32)[None], "seq")
 
     steps = 2 * tiles + pairs
 
@@ -1585,12 +1618,11 @@
     dx, sum_w, small = found[:3]
     if comm:
         sum_late, out_state, flat = found[3:]
-        results = finish(heads, sum_late, sum_w, out_state)
-        sum_up, sum_down, sum_q, sum_k, sum_v, sum_o, sum_state = results
-        sum_feed = flat[0:3]
-        sum_upb = flat[3 : 3 + hidden // width].reshape(-1)
-        sum_upb = jnp.where(first, sum_upb[:shard_width], sum_upb[shard_width:])
-        sum_norm = flat[8 : 8 + heads, : 2 * feats]
+        results = finish(heads, sum_late, sum_w, out_state, flat, small)
+        sum_up, sum_down, sum_q, sum_k, sum_v, sum_o, sum_state = results[:7]
+        mixer_two, sum_feed = results[7:9], results[9:12]
+        sum_upb, sum_norm, sum_gate, gate_bias_sum = results[12:]
+        gate_bias_sum = gate_bias_sum.reshape(-1)
     else:
         own = lax.psum_scatter(
             jnp.stack([up_grad, down_grad]), "seq", scatter_dimension=1, tiled=True
@@ -1600,28 +1632,30 @@
         sum_w, sum_o, sum_state, small, sum_norm, sum_feed = lax.psum(
             (sum_w, output_grad, state_grad, small, norm_grad, feed_three), ("dp", "seq")
         )
+        mixer_two = (small[heads + 1], small[heads + 2])
+        sum_gate, gate_bias_sum = small[:heads], small[heads, :heads]
         sum_w = sum_w.reshape(groups, width, 3, hg * size).transpose(2, 1, 0, 3)
         sum_q, sum_k, sum_v = sum_w.reshape(3, width, width).astype(F32)
         sum_state = sum_state.reshape(heads, size, 2 * feats).astype(F32)
     return (
         out.reshape(inputs.shape),
         dx.reshape(inputs.shape),
-        small[heads + 1],
-        small[heads + 2],
+        mixer_two[0].reshape(-1),
+        mixer_two[1].reshape(-1),
         sum_q,
         sum_k,
         sum_v,
-        small[:heads].T,
-        small[heads, :heads],
+        sum_gate.T,
+        gate_bias_sum,
         sum_o.astype(F32),
         sum_state.transpose(0, 2, 1),
         sum_norm,
-        sum_feed[0],
-        sum_feed[1],
+        sum_feed[0].reshape(-1),
+        sum_feed[1].reshape(-1),
         sum_up.astype(F32),
-        sum_upb,
+        sum_upb.reshape(-1),
         sum_down.astype(F32),
-        sum_feed[2],
+        sum_feed[2].reshape(-1),
     )
 
 

time: 160 us -> 157 us (0.981)
    slice x2 -> x0, local copies, waits for them, and re-layouts: 2.03 us -> none  [the longest x1 1.43 us: local(): sum_feed[2]]
    unnamed x11 -> x6, local copies, waits for them, and re-layouts: 2.9 us -> 3.27 us
where the time goes in v7:
time: 157 us
  Pallas kernels  152 us (97%)
  local copies, waits for them, and re-layouts  4.55 us (3%)
    pallas_call x4, Pallas kernels, call(): pl.pallas_call(kernel, grid=grid, in_specs=[spec(array.shape, block, inde...  152 us
    unnamed x6, local copies, waits for them, and re-layouts  3.27 us

profile of v7, /device:TPU:0, one launch (start us, length us, event | category | flops | bytes accessed | tf_op | source)
XLA Modules:
  0.0 157.0 jit_solution(15851795119680846908)
XLA Ops:
  0.7 1.3 broadcast_in_dim.21.refs_13_
  1.9 32.5 %features.1 = (bf16[1024,512]{1,0:T(8,128)(2,1)}, bf16[1024,512]{1,0:T(8,128)(2,1)}, bf16[1024,512]{1,0:T(8,128)(2,1)}, f32[1024,512]{1,0:T(8,128)}, f32[1024,51...) custom-call(bf16[1024,512]{1,0:T(8,128)(2,1)} %bitcast.21, ...), custom_call_target="tpu_custom_call" | custom-call | tf_op jit(solution)/shard_map/features/pallas_call | solution.py:1173
  34.4 48.7 %feed.1 = (bf16[1024,512]{1,0:T(8,128)(2,1)}, f32[1024,512]{1,0:T(8,128)}, bf16[1024,1024]{1,0:T(8,128)(2,1)}, bf16[64,256]{1,0:T(8,128)(2,1)}, bf16[256,256]{1,...) custom-call(bf16[1024,512]{1,0:T(8,128)(2,1)} %bitcast.22, ...), custom_call_target="tpu_custom_call" | custom-call | tf_op jit(solution)/shard_map/feed/pallas_call | solution.py:1173
  83.1 64.4 %back.1 = (f32[1024,512]{1,0:T(8,128)}, bf16[2,512,768]{2,1,0:T(8,128)(2,1)}, f32[16,512]{1,0:T(8,128)}, bf16[4,1024,256]{2,1,0:T(8,128)(2,1)}, bf16[512,768]{1,0:T(8,128)(2,1)}, /*index=5*/f32[16,512]{1,0:T(8,128)}) custom-call(bf16[1024,2048]{1,0:T(8,128)(2,1)} %get-tuple-element.66.refs_1_.refs_0_, bf16[1024,2048]{1,0:T(8,128)(2,1)} %get-tuple-element.74.refs_1_, ...), custom_call_target="tpu_custom_call" | custom-call | tf_op jit(solution)/shard_map/back/pallas_call | solution.py:1173
  147.6 0.0 copy-start.1
  147.6 6.1 %finish.1 = (f32[512,1024]{1,0:T(8,128)}, f32[512,1024]{1,0:T(8,128)}, f32[512,512]{1,0:T(8,128)}, f32[512,512]{1,0:T(8,128)}, f32[512,512]{1,0:T(8,128)}, /*ind...) custom-call(bf16[4,2,512,256]{3,2,1,0:T(8,128)(2,1)} %bitcast.25, ...), custom_call_target="tpu_custom_call" | custom-call | tf_op jit(solution)/shard_map/finish/pallas_call | solution.py:1173
  153.7 0.0 copy-start
  153.7 0.0 copy-done.1
  153.7 1.0 copy.39
  154.7 1.0 copy-done
  155.7 1.3 copy.40
Async XLA Ops:
  147.6 6.1 %copy-start.1 = (bf16[1024,512]{1,0:T(8,128)(2,1)S(1)}, bf16[1024,512]{1,0:T(8,128)(2,1)}, u32[]{:S(2)}) copy-start(bf16[1024,512]{1,0:T(8,128)(2,1)} %get-tuple-element.73) | copy-start | bytes 3145732
  153.7 2.0 %copy-start = (f32[1024,512]{1,0:T(8,128)S(1)}, f32[1024,512]{1,0:T(8,128)}, u32[]{:S(2)}) copy-start(f32[1024,512]{1,0:T(8,128)} %get-tuple-element.92) | copy-start | bytes 6291460

commit v8 on v7

--- a/solution.py
+++ b/solution.py
@@ -1124,9 +1124,6 @@
             )
             small[heads + 2 : heads + 3, :] += jnp.sum(mixer_grad, axis=0, keepdims=True)
             dx_ref[rows, :] = mg_ref[rows, :] + normalize_back(mixer_grad, gain, xhat, scale)
-            if comm and b % 2 == 1 and b + 1 < tokens // block:
-                advance(now)
-                now += 1
         if comm:
             board.add(
                 plans["small"], small_src, smallsum_ref, small_ref, [now, now + 1, now + 2, now + 3]
@@ -1140,7 +1137,7 @@
 F_TICKS = (5, 7, 8, 9)
 W_GAPS = (0, 2, 4, 5, 6, 7, 8)
 W_PIECES = 3
-SUM_ROWS = 16
+SUM_ROWS = 64
 
 
 def back_plans(os, f, w, small):

time: 157 us -> 154 us (0.981)
  Pallas kernels: 152 us -> 148 us
    pallas_call x4, Pallas kernels: 152 us -> 148 us  [call(): pl.pallas_call(kernel, grid=grid, in_specs=[spec(array.shape, block, inde...]
where the time goes in v8:
time: 154 us; the launch traced here: 153 us
  Pallas kernels  148 us (96%)
  local copies, waits for them, and re-layouts  4.55 us (3%)
    pallas_call x4, Pallas kernels, call(): pl.pallas_call(kernel, grid=grid, in_specs=[spec(array.shape, block, inde...  148 us
    unnamed x6, local copies, waits for them, and re-layouts  3.27 us

profile of v8, /device:TPU:0, one launch (start us, length us, event | category | flops | bytes accessed | tf_op | source)
XLA Modules:
  0.0 153.0 jit_solution(18287194313959967039)
XLA Ops:
  0.7 1.3 broadcast_in_dim.21.refs_13_
  1.9 32.5 %features.1 = (bf16[1024,512]{1,0:T(8,128)(2,1)}, bf16[1024,512]{1,0:T(8,128)(2,1)}, bf16[1024,512]{1,0:T(8,128)(2,1)}, f32[1024,512]{1,0:T(8,128)}, f32[1024,51...) custom-call(bf16[1024,512]{1,0:T(8,128)(2,1)} %bitcast.21, ...), custom_call_target="tpu_custom_call" | custom-call | tf_op jit(solution)/shard_map/features/pallas_call | solution.py:1170
  34.4 47.4 %feed.1 = (bf16[1024,512]{1,0:T(8,128)(2,1)}, f32[1024,512]{1,0:T(8,128)}, bf16[1024,1024]{1,0:T(8,128)(2,1)}, bf16[64,256]{1,0:T(8,128)(2,1)}, bf16[256,256]{1,...) custom-call(bf16[1024,512]{1,0:T(8,128)(2,1)} %bitcast.22, ...), custom_call_target="tpu_custom_call" | custom-call | tf_op jit(solution)/shard_map/feed/pallas_call | solution.py:1170
  81.8 61.8 %back.1 = (f32[1024,512]{1,0:T(8,128)}, bf16[2,512,768]{2,1,0:T(8,128)(2,1)}, f32[16,512]{1,0:T(8,128)}, bf16[4,1024,256]{2,1,0:T(8,128)(2,1)}, bf16[512,768]{1,0:T(8,128)(2,1)}, /*index=5*/f32[16,512]{1,0:T(8,128)}) custom-call(bf16[1024,2048]{1,0:T(8,128)(2,1)} %get-tuple-element.66.refs_1_.refs_0_, bf16[1024,2048]{1,0:T(8,128)(2,1)} %get-tuple-element.74.refs_1_, ...), custom_call_target="tpu_custom_call" | custom-call | tf_op jit(solution)/shard_map/back/pallas_call | solution.py:1170
  143.6 0.0 copy-start.1
  143.6 6.1 %finish.1 = (f32[512,1024]{1,0:T(8,128)}, f32[512,1024]{1,0:T(8,128)}, f32[512,512]{1,0:T(8,128)}, f32[512,512]{1,0:T(8,128)}, f32[512,512]{1,0:T(8,128)}, /*ind...) custom-call(bf16[4,2,512,256]{3,2,1,0:T(8,128)(2,1)} %bitcast.25, ...), custom_call_target="tpu_custom_call" | custom-call | tf_op jit(solution)/shard_map/finish/pallas_call | solution.py:1170
  149.7 0.0 copy-start
  149.7 0.0 copy-done.1
  149.8 1.0 copy.39
  150.7 1.0 copy-done
  151.7 1.3 copy.40
Async XLA Ops:
  143.6 6.1 %copy-start.1 = (bf16[1024,512]{1,0:T(8,128)(2,1)S(1)}, bf16[1024,512]{1,0:T(8,128)(2,1)}, u32[]{:S(2)}) copy-start(bf16[1024,512]{1,0:T(8,128)(2,1)} %get-tuple-element.73) | copy-start | bytes 3145732
  149.7 2.0 %copy-start = (f32[1024,512]{1,0:T(8,128)S(1)}, f32[1024,512]{1,0:T(8,128)}, u32[]{:S(2)}) copy-start(f32[1024,512]{1,0:T(8,128)} %get-tuple-element.92) | copy-start | bytes 6291460
